TPU v7x, 32 devices: a whole 2x2x4 slice. The times are simulated.
32 devices in a mesh: seq: 4 (over y, x), fsdp: 8 (over z, core).
Axes of the slice: x: 2, y: 2, z: 4, core: 2. Of those that a mesh axis runs over, the one named last changes fastest.
Arguments:
- inputs: bfloat16 [4096, 2048], P(('fsdp', 'seq')), may hold values from -6 to 6
- positions: int32 [4096], P(('fsdp', 'seq')), may hold values from 0 to 766, as said below
- seq_ids: int32 [4096], P(('fsdp', 'seq')), may hold values from 0 to 15, as said below
- attn_gain: bfloat16 [2048], P(('fsdp', 'seq')), may hold values from 0.5 to 1.5
- w_query: bfloat16 [2048, 2048], P(('fsdp', 'seq')), may hold values from -0.125 to 0.125
- w_key: bfloat16 [2048, 2048], P(('fsdp', 'seq')), may hold values from -0.125 to 0.125
- w_value: bfloat16 [2048, 2048], P(('fsdp', 'seq')), may hold values from -0.125 to 0.125
- w_out: bfloat16 [2048, 2048], P(('fsdp', 'seq')), may hold values from -1 to 1
- ffn_gain: bfloat16 [2048], P(('fsdp', 'seq')), may hold values from 0.5 to 1.5
- w_gate: bfloat16 [2048, 8192], P(('fsdp', 'seq')), may hold values from -0.125 to 0.125
- w_up: bfloat16 [2048, 8192], P(('fsdp', 'seq')), may hold values from -0.125 to 0.125
- w_down: bfloat16 [8192, 2048], P(('fsdp', 'seq')), may hold values from -0.0625 to 0.0625
- cotangent: bfloat16 [4096, 2048], P(('fsdp', 'seq')), may hold values from -6 to 6
Outputs:
- layer_out: bfloat16 [4096, 2048], P(('fsdp', 'seq'))
- grad_input: float32 [4096, 2048], P(('fsdp', 'seq'))
- grad_attn_gain: float32 [2048], P(('fsdp', 'seq'))
- grad_query: float32 [2048, 2048], P(('fsdp', 'seq'))
- grad_key: float32 [2048, 2048], P(('fsdp', 'seq'))
- grad_value: float32 [2048, 2048], P(('fsdp', 'seq'))
- grad_out: float32 [2048, 2048], P(('fsdp', 'seq'))
- grad_ffn_gain: float32 [2048], P(('fsdp', 'seq'))
- grad_gate: float32 [2048, 8192], P(('fsdp', 'seq'))
- grad_up: float32 [2048, 8192], P(('fsdp', 'seq'))
- grad_down: float32 [8192, 2048], P(('fsdp', 'seq'))
Inputs may be any that keep to these rules, and one draw needn't show every extreme that they name: `seq_ids`: rows g * 512 to (g + 1) * 512 - 1 hold two documents, ids 2 g and 2 g + 1 in this order; the first holds 128 to 384 rows, exactly 384 in the first packed sequence. Within each document positions start at 0 at its first row and rise by 1 or 2 from one row to the next; in the first packed sequence they rise by 2 at every row.
All inputs are finite; a program needn't handle non-finite values.
Results may differ from a plain program's by a relative error of at most 0.014.
Values may be sent and summed in bfloat16 or wider, within the bound.
No kernel may reach another device: no remote copies, remote signals or barrier semaphores. Data moves between devices by JAX's collectives and lax.ppermute only.
A program may use at most 704 MiB of HBM per device.

v0:
```python
import math

import jax
import jax.numpy as jnp
from jax import lax
from jax.sharding import PartitionSpec as P

HEADS = 16
HEAD_DIM = 128


EPSILON = 1e-05


def rope_tables(positions, head_dim):
    half_dim = head_dim // 2
    frequency = 10000.0 ** (-(jnp.arange(half_dim, dtype=jnp.float32) * 2.0) / head_dim)
    angles = positions.astype(jnp.float32)[:, None] * frequency[None, :]
    return (jnp.cos(angles)[:, None, :], jnp.sin(angles)[:, None, :])


def rotate(field, cosine_table, sine_table):
    half_dim = field.shape[-1] // 2
    front_half, back_half = (field[..., :half_dim], field[..., half_dim:])
    return jnp.concatenate(
        [
            front_half * cosine_table - back_half * sine_table,
            back_half * cosine_table + front_half * sine_table,
        ],
        axis=-1,
    )


def rotate_back(gradient, cosine_table, sine_table):
    half_dim = gradient.shape[-1] // 2
    front_half, back_half = (gradient[..., :half_dim], gradient[..., half_dim:])
    return jnp.concatenate(
        [
            front_half * cosine_table + back_half * sine_table,
            back_half * cosine_table - front_half * sine_table,
        ],
        axis=-1,
    )


def times_trans(left, right):
    return lax.dot_general(
        left, right, (((1,), (1,)), ((), ())), preferred_element_type=jnp.float32
    )


def inner_rows(left, right):
    return lax.dot_general(
        left, right, (((0,), (0,)), ((), ())), preferred_element_type=jnp.float32
    )


def norm_back(d_normed, unit_rows, inverse, gain_float):
    scaled = d_normed * gain_float
    return inverse * (scaled - unit_rows * jnp.mean(scaled * unit_rows, axis=-1, keepdims=True))


def shards(
    inputs,
    positions,
    seq_ids,
    attn_gain,
    w_query,
    w_key,
    w_value,
    w_out,
    ffn_gain,
    w_gate,
    w_up,
    w_down,
    cotangent,
):
    tokens, model_width = inputs.shape
    group_rows = tokens * lax.axis_size("seq")
    score_scale = HEAD_DIM ** (-0.5)
    score_bias = -math.log(group_rows)
    query_rows = lax.axis_index("seq") * tokens + jnp.arange(tokens, dtype=jnp.int32)
    attn_full = (
        lax.all_gather(attn_gain, ("fsdp", "seq"), axis=0, tiled=True),
        lax.all_gather(w_query, ("fsdp", "seq"), axis=0, tiled=True),
        lax.all_gather(w_key, ("fsdp", "seq"), axis=0, tiled=True),
        lax.all_gather(w_value, ("fsdp", "seq"), axis=0, tiled=True),
        lax.all_gather(w_out, ("fsdp", "seq"), axis=0, tiled=True),
    )
    gain_one, full_query, full_key, full_value, full_out = attn_full
    input_float = inputs.astype(jnp.float32)
    inverse_one = lax.rsqrt(jnp.mean(input_float * input_float, axis=-1, keepdims=True) + EPSILON)
    unit_one = input_float * inverse_one
    normed1 = (unit_one * gain_one.astype(jnp.float32)).astype(jnp.bfloat16)
    cosine_table, sine_table = rope_tables(positions, HEAD_DIM)

    def project(weight):
        return jnp.dot(normed1, weight, preferred_element_type=jnp.float32).reshape(
            tokens, HEADS, HEAD_DIM
        )

    query = rotate(project(full_query), cosine_table, sine_table).astype(jnp.bfloat16)
    keys = (
        rotate(project(full_key), cosine_table, sine_table)
        .reshape(tokens, model_width)
        .astype(jnp.bfloat16)
    )
    values = project(full_value).reshape(tokens, model_width).astype(jnp.bfloat16)

    def scores_of(key_piece, id_piece, first_row):
        raw_scores = jnp.einsum(
            "qhd,khd->hqk", query, key_piece, preferred_element_type=jnp.float32
        )
        key_rows = first_row + jnp.arange(key_piece.shape[0], dtype=jnp.int32)
        allowed = (key_rows[None, :] <= query_rows[:, None]) & (
            id_piece[None, :] == seq_ids[:, None]
        )
        return jnp.where(allowed[None], jax.nn.sigmoid(raw_scores * score_scale + score_bias), 0.0)

    key_piece = lax.all_gather(keys, "seq", axis=0, tiled=True)
    value_piece = lax.all_gather(values, "seq", axis=0, tiled=True)
    id_piece = lax.all_gather(seq_ids, "seq", axis=0, tiled=True)
    count = key_piece.shape[0]
    key_heads = key_piece.reshape(count, HEADS, HEAD_DIM)
    value_heads = value_piece.reshape(count, HEADS, HEAD_DIM)
    weights = scores_of(key_heads, id_piece, jnp.int32(0)).astype(jnp.bfloat16)
    mixed = jnp.einsum("hqk,khd->qhd", weights, value_heads, preferred_element_type=jnp.float32)
    mixed_low = mixed.reshape(tokens, model_width).astype(jnp.bfloat16)
    residual = input_float + jnp.dot(mixed_low, full_out, preferred_element_type=jnp.float32)
    ffn_full = (
        lax.all_gather(ffn_gain, ("fsdp", "seq"), axis=0, tiled=True),
        lax.all_gather(w_gate, ("fsdp", "seq"), axis=0, tiled=True),
        lax.all_gather(w_up, ("fsdp", "seq"), axis=0, tiled=True),
        lax.all_gather(w_down, ("fsdp", "seq"), axis=0, tiled=True),
    )
    gain_two, full_gate, full_up, full_down = ffn_full
    inverse_two = lax.rsqrt(jnp.mean(residual * residual, axis=-1, keepdims=True) + EPSILON)
    unit_two = residual * inverse_two
    normed2 = (unit_two * gain_two.astype(jnp.float32)).astype(jnp.bfloat16)
    gate = jnp.dot(normed2, full_gate, preferred_element_type=jnp.float32)
    upward = jnp.dot(normed2, full_up, preferred_element_type=jnp.float32)
    sigma_gate = jax.nn.sigmoid(gate)
    inner = (gate * sigma_gate * upward).astype(jnp.bfloat16)
    layer_out = (residual + jnp.dot(inner, full_down, preferred_element_type=jnp.float32)).astype(
        jnp.bfloat16
    )
    attn_back = (
        lax.all_gather(attn_gain, ("fsdp", "seq"), axis=0, tiled=True),
        lax.all_gather(w_query, ("fsdp", "seq"), axis=0, tiled=True),
        lax.all_gather(w_key, ("fsdp", "seq"), axis=0, tiled=True),
        lax.all_gather(w_value, ("fsdp", "seq"), axis=0, tiled=True),
        lax.all_gather(w_out, ("fsdp", "seq"), axis=0, tiled=True),
    )
    ffn_back = (
        lax.all_gather(ffn_gain, ("fsdp", "seq"), axis=0, tiled=True),
        lax.all_gather(w_gate, ("fsdp", "seq"), axis=0, tiled=True),
        lax.all_gather(w_up, ("fsdp", "seq"), axis=0, tiled=True),
        lax.all_gather(w_down, ("fsdp", "seq"), axis=0, tiled=True),
    )
    gain_two_b, back_gate, back_up, back_down = ffn_back
    gain_one_b, back_query, back_key, back_value, back_out = attn_back
    hidden_width = gate.shape[1]
    d_inner = times_trans(cotangent, back_down)
    d_gate = (d_inner * upward * sigma_gate * (1.0 + gate * (1.0 - sigma_gate))).astype(
        jnp.bfloat16
    )
    d_up = (d_inner * gate * sigma_gate).astype(jnp.bfloat16)
    d_normed2 = times_trans(d_gate, back_gate) + times_trans(d_up, back_up)
    gain_two_term = jnp.sum(d_normed2 * unit_two, axis=0)
    d_residual = cotangent.astype(jnp.float32) + norm_back(
        d_normed2, unit_two, inverse_two, gain_two_b.astype(jnp.float32)
    )
    stacked_d = jnp.concatenate([d_gate, d_up], axis=1)
    gate_up_grad = lax.psum_scatter(
        inner_rows(normed2, stacked_d), ("fsdp", "seq"), scatter_dimension=0, tiled=True
    )
    grad_gate = gate_up_grad[:, :hidden_width]
    grad_up = gate_up_grad[:, hidden_width:]
    grad_down = lax.psum_scatter(
        inner_rows(inner, cotangent), ("fsdp", "seq"), scatter_dimension=0, tiled=True
    )
    d_attended = d_residual.astype(jnp.bfloat16)
    d_mixed = (
        times_trans(d_attended, back_out).reshape(tokens, HEADS, HEAD_DIM).astype(jnp.bfloat16)
    )
    grad_out_term = inner_rows(mixed_low, d_attended)
    key_back, value_back, id_back = (
        lax.all_gather(keys, "seq", axis=0, tiled=True),
        lax.all_gather(values, "seq", axis=0, tiled=True),
        lax.all_gather(seq_ids, "seq", axis=0, tiled=True),
    )
    block_rows = min(512, group_rows)
    block_count = group_rows // block_rows
    key_blocks = key_back.reshape(block_count, block_rows, HEADS, HEAD_DIM)
    value_blocks = value_back.reshape(block_count, block_rows, HEADS, HEAD_DIM)
    id_blocks = id_back.reshape(block_count, block_rows)
    block_starts = jnp.arange(block_count, dtype=jnp.int32) * block_rows

    def key_step(d_query_sum, blocked):
        key_piece, value_piece, id_piece, first_row = blocked
        weights = scores_of(key_piece, id_piece, first_row)
        d_weights = jnp.einsum(
            "qhd,khd->hqk", d_mixed, value_piece, preferred_element_type=jnp.float32
        )
        d_scores = (d_weights * weights * (1.0 - weights)).astype(jnp.bfloat16)
        d_query_sum = d_query_sum + jnp.einsum(
            "hqk,khd->qhd", d_scores, key_piece, preferred_element_type=jnp.float32
        )
        d_key_piece = jnp.einsum(
            "hqk,qhd->khd", d_scores, query, preferred_element_type=jnp.float32
        )
        d_value_piece = jnp.einsum(
            "hqk,qhd->khd",
            weights.astype(jnp.bfloat16),
            d_mixed,
            preferred_element_type=jnp.float32,
        )
        return (d_query_sum, (d_key_piece, d_value_piece))

    d_query_sum, (key_terms, value_terms) = lax.scan(
        key_step,
        jnp.zeros((tokens, HEADS, HEAD_DIM), jnp.float32),
        (key_blocks, value_blocks, id_blocks, block_starts),
    )
    key_terms = key_terms.reshape(group_rows, model_width) * score_scale
    value_terms = value_terms.reshape(group_rows, model_width)
    d_key_sum, d_value_sum = (
        lax.psum_scatter(key_terms, "seq", scatter_dimension=0, tiled=True),
        lax.psum_scatter(value_terms, "seq", scatter_dimension=0, tiled=True),
    )
    d_query = (
        rotate_back(d_query_sum * score_scale, cosine_table, sine_table)
        .reshape(tokens, model_width)
        .astype(jnp.bfloat16)
    )
    d_key = (
        rotate_back(d_key_sum.reshape(tokens, HEADS, HEAD_DIM), cosine_table, sine_table)
        .reshape(tokens, model_width)
        .astype(jnp.bfloat16)
    )
    d_value = d_value_sum.astype(jnp.bfloat16)
    d_normed1 = (
        times_trans(d_query, back_query)
        + times_trans(d_key, back_key)
        + times_trans(d_value, back_value)
    )
    grad_query_term = inner_rows(normed1, d_query)
    grad_key_term = inner_rows(normed1, d_key)
    grad_value_term = inner_rows(normed1, d_value)
    gain_one_term = jnp.sum(d_normed1 * unit_one, axis=0)
    grad_input = d_residual + norm_back(
        d_normed1, unit_one, inverse_one, gain_one_b.astype(jnp.float32)
    )
    grad_attn_gain, grad_ffn_gain, grad_query, grad_key, grad_value, grad_out = (
        lax.psum_scatter(gain_one_term, ("fsdp", "seq"), scatter_dimension=0, tiled=True),
        lax.psum_scatter(gain_two_term, ("fsdp", "seq"), scatter_dimension=0, tiled=True),
        lax.psum_scatter(grad_query_term, ("fsdp", "seq"), scatter_dimension=0, tiled=True),
        lax.psum_scatter(grad_key_term, ("fsdp", "seq"), scatter_dimension=0, tiled=True),
        lax.psum_scatter(grad_value_term, ("fsdp", "seq"), scatter_dimension=0, tiled=True),
        lax.psum_scatter(grad_out_term, ("fsdp", "seq"), scatter_dimension=0, tiled=True),
    )
    return (
        layer_out,
        grad_input,
        grad_attn_gain,
        grad_query,
        grad_key,
        grad_value,
        grad_out,
        grad_ffn_gain,
        grad_gate,
        grad_up,
        grad_down,
    )


def solution(mesh):
    placed = (
        P(("fsdp", "seq"), None),
        P(("fsdp", "seq")),
        P(("fsdp", "seq")),
        P(("fsdp", "seq")),
        P(("fsdp", "seq"), None),
        P(("fsdp", "seq"), None),
        P(("fsdp", "seq"), None),
        P(("fsdp", "seq"), None),
        P(("fsdp", "seq")),
        P(("fsdp", "seq"), None),
        P(("fsdp", "seq"), None),
        P(("fsdp", "seq"), None),
        P(("fsdp", "seq"), None),
    )
    return jax.shard_map(
        shards,
        mesh=mesh,
        in_specs=placed,
        out_specs=(
            P(("fsdp", "seq"), None),
            P(("fsdp", "seq"), None),
            P(("fsdp", "seq")),
            P(("fsdp", "seq"), None),
            P(("fsdp", "seq"), None),
            P(("fsdp", "seq"), None),
            P(("fsdp", "seq"), None),
            P(("fsdp", "seq")),
            P(("fsdp", "seq"), None),
            P(("fsdp", "seq"), None),
            P(("fsdp", "seq"), None),
        ),
        check_vma=False,
    )
```

profile of v0, /device:TPU:0, one launch (start us, length us, event | category | flops | bytes accessed | tf_op | source)
XLA Modules:
  0.0 5915.8 jit_solution(13926811781391948825)
XLA Ops:
  13.1 42.5 all-reduce.6
  57.9 33.5 all-gather.15.cloned.1.call-done
  96.5 74.0 %all-gather.17.cloned.1.call-done = bf16[2048,2048]{1,0:T(8,128)(2,1)} async-done(((bf16[64,2048]{1,0:T(8,128)(2,1)}), bf16[2048,2048]{1,0:T(8,128)(2,1)}) %all-gather.17.cloned.1.call-update) | async-done | bytes 8388624 | tf_op jit(solution)/shard_map/all_gather | solution.py:86
  178.9 70.7 %all-gather.11.cloned.1.call-done = bf16[2048,2048]{1,0:T(8,128)(2,1)} async-done(((bf16[64,2048]{1,0:T(8,128)(2,1)}), bf16[2048,2048]{1,0:T(8,128)(2,1)}) %all-gather.11.cloned.1.call-update) | async-done | bytes 8388624 | tf_op jit(solution)/shard_map/all_gather | solution.py:87
  266.2 19.4 all-gather.19.cloned.1.call-done
  290.8 32.4 all-gather.13.cloned.1.call-done
  326.9 76.6 %all-gather.21.cloned.1.call-done = bf16[2048,2048]{1,0:T(8,128)(2,1)} async-done(((bf16[64,2048]{1,0:T(8,128)(2,1)}), bf16[2048,2048]{1,0:T(8,128)(2,1)}) %all-gather.21.cloned.1.call-update) | async-done | bytes 8388624 | tf_op jit(solution)/shard_map/all_gather | solution.py:88
  408.5 191.3 %all-gather.23.cloned.1.call-done = bf16[2048,8192]{1,0:T(8,128)(2,1)} async-done(((bf16[64,8192]{1,0:T(8,128)(2,1)}), bf16[2048,8192]{1,0:T(8,128)(2,1)}) %all-gather.23.cloned.1.call-update) | async-done | bytes 33554448 | tf_op jit(solution)/shard_map/all_gather | solution.py:132
  599.8 17.9 fusion.51
  617.7 178.0 %all-gather.25.cloned.1.call-done = bf16[2048,8192]{1,0:T(8,128)(2,1)} async-done(((bf16[64,8192]{1,0:T(8,128)(2,1)}), bf16[2048,8192]{1,0:T(8,128)(2,1)}) %all-gather.25.cloned.1.call-update) | async-done | bytes 33554448 | tf_op jit(solution)/shard_map/all_gather | solution.py:133
  795.7 18.2 fusion.52
  814.0 177.6 %all-gather.27.cloned.1.call-done = bf16[8192,2048]{1,0:T(8,128)(2,1)} async-done(((bf16[256,2048]{1,0:T(8,128)(2,1)}), bf16[8192,2048]{1,0:T(8,128)(2,1)}) %all-gather.27.cloned.1.call-update) | async-done | bytes 33554448 | tf_op jit(solution)/shard_map/all_gather | solution.py:134
  991.6 20.9 multiply_convert_fusion.1
  1028.9 17.8 multiply_reduce_fusion
  1068.3 49.5 fusion
  1180.2 26.7 fusion.55
  1208.2 16.8 fusion.4
  1243.0 40.7 all-reduce.5
  1287.5 1767.5 %all-reduce.9.cloned.1.call-done = f32[2048,16384]{1,0:T(8,128)} async-done(((f32[2048,16384]{1,0:T(8,128)}), f32[2048,16384]{1,0:T(8,128)}) %all-reduce.9.cloned.1.call-update) | async-done | bytes 134217744
  3059.8 355.0 %reduce-scatter.18.cloned.1.call-done = f32[64,2048]{1,0:T(8,128)} async-done(((f32[2048,2048]{1,0:T(8,128)}), f32[64,2048]{1,0:T(8,128)}) %reduce-scatter.18.cloned.1.call-update) | async-done | bytes 524304 | tf_op jit(solution)/shard_map/reduce_scatter | solution.py:260
  3414.8 361.8 %reduce-scatter.12.cloned.1.call-done = f32[64,2048]{1,0:T(8,128)} async-done(((f32[2048,2048]{1,0:T(8,128)}), f32[64,2048]{1,0:T(8,128)}) %reduce-scatter.12.cloned.1.call-update) | async-done | bytes 524304 | tf_op jit(solution)/shard_map/reduce_scatter | solution.py:257
  3776.6 361.8 %reduce-scatter.14.cloned.1.call-done = f32[64,2048]{1,0:T(8,128)} async-done(((f32[2048,2048]{1,0:T(8,128)}), f32[64,2048]{1,0:T(8,128)}) %reduce-scatter.14.cloned.1.call-update) | async-done | bytes 524304 | tf_op jit(solution)/shard_map/reduce_scatter | solution.py:258
  4138.4 361.8 %reduce-scatter.16.cloned.1.call-done = f32[64,2048]{1,0:T(8,128)} async-done(((f32[2048,2048]{1,0:T(8,128)}), f32[64,2048]{1,0:T(8,128)}) %reduce-scatter.16.cloned.1.call-update) | async-done | bytes 524304 | tf_op jit(solution)/shard_map/reduce_scatter | solution.py:259
  4500.1 1408.6 %reduce-scatter.20.cloned.1.call-done = f32[256,2048]{1,0:T(8,128)} async-done(((f32[8192,2048]{1,0:T(8,128)}), f32[256,2048]{1,0:T(8,128)}) %reduce-scatter.20.cloned.1.call-update) | async-done | bytes 2097168 | tf_op jit(solution)/shard_map/reduce_scatter | solution.py:179
  (157 shorter events, 178.4 us)
Async XLA Ops:
  7.2 84.3 %all-gather.15.cloned.1.call-start = ((), (), s32[]{:S(2)}) async-start(), calls=%async_computation.9 | async-start | bytes 8650752 | tf_op jit(solution)/shard_map/all_gather | solution.py:85
  7.9 162.6 %all-gather.17.cloned.1.call-start = ((), (), s32[]{:S(2)}) async-start(), calls=%async_computation.10 | async-start | bytes 8650752 | tf_op jit(solution)/shard_map/all_gather | solution.py:86
  8.7 240.9 %all-gather.11.cloned.1.call-start = ((), (), s32[]{:S(2)}) async-start(), calls=%async_computation.7 | async-start | bytes 8650752 | tf_op jit(solution)/shard_map/all_gather | solution.py:87
  9.4 276.2 %all-gather.19.cloned.1.call-start = ((), (), s32[]{:S(2)}) async-start(), calls=%async_computation.11 | async-start | bytes 2621440 | tf_op jit(solution)/shard_map/all_gather | solution.py:120
  55.6 193.9 %copy-start.11 = (f32[2048]{0:T(1024)}, f32[2048]{0:T(1024)S(1)}, u32[]{:S(2)}) copy-start(f32[2048]{0:T(1024)S(1)} %convert_element_type.82) | copy-start | bytes 24580
  57.6 192.0 %copy-start.25 = (f32[128]{0:T(128)}, f32[128]{0:T(128)S(1)}, u32[]{:S(2)}) copy-start(f32[128]{0:T(128)S(1)} %add_rsqrt_fusion.1) | copy-start | bytes 1540
  57.9 118.2 %copy-start.21 = (f32[128,64]{1,0:T(8,128)}, f32[128,64]{1,0:T(8,128)S(1)}, u32[]{:S(2)}) copy-start(f32[128,64]{1,0:T(8,128)S(1)} %get-tuple-element.75) | copy-start | bytes 98308
  57.9 118.2 %copy-start.23 = (f32[128,64]{1,0:T(8,128)}, f32[128,64]{1,0:T(8,128)S(1)}, u32[]{:S(2)}) copy-start(f32[128,64]{1,0:T(8,128)S(1)} %get-tuple-element.76) | copy-start | bytes 98308
  178.8 144.4 %all-gather.13.cloned.1.call-start = ((), (), s32[]{:S(2)}) async-start(), calls=%async_computation.8 | async-start | bytes 2621440 | tf_op jit(solution)/shard_map/all_gather | solution.py:121
  255.1 148.5 %all-gather.21.cloned.1.call-start = ((), (), s32[]{:S(2)}) async-start(), calls=%async_computation.12 | async-start | bytes 8650752 | tf_op jit(solution)/shard_map/all_gather | solution.py:88
  255.6 344.2 %all-gather.23.cloned.1.call-start = ((), (), s32[]{:S(2)}) async-start(), calls=%async_computation.13 | async-start | bytes 34603008 | tf_op jit(solution)/shard_map/all_gather | solution.py:132
  256.4 539.3 %all-gather.25.cloned.1.call-start = ((), (), s32[]{:S(2)}) async-start(), calls=%async_computation.14 | async-start | bytes 34603008 | tf_op jit(solution)/shard_map/all_gather | solution.py:133
  257.1 734.4 %all-gather.27.cloned.1.call-start = ((), (), s32[]{:S(2)}) async-start(), calls=%async_computation.15 | async-start | bytes 34603008 | tf_op jit(solution)/shard_map/all_gather | solution.py:134
  257.9 872.9 %reduce-scatter.8.cloned.1.call-start = ((), (), s32[]{:S(2)}) async-start(), calls=%async_computation.16 | async-start | bytes 5242880 | tf_op jit(solution)/shard_map/reduce_scatter | solution.py:228
  408.3 638.4 %copy-start.2 = (f32[128,2048]{1,0:T(8,128)}, f32[128,2048]{1,0:T(8,128)S(1)}, u32[]{:S(2)}) copy-start(f32[128,2048]{1,0:T(8,128)S(1)} %get-tuple-element.80) | copy-start | bytes 3145732
  408.5 387.2 %copy-start.6 = (bf16[128,2048]{1,0:T(8,128)(2,1)}, bf16[128,2048]{1,0:T(8,128)(2,1)S(1)}, u32[]{:S(2)}) copy-start(bf16[128,2048]{1,0:T(8,128)(2,1)S(1)} %multiply_convert_fusion.4) | copy-start | bytes 1572868
  617.7 373.9 %copy-start.13 = (bf16[128,2048]{1,0:T(8,128)(2,1)S(1)}, bf16[128,2048]{1,0:T(8,128)(2,1)}, u32[]{:S(2)}) copy-start(bf16[128,2048]{1,0:T(8,128)(2,1)} %param.25) | copy-start | bytes 1572868
  1062.8 106.9 %reduce-scatter.10.cloned.1.call-start = ((), (), s32[]{:S(2)}) async-start(), calls=%async_computation.17 | async-start | bytes 5242880 | tf_op jit(solution)/shard_map/reduce_scatter | solution.py:229
  1068.2 1986.7 %all-reduce.9.cloned.1.call-start = ((), (), s32[]{:S(2)}) async-start(), calls=%async_computation.23 | async-start | bytes 268435456
  1117.8 2297.0 %reduce-scatter.18.cloned.1.call-start = ((), (), s32[]{:S(2)}) async-start(), calls=%async_computation.21 | async-start | bytes 17301504 | tf_op jit(solution)/shard_map/reduce_scatter | solution.py:260
  1127.5 2649.1 %reduce-scatter.12.cloned.1.call-start = ((), (), s32[]{:S(2)}) async-start(), calls=%async_computation.18 | async-start | bytes 17301504 | tf_op jit(solution)/shard_map/reduce_scatter | solution.py:257
  1147.2 2991.2 %reduce-scatter.14.cloned.1.call-start = ((), (), s32[]{:S(2)}) async-start(), calls=%async_computation.19 | async-start | bytes 17301504 | tf_op jit(solution)/shard_map/reduce_scatter | solution.py:258
  1159.5 3340.7 %reduce-scatter.16.cloned.1.call-start = ((), (), s32[]{:S(2)}) async-start(), calls=%async_computation.20 | async-start | bytes 17301504 | tf_op jit(solution)/shard_map/reduce_scatter | solution.py:259
  1179.2 4729.6 %reduce-scatter.20.cloned.1.call-start = ((), (), s32[]{:S(2)}) async-start(), calls=%async_computation.22 | async-start | bytes 69206016 | tf_op jit(solution)/shard_map/reduce_scatter | solution.py:179
  (24 other events, 597.4 us)
Sparse Core Ops, SparseCore 0:
  10.9 80.5 all-gather.14
  94.3 76.1 all-gather.16
  173.4 76.1 all-gather.10
  251.8 33.7 all-gather.18
  287.9 35.3 all-gather.12
  326.0 77.5 all-gather.20
  406.4 193.3 all-gather.22
  602.7 192.9 all-gather.24
  798.6 192.9 all-gather.26
  1062.9 50.8 reduce-scatter.7
  1117.1 52.6 reduce-scatter.9
  1176.0 1878.8 all-reduce.8
  3057.8 356.9 reduce-scatter.17
  3417.5 359.0 reduce-scatter.11
  3779.3 359.0 reduce-scatter.13
  4141.1 359.0 reduce-scatter.15
  4502.9 1405.8 reduce-scatter.19
where the time goes:
time: 5920 us
  waiting for transfers between devices  5490 us (93%)
  matrix products  288 us (5%)
  blocking collectives  91.3 us (2%)
    unnamed x18, waiting for transfers between devices  1770 us
    reduce_scatter x1, waiting for transfers between devices, shards(): lax.psum_scatter(inner_rows(inner, cotangent), ('fsdp', 'seq'), scatter_d...  1410 us
    reduce_scatter x1, waiting for transfers between devices, shards(): lax.psum_scatter(grad_query_term, ('fsdp', 'seq'), scatter_dimension=0, t...  362 us
    reduce_scatter x1, waiting for transfers between devices, shards(): lax.psum_scatter(grad_value_term, ('fsdp', 'seq'), scatter_dimension=0, t...  362 us
    reduce_scatter x1, waiting for transfers between devices, shards(): lax.psum_scatter(grad_key_term, ('fsdp', 'seq'), scatter_dimension=0, til...  362 us
    reduce_scatter x1, waiting for transfers between devices, shards(): lax.psum_scatter(grad_out_term, ('fsdp', 'seq'), scatter_dimension=0, til...  355 us
    all_gather x1, waiting for transfers between devices, shards(): lax.all_gather(w_gate, ('fsdp', 'seq'), axis=0, tiled=True)  191 us
    all_gather x1, waiting for transfers between devices, shards(): lax.all_gather(w_up, ('fsdp', 'seq'), axis=0, tiled=True)  178 us
  transfers between devices with their start and end apart: 17, of which 16 were waited for; matrix products, arithmetic and copies ran while one was open for 4% of the time, Pallas kernels for 0%

commit v1 on v0

v1 whole, which is shorter than its diff:
```python
import math

import jax
import jax.numpy as jnp
from jax import lax
from jax.sharding import PartitionSpec as P

HEADS = 16
HEAD_DIM = 128
EPSILON = 1e-05
BOTH = ("seq", "fsdp")
BF = jnp.bfloat16
F32 = jnp.float32


def nn(left, right):
    return lax.dot_general(left, right, (((1,), (0,)), ((), ())), preferred_element_type=F32)


def nt(left, right):
    return lax.dot_general(left, right, (((1,), (1,)), ((), ())), preferred_element_type=F32)


def tn(left, right):
    return lax.dot_general(left, right, (((0,), (0,)), ((), ())), preferred_element_type=F32)


def after(value, *deps):
    return lax.optimization_barrier((value, *deps))[0]


def pick(blocks, index):
    return lax.dynamic_index_in_dim(blocks, index, 0, keepdims=False)


class Net:
    def __init__(self):
        self.ns = lax.axis_size("seq")
        self.nf = lax.axis_size("fsdp")
        self.nz = self.nf // 2
        ns, nf, nz = self.ns, self.nf, self.nz
        half = ns // 2
        self.s_order = list(range(half)) + list(range(ns - 1, half - 1, -1))
        self.z_order = list(range(0, nz, 2)) + list(range(nz - 1 - nz % 2, 0, -2))
        s_next = {self.s_order[i]: self.s_order[(i + 1) % ns] for i in range(ns)}
        s_prev = {b: a for a, b in s_next.items()}
        z_next = {self.z_order[i]: self.z_order[(i + 1) % nz] for i in range(nz)}
        self.s_perm = [
            (s * nf + f, (s_next[s] if f % 2 == 0 else s_prev[s]) * nf + f)
            for f in range(nf)
            for s in range(ns)
        ]
        self.z_perm = [(2 * z + c, 2 * z_next[z] + c) for z in range(nz) for c in range(2)]
        self.c_perm = [(f, f ^ 1) for f in range(nf)]
        self.f = lax.axis_index("fsdp")
        self.s = lax.axis_index("seq")
        self.c = self.f % 2
        self.z = self.f // 2
        s_at = [self.s_order.index(s) for s in range(ns)]
        z_at = [self.z_order.index(z) for z in range(nz)]
        self.s_place = jnp.array(s_at, jnp.int32)[self.s]
        self.z_place = jnp.array(z_at, jnp.int32)[self.z]
        self.s_sign = 1 - 2 * self.c

    def s_back(self, k):
        return jnp.array(self.s_order, jnp.int32)[(self.s_place - self.s_sign * k) % self.ns]

    def z_back(self, k):
        return jnp.array(self.z_order, jnp.int32)[(self.z_place - k) % self.nz]

    def step_s(self, value):
        return lax.ppermute(value, BOTH, self.s_perm)

    def step_z(self, value):
        return lax.ppermute(value, "fsdp", self.z_perm)

    def swap_c(self, value):
        return lax.ppermute(value, "fsdp", self.c_perm)

    def gather_s(self, value, axis=0):
        shape = list(value.shape)
        shape.insert(axis, self.ns)
        out = jnp.zeros(shape, value.dtype)
        held = value
        for k in range(self.ns):
            if k:
                held = self.step_s(held)
            out = lax.dynamic_update_slice_in_dim(
                out, jnp.expand_dims(held, axis), self.s_back(k), axis
            )
        return out

    def gather_f(self, value):
        out = jnp.zeros((self.nz, 2, *value.shape), value.dtype)
        zero = jnp.int32(0)
        rest = (zero,) * value.ndim
        held = value
        for k in range(self.nz):
            if k:
                held = self.step_z(held)
            other = self.swap_c(held)
            row = self.z_back(k)
            out = lax.dynamic_update_slice(out, held[None, None], (row, self.c, *rest))
            out = lax.dynamic_update_slice(out, other[None, None], (row, 1 - self.c, *rest))
        return out.reshape(self.nf, *value.shape)

    def scatter_s(self, part):
        total = part(self.s_back(1))
        for k in range(1, self.ns):
            came = self.step_s(total.astype(BF))
            total = part(self.s_back(k + 1)) + came.astype(F32)
        return total

    def scatter_f(self, blocks):
        pairs = blocks.reshape(self.nz, 2, *blocks.shape[1:])
        away = lax.dynamic_index_in_dim(pairs, 1 - self.c, 1, keepdims=False)
        mine = lax.dynamic_index_in_dim(pairs, self.c, 1, keepdims=False)
        mine = mine.astype(F32) + self.swap_c(away.astype(BF)).astype(F32)
        total = pick(mine, self.z_back(1))
        for k in range(1, self.nz):
            came = self.step_z(total.astype(BF))
            total = pick(mine, self.z_back(k + 1)) + came.astype(F32)
        return total

    def swap_f(self, blocks):
        pairs = blocks.reshape(self.nz, 2, *blocks.shape[1:])
        away = lax.dynamic_index_in_dim(pairs, 1 - self.c, 1, keepdims=False)
        mine = lax.dynamic_index_in_dim(pairs, self.c, 1, keepdims=False)
        came = self.swap_c(away)
        first = jnp.where(self.c == 0, mine, came)
        second = jnp.where(self.c == 0, came, mine)
        both = jnp.stack([first, second], axis=1)
        out = both
        for k in range(1, self.nz):
            perm = [
                (2 * z + c, 2 * ((z + k) % self.nz) + c) for z in range(self.nz) for c in range(2)
            ]
            got = lax.ppermute(pick(both, (self.z + k) % self.nz), "fsdp", perm)
            out = lax.dynamic_update_slice_in_dim(out, got[None], (self.z - k) % self.nz, 0)
        return out.reshape(blocks.shape)

    def swap_s(self, blocks):
        out = blocks
        for k in range(1, self.ns):
            perm = [(s, s ^ k) for s in range(self.ns)]
            got = lax.ppermute(pick(blocks, self.s ^ k), "seq", perm)
            out = lax.dynamic_update_slice_in_dim(out, got[None], self.s ^ k, 0)
        return out


def rotate(field, cosine, sine):
    half = field.shape[-1] // 2
    front, back = field[..., :half], field[..., half:]
    return jnp.concatenate([front * cosine - back * sine, back * cosine + front * sine], axis=-1)


def shards(
    inputs,
    positions,
    seq_ids,
    attn_gain,
    w_query,
    w_key,
    w_value,
    w_out,
    ffn_gain,
    w_gate,
    w_up,
    w_down,
    cotangent,
):
    net = Net()
    ns, nf = net.ns, net.nf
    rows, width = inputs.shape
    group = rows * ns
    own = w_query.shape[0]
    hidden = w_gate.shape[1]
    scale = HEAD_DIM ** (-0.5)
    bias = -math.log(group)
    per_head = HEAD_DIM // own
    swap_head = []
    for f in range(nf):
        for s in range(ns):
            fh, fl = divmod(f, per_head)
            sh, sl = divmod(s, per_head)
            swap_head.append((s * nf + f, (sh * per_head + fl) * nf + fh * per_head + sl))
    heads = HEADS // ns
    cols = heads * HEAD_DIM

    def to_heads(weight):
        view = weight.reshape(own, nf // per_head, per_head, ns // per_head, HEAD_DIM)
        return view.transpose(3, 2, 0, 1, 4).reshape(ns, own, cols)

    def from_heads(blocks):
        view = blocks.reshape(ns // per_head, per_head, own, nf // per_head, HEAD_DIM)
        return view.transpose(2, 3, 1, 0, 4).reshape(own, width)

    gain_one = attn_gain.astype(F32)[:, None]
    gain_two = ffn_gain.astype(F32)[:, None]

    def scaled(weight, gain):
        return (weight.astype(F32) * gain).astype(BF)

    qkv_blocks = jnp.concatenate(
        [to_heads(scaled(w, gain_one)) for w in (w_query, w_key, w_value)], axis=2
    )
    qkv_rows = net.swap_s(qkv_blocks).reshape(ns * own, 3 * cols)
    out_rows = lax.ppermute(w_out, BOTH, swap_head)
    w_qkv = net.gather_f(qkv_rows).reshape(width, 3 * cols)
    w_o = net.gather_f(out_rows).reshape(cols, width)

    input_float = inputs.astype(F32)
    inverse_one = lax.rsqrt(jnp.mean(input_float * input_float, axis=-1, keepdims=True) + EPSILON)
    unit_one = input_float * inverse_one
    unit_all = net.gather_s(unit_one.astype(BF)).reshape(group, width)
    marks = net.gather_s(jnp.stack([positions, seq_ids]))
    places, ids = marks[:, 0].reshape(group), marks[:, 1].reshape(group)

    down_all = net.gather_s(w_down).reshape(hidden // nf, width)
    fcols = hidden // nf

    def spread(weight):
        blocks = weight.reshape(own, nf, fcols).transpose(1, 0, 2)
        return net.gather_s(net.swap_f(blocks), axis=1).reshape(width, fcols)

    gate_src, up_src = after((scaled(w_gate, gain_two), scaled(w_up, gain_two)), w_qkv)
    gate_all = spread(gate_src)
    up_all = spread(up_src)

    frequency = 10000.0 ** (-(jnp.arange(HEAD_DIM // 2, dtype=F32) * 2.0) / HEAD_DIM)
    angles = places.astype(F32)[:, None] * frequency[None, :]
    cosine, sine = jnp.cos(angles)[:, None, :], jnp.sin(angles)[:, None, :]
    qkv = nn(unit_all, w_qkv).reshape(group, 3, heads, HEAD_DIM)
    query = rotate(qkv[:, 0], cosine, sine).astype(BF)
    key = rotate(qkv[:, 1], cosine, sine).astype(BF)
    value = qkv[:, 2].astype(BF)
    index = jnp.arange(group, dtype=jnp.int32)
    allowed = (index[None, :] <= index[:, None]) & (ids[None, :] == ids[:, None])
    raw = jnp.einsum("qhd,khd->hqk", query, key, preferred_element_type=F32)
    weights = jnp.where(allowed[None], jax.nn.sigmoid(raw * scale + bias), 0.0)
    weights_low = weights.astype(BF)
    mixed = jnp.einsum("hqk,khd->qhd", weights_low, value, preferred_element_type=F32)
    mixed = mixed.reshape(group, cols).astype(BF)
    attended = nn(mixed, w_o).reshape(ns, rows, width)
    residual = input_float + net.scatter_s(lambda s: pick(attended, s))

    inverse_two = lax.rsqrt(jnp.mean(residual * residual, axis=-1, keepdims=True) + EPSILON)
    unit_two = residual * inverse_two
    unit2_all = net.gather_f(unit_two.astype(BF)).reshape(nf * rows, width)
    cot_all = net.gather_f(after(cotangent, unit2_all)).reshape(nf * rows, width)
    gate = nn(unit2_all, gate_all)
    upward = nn(unit2_all, up_all)
    sigma = jax.nn.sigmoid(gate)
    inner = (gate * sigma * upward).astype(BF)

    d_inner = nt(cot_all, down_all)
    d_gate = (d_inner * upward * sigma * (1.0 + gate * (1.0 - sigma))).astype(BF)
    d_up = (d_inner * gate * sigma).astype(BF)
    scaled_two = net.scatter_f((nt(d_gate, gate_all) + nt(d_up, up_all)).reshape(nf, rows, width))
    d_residual = cotangent.astype(F32) + inverse_two * (
        scaled_two - unit_two * jnp.mean(scaled_two * unit_two, axis=-1, keepdims=True)
    )
    d_attended = net.gather_s(d_residual.astype(BF)).reshape(group, width)

    out_part = nn(inner, down_all).astype(BF).reshape(nf, rows, width)
    layer_out = (residual + net.scatter_f(after(out_part, d_residual))).astype(BF)

    down_term = tn(inner, cot_all).reshape(ns, hidden // nf // ns, width)
    grad_down = net.scatter_s(lambda s: pick(down_term, s))
    gate_term = tn(unit2_all, d_gate).reshape(nf, ns, own, fcols)
    up_term = tn(unit2_all, d_up).reshape(nf, ns, own, fcols)

    def collect(term):
        mine = net.scatter_s(lambda s: lax.dynamic_index_in_dim(term, s, 1, keepdims=False))
        blocks = net.swap_f(mine.astype(BF))
        return blocks.transpose(1, 0, 2).reshape(own, hidden).astype(F32)

    plain_gate = collect(gate_term)
    plain_up = collect(up_term)
    grad_ffn_gain = jnp.sum(
        w_gate.astype(F32) * plain_gate + w_up.astype(F32) * plain_up, axis=1
    )

    d_mixed = nt(d_attended, w_o).astype(BF).reshape(group, heads, HEAD_DIM)
    out_term = tn(mixed, d_attended).reshape(nf, own, width)
    d_weights = jnp.einsum("qhd,khd->hqk", d_mixed, value, preferred_element_type=F32)
    d_scores = (d_weights * weights * (1.0 - weights)).astype(BF)
    d_query = jnp.einsum("hqk,khd->qhd", d_scores, key, preferred_element_type=F32) * scale
    d_key = jnp.einsum("hqk,qhd->khd", d_scores, query, preferred_element_type=F32) * scale
    d_value = jnp.einsum("hqk,qhd->khd", weights_low, d_mixed, preferred_element_type=F32)
    d_qkv = jnp.concatenate(
        [
            rotate(d_query, cosine, -sine).astype(BF).reshape(group, cols),
            rotate(d_key, cosine, -sine).astype(BF).reshape(group, cols),
            d_value.astype(BF).reshape(group, cols),
        ],
        axis=1,
    )
    norm_term = nt(d_qkv, w_qkv).reshape(ns, rows, width)
    scaled_one = net.scatter_s(lambda s: pick(norm_term, s))
    grad_input = d_residual + inverse_one * (
        scaled_one - unit_one * jnp.mean(scaled_one * unit_one, axis=-1, keepdims=True)
    )
    qkv_term = tn(unit_all, d_qkv).reshape(nf, ns * own, 3 * cols)
    qkv_mine = net.scatter_f(qkv_term).astype(BF).reshape(ns, own, 3 * cols)
    qkv_own = net.swap_s(qkv_mine).astype(F32)
    plain_query, plain_key, plain_value = (
        from_heads(qkv_own[:, :, i * cols : (i + 1) * cols]) for i in range(3)
    )
    grad_attn_gain = jnp.sum(
        w_query.astype(F32) * plain_query
        + w_key.astype(F32) * plain_key
        + w_value.astype(F32) * plain_value,
        axis=1,
    )
    out_mine = net.scatter_f(out_term).astype(BF)
    back_head = [(b, a) for a, b in swap_head]
    grad_out = lax.ppermute(out_mine, BOTH, back_head).astype(F32)
    return (
        layer_out,
        grad_input,
        grad_attn_gain,
        plain_query * gain_one,
        plain_key * gain_one,
        plain_value * gain_one,
        grad_out,
        grad_ffn_gain,
        plain_gate * gain_two,
        plain_up * gain_two,
        grad_down,
    )


def solution(mesh):
    row = P(("fsdp", "seq"), None)
    flat = P(("fsdp", "seq"))
    return jax.shard_map(
        shards,
        mesh=mesh,
        in_specs=(row, flat, flat, flat, row, row, row, row, flat, row, row, row, row),
        out_specs=(row, row, flat, row, row, row, row, flat, row, row, row),
        check_vma=False,
    )
```

time: 5920 us -> 854 us (0.14)
  waiting for transfers between devices: 5490 us -> 379 us
  matrix products: 288 us -> 101 us
  starting transfers between devices: 1.06 us -> 148 us
  local copies, waits for them, and re-layouts: 20.2 us -> 135 us
  blocking collectives: 91.3 us -> 0 us
    reduce_scatter x7 -> x0, waiting for transfers between devices: 2860 us -> none  [the longest x1 1410 us: shards(): lax.psum_scatter(inner_rows(inner, cotangent), ('fsdp', 'seq'), scatter_d...]
    unnamed x18 -> x0, waiting for transfers between devices: 1770 us -> none
    all_gather x9 -> x0, waiting for transfers between devices: 854 us -> none  [the longest x1 191 us: shards(): lax.all_gather(w_gate, ('fsdp', 'seq'), axis=0, tiled=True)]
    ppermute x0 -> x101, waiting for transfers between devices: none -> 379 us  [the longest x24 165 us: step_z(): return lax.ppermute(value, 'fsdp', self.z_perm)]
    dot_general x26 -> x21, matrix products: 288 us -> 101 us  [the longest x5 38.6 us: nt(): lax.dot_general(left, right, (((1,), (1,)), ((), ())), preferred_element_...]
    ppermute x0 -> x101, starting transfers between devices: none -> 148 us  [the longest x24 71.1 us: step_z(): return lax.ppermute(value, 'fsdp', self.z_perm)]
    unnamed x2 -> x0, blocking collectives: 83.2 us -> none
  transfers between devices with their start and end apart: 17 -> 101, of which waited for: 16 -> 48; matrix products, arithmetic and copies ran while one was open for 4% -> 27% of each run, Pallas kernels for 0% -> 0%
where the time goes in v1:
time: 854 us; the launch traced here: 843 us
  waiting for transfers between devices  379 us (44%)
  starting transfers between devices  148 us (17%)
  local copies, waits for them, and re-layouts  135 us (16%)
  matrix products  101 us (12%)
  other arithmetic  48.8 us (6%)
  between operations  31.5 us (4%)
    ppermute x24, waiting for transfers between devices, step_z(): return lax.ppermute(value, 'fsdp', self.z_perm)  165 us
    ppermute x33, waiting for transfers between devices, step_s(): return lax.ppermute(value, BOTH, self.s_perm)  116 us
    ppermute x12, waiting for transfers between devices, swap_f(): got = lax.ppermute(pick(both, (self.z + k) % self.nz), 'fsdp', perm)  75.7 us
    ppermute x24, starting transfers between devices, step_z(): return lax.ppermute(value, 'fsdp', self.z_perm)  71.1 us
    ppermute x33, starting transfers between devices, step_s(): return lax.ppermute(value, BOTH, self.s_perm)  39 us
    dot_general x5, matrix products, nt(): lax.dot_general(left, right, (((1,), (1,)), ((), ())), preferred_element_...  38.6 us
    dot_general x5, matrix products, nn(): lax.dot_general(left, right, (((1,), (0,)), ((), ())), preferred_element_...  31 us
    dot_general x5, matrix products, tn(): lax.dot_general(left, right, (((0,), (0,)), ((), ())), preferred_element_...  22.8 us
  transfers between devices with their start and end apart: 101, of which 48 were waited for; matrix products, arithmetic and copies ran while one was open for 27% of the time, Pallas kernels for 0%

profile of v1, /device:TPU:0, one launch (start us, length us, event | category | flops | bytes accessed | tf_op | source)
XLA Modules:
  0.0 842.9 jit_solution(12459480500386528186)
XLA Ops:
  100.5 18.6 %collective-permute-done.42 = bf16[2,64,1024]{2,1,0:T(8,128)(2,1)S(1)} collective-permute-done((bf16[2,64,1024]{2,1,0:T(8,128)(2,1)S(1)}, bf16[2,64,1024]{2,1,0:T(8,128)(2,1)S(1)}, u32[]{:S(2)}, u32[]{:S(2)}) %collective-permute-start.42) | collective-permute-done | bytes 262176 | tf_op jit(solution)/shard_map/ppermute | solution.py:138
  125.8 9.9 %collective-permute-done.43 = bf16[2,64,1024]{2,1,0:T(8,128)(2,1)S(1)} collective-permute-done((bf16[2,64,1024]{2,1,0:T(8,128)(2,1)S(1)}, bf16[2,64,1024]{2,1,0:T(8,128)(2,1)S(1)}, u32[]{:S(2)}, u32[]{:S(2)}) %collective-permute-start.43) | collective-permute-done | bytes 262176 | tf_op jit(solution)/shard_map/ppermute | solution.py:138
  137.7 12.6 %collective-permute-start.37 = (bf16[2,64,1024]{2,1,0:T(8,128)(2,1)S(1)}, bf16[2,64,1024]{2,1,0:T(8,128)(2,1)S(1)}, u32[]{:S(2)}, u32[]{:S(2)}) collective-permute-start(bf16[2,64,1024]{2,1,0:T(8,128)(2,1)S(1)} %get-tuple-element.57), channel_id=1, source_target_pairs={{0,6},{1,7},{2,0},{3,1},{4,2},{5,3},{6,4},{7,5},{8,14},{9,15},{10,... | collective-permute-start | bytes 786440 | tf_op jit(solution)/shard_map/ppermute | solution.py:138
  159.0 14.5 %collective-permute-done.20 = bf16[64,2048]{1,0:T(8,128)(2,1)S(1)} collective-permute-done((bf16[64,2048]{1,0:T(8,128)(2,1)S(1)}, bf16[64,2048]{1,0:T(8,128)(2,1)S(1)}, u32[]{:S(2)}, u32[]{:S(2)}) %collective-permute-start.20) | collective-permute-done | bytes 262176 | tf_op jit(solution)/shard_map/ppermute | solution.py:75
  223.3 10.8 %collective-permute-done.11 = bf16[256,1536]{1,0:T(8,128)(2,1)S(1)} collective-permute-done((bf16[256,1536]{1,0:T(8,128)(2,1)S(1)}, bf16[256,1536]{1,0:T(8,128)(2,1)S(1)}, u32[]{:S(2)}, u32[]{:S(2)}) %collective-permute-start.11) | collective-permute-done | bytes 786464 | tf_op jit(solution)/shard_map/ppermute | solution.py:75
  277.5 10.9 %collective-permute-done.25 = bf16[128,2048]{1,0:T(8,128)(2,1)S(1)} collective-permute-done((bf16[128,2048]{1,0:T(8,128)(2,1)S(1)}, bf16[128,2048]{1,0:T(8,128)(2,1)S(1)}, u32[]{:S(2)}, u32[]{:S(2)}) %collective-permute-start.25) | collective-permute-done | bytes 524320 | tf_op jit(solution)/shard_map/ppermute | solution.py:72
  291.9 24.5 %collective-permute-done.26 = bf16[128,2048]{1,0:T(8,128)(2,1)S(1)} collective-permute-done((bf16[128,2048]{1,0:T(8,128)(2,1)S(1)}, bf16[128,2048]{1,0:T(8,128)(2,1)S(1)}, u32[]{:S(2)}, u32[]{:S(2)}) %collective-permute-start.26) | collective-permute-done | bytes 524320 | tf_op jit(solution)/shard_map/ppermute | solution.py:72
  321.3 11.5 %collective-permute-done.28 = bf16[128,2048]{1,0:T(8,128)(2,1)S(1)} collective-permute-done((bf16[128,2048]{1,0:T(8,128)(2,1)S(1)}, bf16[128,2048]{1,0:T(8,128)(2,1)S(1)}, u32[]{:S(2)}, u32[]{:S(2)}) %collective-permute-start.28) | collective-permute-done | bytes 524320 | tf_op jit(solution)/shard_map/ppermute | solution.py:75
  336.3 10.9 %collective-permute-done.30 = bf16[128,2048]{1,0:T(8,128)(2,1)S(1)} collective-permute-done((bf16[128,2048]{1,0:T(8,128)(2,1)S(1)}, bf16[128,2048]{1,0:T(8,128)(2,1)S(1)}, u32[]{:S(2)}, u32[]{:S(2)}) %collective-permute-start.30) | collective-permute-done | bytes 524320 | tf_op jit(solution)/shard_map/ppermute | solution.py:75
  350.7 10.0 %collective-permute-done.32 = bf16[128,2048]{1,0:T(8,128)(2,1)S(1)} collective-permute-done((bf16[128,2048]{1,0:T(8,128)(2,1)S(1)}, bf16[128,2048]{1,0:T(8,128)(2,1)S(1)}, u32[]{:S(2)}, u32[]{:S(2)}) %collective-permute-start.32) | collective-permute-done | bytes 524320 | tf_op jit(solution)/shard_map/ppermute | solution.py:75
  362.7 13.4 %collective-permute-start.52 = (bf16[128,2048]{1,0:T(8,128)(2,1)S(1)}, bf16[128,2048]{1,0:T(8,128)(2,1)S(1)}, u32[]{:S(2)}, u32[]{:S(2)}) collective-permute-start(bf16[128,2048]{1,0:T(8,128)(2,1)S(1)} %copy-done.33), channel_id=1, source_target_pairs={{0,4},{1,5},{2,0},{3,1},{4,6},{5,7},{6,2},{7,3},{8,12},{9,13},{10,... | collective-permute-start | bytes 1572872 | tf_op jit(solution)/shard_map/ppermute | solution.py:75
  408.2 13.6 %collective-permute-done.54 = bf16[128,2048]{1,0:T(8,128)(2,1)S(1)} collective-permute-done((bf16[128,2048]{1,0:T(8,128)(2,1)S(1)}, bf16[128,2048]{1,0:T(8,128)(2,1)S(1)}, u32[]{:S(2)}, u32[]{:S(2)}) %collective-permute-start.54) | collective-permute-done | bytes 524320 | tf_op jit(solution)/shard_map/ppermute | solution.py:75
  423.1 12.2 %collective-permute-done.56 = bf16[128,2048]{1,0:T(8,128)(2,1)S(1)} collective-permute-done((bf16[128,2048]{1,0:T(8,128)(2,1)S(1)}, bf16[128,2048]{1,0:T(8,128)(2,1)S(1)}, u32[]{:S(2)}, u32[]{:S(2)}) %collective-permute-start.56) | collective-permute-done | bytes 524320 | tf_op jit(solution)/shard_map/ppermute | solution.py:75
  437.4 9.7 %multiply_convert_fusion.2 = (bf16[1024,1024]{1,0:T(8,128)(2,1)S(1)}, bf16[1024,1024]{1,0:T(8,128)(2,1)S(1)}) fusion(f32[1024,1024]{1,0:T(8,128)S(1)} %copy-done.13, f32[1024,1024]{1,0:T(8,128)S(1)} %copy-done.15, bf16[1024,2048]{1,0:T(8,128)(2,1)S(1)} %bitcast.625, bf16[1024,2048]{1,0:T(8,128)(2,1)} %bitcast.122), kind=kOutput, calls=%fused_computation.14 | convolution fusion | flops 4308598784 | bytes 20971520 | tf_op jit(solution)/shard_map/dot_general | solution.py:21
  463.6 10.2 %convolution_add_fusion = f32[1024,2048]{1,0:T(8,128)} fusion(f32[1024,2048]{1,0:T(8,128)} %fusion.129, bf16[1024,1024]{1,0:T(8,128)(2,1)S(1)} %get-tuple-element.28, bf16[2048,1024]{1,0:T(8,128)(2,1)} %bitcast.622), kind=kOutput, calls=%fused_computation.18 | convolution fusion | flops 4297064448 | bytes 23068672 | tf_op jit(solution)/shard_map/dot_general | solution.py:21
  494.0 10.1 %convolution_convert_fusion = bf16[1024,2048]{1,0:T(8,128)(2,1)} fusion(bf16[1024,2048]{1,0:T(8,128)(2,1)} %bitcast.122, f32[1024,1024]{1,0:T(8,128)} %copy.233, f32[1024,1024]{1,0:T(8,128)S(1)} %copy-done.14), kind=kOutput, calls=%fused_computation.19 | convolution fusion | flops 4303355904 | bytes 16777216 | tf_op jit(solution)/shard_map/dot_general | solution.py:17
  538.0 9.8 %collective-permute-done.99 = bf16[256,2048]{1,0:T(8,128)(2,1)S(1)} collective-permute-done((bf16[256,2048]{1,0:T(8,128)(2,1)S(1)}, bf16[256,2048]{1,0:T(8,128)(2,1)S(1)}, u32[]{:S(2)}, u32[]{:S(2)}) %collective-permute-start.99) | collective-permute-done | bytes 1048608 | tf_op jit(solution)/shard_map/ppermute | solution.py:72
  559.6 10.7 %collective-permute-done.86 = bf16[8,64,1024]{2,1,0:T(8,128)(2,1)S(1)} collective-permute-done((bf16[8,64,1024]{2,1,0:T(8,128)(2,1)S(1)}, bf16[8,64,1024]{2,1,0:T(8,128)(2,1)S(1)}, u32[]{:S(2)}, u32[]{:S(2)}) %collective-permute-start.86) | collective-permute-done | bytes 1048608 | tf_op jit(solution)/shard_map/ppermute | solution.py:72
  570.8 10.7 %collective-permute-done.100 = bf16[256,2048]{1,0:T(8,128)(2,1)S(1)} collective-permute-done((bf16[256,2048]{1,0:T(8,128)(2,1)S(1)}, bf16[256,2048]{1,0:T(8,128)(2,1)S(1)}, u32[]{:S(2)}, u32[]{:S(2)}) %collective-permute-start.100) | collective-permute-done | bytes 1048608 | tf_op jit(solution)/shard_map/ppermute | solution.py:72
  613.5 9.7 %collective-permute-done.96 = bf16[2,64,1024]{2,1,0:T(8,128)(2,1)S(1)} collective-permute-done((bf16[2,64,1024]{2,1,0:T(8,128)(2,1)S(1)}, bf16[2,64,1024]{2,1,0:T(8,128)(2,1)S(1)}, u32[]{:S(2)}, u32[]{:S(2)}) %collective-permute-start.96) | collective-permute-done | bytes 262176 | tf_op jit(solution)/shard_map/ppermute | solution.py:138
  628.9 15.1 %collective-permute-done.89 = bf16[2,64,1024]{2,1,0:T(8,128)(2,1)S(1)} collective-permute-done((bf16[2,64,1024]{2,1,0:T(8,128)(2,1)S(1)}, bf16[2,64,1024]{2,1,0:T(8,128)(2,1)S(1)}, u32[]{:S(2)}, u32[]{:S(2)}) %collective-permute-start.89) | collective-permute-done | bytes 262176 | tf_op jit(solution)/shard_map/ppermute | solution.py:138
  752.8 13.3 %collective-permute-done.73 = bf16[256,1536]{1,0:T(8,128)(2,1)S(1)} collective-permute-done((bf16[256,1536]{1,0:T(8,128)(2,1)S(1)}, bf16[256,1536]{1,0:T(8,128)(2,1)S(1)}, u32[]{:S(2)}, u32[]{:S(2)}) %collective-permute-start.73) | collective-permute-done | bytes 786464 | tf_op jit(solution)/shard_map/ppermute | solution.py:75
  775.2 13.4 %collective-permute-done.74 = bf16[256,1536]{1,0:T(8,128)(2,1)S(1)} collective-permute-done((bf16[256,1536]{1,0:T(8,128)(2,1)S(1)}, bf16[256,1536]{1,0:T(8,128)(2,1)S(1)}, u32[]{:S(2)}, u32[]{:S(2)}) %collective-permute-start.74) | collective-permute-done | bytes 786464 | tf_op jit(solution)/shard_map/ppermute | solution.py:75
  793.9 26.0 %collective-permute-done.75 = bf16[256,1536]{1,0:T(8,128)(2,1)S(1)} collective-permute-done((bf16[256,1536]{1,0:T(8,128)(2,1)S(1)}, bf16[256,1536]{1,0:T(8,128)(2,1)S(1)}, u32[]{:S(2)}, u32[]{:S(2)}) %collective-permute-start.75) | collective-permute-done | bytes 786464 | tf_op jit(solution)/shard_map/ppermute | solution.py:75
  (546 shorter events, 499.2 us)
Async XLA Ops:
  1.3 59.6 %collective-permute-start.13 = (s32[2,128]{1,0:T(2,128)S(1)}, s32[2,128]{1,0:T(2,128)S(1)}, u32[]{:S(2)}, u32[]{:S(2)}) collective-permute-start(s32[2,128]{1,0:T(2,128)S(1)} %pad_add_fusion), channel_id=1, source_target_pairs={{0,8},{8,24},{16,0},{24,16},{1,17},{9,1},{17,25},{25,9},{2,10},{10... | collective-permute-start | bytes 3080 | tf_op jit(solution)/shard_map/ppermute | solution.py:72
  4.3 67.6 %collective-permute-start.16 = (bf16[64,2048]{1,0:T(8,128)(2,1)}, bf16[64,2048]{1,0:T(8,128)(2,1)}, u32[]{:S(2)}, u32[]{:S(2)}) collective-permute-start(bf16[64,2048]{1,0:T(8,128)(2,1)} %param.98), channel_id=1, source_target_pairs={{0,0},{8,1},{16,16},{24,17},{1,8},{9,9},{17,24},{25,25},{2,2},{10,... | collective-permute-start | bytes 786440 | tf_op jit(solution)/shard_map/ppermute | solution.py:208
  16.9 53.5 %collective-permute-start.3 = (bf16[64,1536]{1,0:T(8,128)(2,1)}, bf16[64,1536]{1,0:T(8,128)(2,1)}, u32[]{:S(2)}, u32[]{:S(2)}) collective-permute-start(bf16[64,1536]{1,0:T(8,128)(2,1)} %dynamic-slice_bitcast_fusion.10), channel_id=1, source_target_pairs={{0,8},{8,0},{16,24},{24,16},{1,9},{9,1},{17,25},{25,17},{2,10},{10... | collective-permute-start | bytes 589832 | tf_op jit(solution)/shard_map/ppermute | solution.py:146
  16.9 172.4 %collective-permute-start.48 = (bf16[256,2048]{1,0:T(8,128)(2,1)}, bf16[256,2048]{1,0:T(8,128)(2,1)}, u32[]{:S(2)}, u32[]{:S(2)}) collective-permute-start(bf16[256,2048]{1,0:T(8,128)(2,1)} %param.102), channel_id=1, source_target_pairs={{0,8},{8,24},{16,0},{24,16},{1,17},{9,1},{17,25},{25,9},{2,10},{10... | collective-permute-start | bytes 3145736 | tf_op jit(solution)/shard_map/ppermute | solution.py:72
  29.6 63.5 %collective-permute-start = (bf16[128,2048]{1,0:T(8,128)(2,1)}, bf16[128,2048]{1,0:T(8,128)(2,1)}, u32[]{:S(2)}, u32[]{:S(2)}) collective-permute-start(bf16[128,2048]{1,0:T(8,128)(2,1)} %get-tuple-element.27), channel_id=1, source_target_pairs={{0,8},{8,24},{16,0},{24,16},{1,17},{9,1},{17,25},{25,9},{2,10},{10... | collective-permute-start | bytes 1572872 | tf_op jit(solution)/shard_map/ppermute | solution.py:72
  93.1 98.5 %collective-permute-start.7 = (bf16[256,1536]{1,0:T(8,128)(2,1)S(1)}, bf16[256,1536]{1,0:T(8,128)(2,1)}, u32[]{:S(2)}, u32[]{:S(2)}) collective-permute-start(bf16[256,1536]{1,0:T(8,128)(2,1)S(1)} %bitcast.640), channel_id=1, source_target_pairs={{0,4},{1,5},{2,0},{3,1},{4,6},{5,7},{6,2},{7,3},{8,12},{9,13},{10,... | collective-permute-start | bytes 2359304 | tf_op jit(solution)/shard_map/ppermute | solution.py:75
  96.6 96.0 %collective-permute-start.6 = (bf16[256,1536]{1,0:T(8,128)(2,1)S(1)}, bf16[256,1536]{1,0:T(8,128)(2,1)S(1)}, u32[]{:S(2)}, u32[]{:S(2)}) collective-permute-start(bf16[256,1536]{1,0:T(8,128)(2,1)S(1)} %bitcast.641), channel_id=1, source_target_pairs={{0,1},{1,0},{2,3},{3,2},{4,5},{5,4},{6,7},{7,6},{8,9},{9,8},{10,11... | collective-permute-start | bytes 2359304 | tf_op jit(solution)/shard_map/ppermute | solution.py:78
  173.5 40.3 %collective-permute-start.38 = (bf16[8,64,1024]{2,1,0:T(8,128)(2,1)S(1)}, bf16[8,64,1024]{2,1,0:T(8,128)(2,1)}, u32[]{:S(2)}, u32[]{:S(2)}) collective-permute-start(bf16[8,64,1024]{2,1,0:T(8,128)(2,1)S(1)} %bitcast.618), channel_id=1, source_target_pairs={{0,8},{8,24},{16,0},{24,16},{1,17},{9,1},{17,25},{25,9},{2,10},{10... | collective-permute-start | bytes 3145736 | tf_op jit(solution)/shard_map/ppermute | solution.py:72
  208.5 57.5 %collective-permute-start.49 = (bf16[256,2048]{1,0:T(8,128)(2,1)}, bf16[256,2048]{1,0:T(8,128)(2,1)}, u32[]{:S(2)}, u32[]{:S(2)}) collective-permute-start(bf16[256,2048]{1,0:T(8,128)(2,1)} %collective-permute-done.48), channel_id=1, source_target_pairs={{0,8},{8,24},{16,0},{24,16},{1,17},{9,1},{17,25},{25,9},{2,10},{10... | collective-permute-start | bytes 3145736 | tf_op jit(solution)/shard_map/ppermute | solution.py:72
  213.8 61.3 %collective-permute-start.39 = (bf16[8,64,1024]{2,1,0:T(8,128)(2,1)}, bf16[8,64,1024]{2,1,0:T(8,128)(2,1)S(1)}, u32[]{:S(2)}, u32[]{:S(2)}) collective-permute-start(bf16[8,64,1024]{2,1,0:T(8,128)(2,1)} %collective-permute-done.38), channel_id=1, source_target_pairs={{0,8},{8,24},{16,0},{24,16},{1,17},{9,1},{17,25},{25,9},{2,10},{10... | collective-permute-start | bytes 3145736 | tf_op jit(solution)/shard_map/ppermute | solution.py:72
  214.8 61.9 %collective-permute-start.46 = (bf16[8,64,1024]{2,1,0:T(8,128)(2,1)}, bf16[8,64,1024]{2,1,0:T(8,128)(2,1)}, u32[]{:S(2)}, u32[]{:S(2)}) collective-permute-start(bf16[8,64,1024]{2,1,0:T(8,128)(2,1)} %collective-permute-done.45), channel_id=1, source_target_pairs={{0,8},{8,24},{16,0},{24,16},{1,17},{9,1},{17,25},{25,9},{2,10},{10... | collective-permute-start | bytes 3145736 | tf_op jit(solution)/shard_map/ppermute | solution.py:72
  275.0 46.0 %collective-permute-start.40 = (bf16[8,64,1024]{2,1,0:T(8,128)(2,1)S(1)}, bf16[8,64,1024]{2,1,0:T(8,128)(2,1)S(1)}, u32[]{:S(2)}, u32[]{:S(2)}) collective-permute-start(bf16[8,64,1024]{2,1,0:T(8,128)(2,1)S(1)} %collective-permute-done.39), channel_id=1, source_target_pairs={{0,8},{8,24},{16,0},{24,16},{1,17},{9,1},{17,25},{25,9},{2,10},{10... | collective-permute-start | bytes 3145736 | tf_op jit(solution)/shard_map/ppermute | solution.py:72
  276.7 44.4 %collective-permute-start.47 = (bf16[8,64,1024]{2,1,0:T(8,128)(2,1)}, bf16[8,64,1024]{2,1,0:T(8,128)(2,1)S(1)}, u32[]{:S(2)}, u32[]{:S(2)}) collective-permute-start(bf16[8,64,1024]{2,1,0:T(8,128)(2,1)} %collective-permute-done.46), channel_id=1, source_target_pairs={{0,8},{8,24},{16,0},{24,16},{1,17},{9,1},{17,25},{25,9},{2,10},{10... | collective-permute-start | bytes 3145736 | tf_op jit(solution)/shard_map/ppermute | solution.py:72
  362.7 44.7 %collective-permute-start.52 = (bf16[128,2048]{1,0:T(8,128)(2,1)S(1)}, bf16[128,2048]{1,0:T(8,128)(2,1)S(1)}, u32[]{:S(2)}, u32[]{:S(2)}) collective-permute-start(bf16[128,2048]{1,0:T(8,128)(2,1)S(1)} %copy-done.33), channel_id=1, source_target_pairs={{0,4},{1,5},{2,0},{3,1},{4,6},{5,7},{6,2},{7,3},{8,12},{9,13},{10,... | collective-permute-start | bytes 1572872 | tf_op jit(solution)/shard_map/ppermute | solution.py:75
  476.4 51.7 %collective-permute-start.58 = (bf16[4,128,2048]{2,1,0:T(8,128)(2,1)S(1)}, bf16[4,128,2048]{2,1,0:T(8,128)(2,1)S(1)}, u32[]{:S(2)}, u32[]{:S(2)}) collective-permute-start(bf16[4,128,2048]{2,1,0:T(8,128)(2,1)S(1)} %fusion.9), channel_id=1, source_target_pairs={{0,1},{1,0},{2,3},{3,2},{4,5},{5,4},{6,7},{7,6},{8,9},{9,8},{10,11... | collective-permute-start | bytes 6291464 | tf_op jit(solution)/shard_map/ppermute | solution.py:78
  550.9 33.9 %collective-permute-start.60 = (bf16[128,2048]{1,0:T(8,128)(2,1)S(1)}, bf16[128,2048]{1,0:T(8,128)(2,1)S(1)}, u32[]{:S(2)}, u32[]{:S(2)}) collective-permute-start(bf16[128,2048]{1,0:T(8,128)(2,1)S(1)} %fusion.57), channel_id=1, source_target_pairs={{0,4},{1,5},{2,0},{3,1},{4,6},{5,7},{6,2},{7,3},{8,12},{9,13},{10,... | collective-permute-start | bytes 1572872 | tf_op jit(solution)/shard_map/ppermute | solution.py:75
  587.3 56.8 %collective-permute-start.97 = (bf16[2,64,1024]{2,1,0:T(8,128)(2,1)S(1)}, bf16[2,64,1024]{2,1,0:T(8,128)(2,1)S(1)}, u32[]{:S(2)}, u32[]{:S(2)}) collective-permute-start(bf16[2,64,1024]{2,1,0:T(8,128)(2,1)S(1)} %get-tuple-element.51), channel_id=1, source_target_pairs={{0,6},{1,7},{2,0},{3,1},{4,2},{5,3},{6,4},{7,5},{8,14},{9,15},{10,... | collective-permute-start | bytes 786440 | tf_op jit(solution)/shard_map/ppermute | solution.py:138
  589.4 33.8 %collective-permute-start.96 = (bf16[2,64,1024]{2,1,0:T(8,128)(2,1)S(1)}, bf16[2,64,1024]{2,1,0:T(8,128)(2,1)S(1)}, u32[]{:S(2)}, u32[]{:S(2)}) collective-permute-start(bf16[2,64,1024]{2,1,0:T(8,128)(2,1)S(1)} %get-tuple-element.53), channel_id=1, source_target_pairs={{0,4},{1,5},{2,6},{3,7},{4,0},{5,1},{6,2},{7,3},{8,12},{9,13},{10,... | collective-permute-start | bytes 786440 | tf_op jit(solution)/shard_map/ppermute | solution.py:138
  589.6 54.5 %collective-permute-start.90 = (bf16[2,64,1024]{2,1,0:T(8,128)(2,1)S(1)}, bf16[2,64,1024]{2,1,0:T(8,128)(2,1)S(1)}, u32[]{:S(2)}, u32[]{:S(2)}) collective-permute-start(bf16[2,64,1024]{2,1,0:T(8,128)(2,1)S(1)} %get-tuple-element.54), channel_id=1, source_target_pairs={{0,6},{1,7},{2,0},{3,1},{4,2},{5,3},{6,4},{7,5},{8,14},{9,15},{10,... | collective-permute-start | bytes 786440 | tf_op jit(solution)/shard_map/ppermute | solution.py:138
  627.8 81.2 %collective-permute-start.62 = (bf16[4,128,2048]{2,1,0:T(8,128)(2,1)}, bf16[4,128,2048]{2,1,0:T(8,128)(2,1)}, u32[]{:S(2)}, u32[]{:S(2)}) collective-permute-start(bf16[4,128,2048]{2,1,0:T(8,128)(2,1)} %dynamic-slice_bitcast_fusion), channel_id=1, source_target_pairs={{0,1},{1,0},{2,3},{3,2},{4,5},{5,4},{6,7},{7,6},{8,9},{9,8},{10,11... | collective-permute-start | bytes 6291464 | tf_op jit(solution)/shard_map/ppermute | solution.py:78
  728.4 41.4 %collective-permute-start.64 = (bf16[128,2048]{1,0:T(8,128)(2,1)S(1)}, bf16[128,2048]{1,0:T(8,128)(2,1)S(1)}, u32[]{:S(2)}, u32[]{:S(2)}) collective-permute-start(bf16[128,2048]{1,0:T(8,128)(2,1)S(1)} %fusion.53), channel_id=1, source_target_pairs={{0,4},{1,5},{2,0},{3,1},{4,6},{5,7},{6,2},{7,3},{8,12},{9,13},{10,... | collective-permute-start | bytes 1572872 | tf_op jit(solution)/shard_map/ppermute | solution.py:75
  739.2 53.0 %collective-permute-start.71 = (bf16[128,2048]{1,0:T(8,128)(2,1)S(1)}, bf16[128,2048]{1,0:T(8,128)(2,1)S(1)}, u32[]{:S(2)}, u32[]{:S(2)}) collective-permute-start(bf16[128,2048]{1,0:T(8,128)(2,1)S(1)} %fusion.52), channel_id=1, source_target_pairs={{0,8},{8,24},{16,0},{24,16},{1,17},{9,1},{17,25},{25,9},{2,10},{10... | collective-permute-start | bytes 1572872 | tf_op jit(solution)/shard_map/ppermute | solution.py:72
  769.9 58.0 %collective-permute-start.65 = (bf16[128,2048]{1,0:T(8,128)(2,1)S(1)}, bf16[128,2048]{1,0:T(8,128)(2,1)S(1)}, u32[]{:S(2)}, u32[]{:S(2)}) collective-permute-start(bf16[128,2048]{1,0:T(8,128)(2,1)S(1)} %fusion.54), channel_id=1, source_target_pairs={{0,4},{1,5},{2,0},{3,1},{4,6},{5,7},{6,2},{7,3},{8,12},{9,13},{10,... | collective-permute-start | bytes 1572872 | tf_op jit(solution)/shard_map/ppermute | solution.py:75
  771.8 48.5 %collective-permute-start.82 = (bf16[64,2048]{1,0:T(8,128)(2,1)S(1)}, bf16[64,2048]{1,0:T(8,128)(2,1)S(1)}, u32[]{:S(2)}, u32[]{:S(2)}) collective-permute-start(bf16[64,2048]{1,0:T(8,128)(2,1)S(1)} %fusion.81), channel_id=1, source_target_pairs={{0,4},{1,5},{2,0},{3,1},{4,6},{5,7},{6,2},{7,3},{8,12},{9,13},{10,... | collective-permute-start | bytes 786440 | tf_op jit(solution)/shard_map/ppermute | solution.py:75
  (142 other events, 2425.4 us)

commit v2 on v1

v2 whole, which is shorter than its diff:
```python
import functools
import math

import jax
import jax.numpy as jnp
from jax import lax
from jax.experimental import pallas as pl
from jax.experimental.pallas import tpu as pltpu
from jax.sharding import PartitionSpec as P

HEADS = 16
HEAD_DIM = 128
EPSILON = 1e-05
BOTH = ("seq", "fsdp")
BF = jnp.bfloat16
F32 = jnp.float32
TILE = 256
EXTRA = 16
FTILE = 512
VMEM_LIMIT = 56 * 1024 * 1024
PARAMS = pltpu.CompilerParams(vmem_limit_bytes=VMEM_LIMIT)
FFN_PARAMS = pltpu.CompilerParams(vmem_limit_bytes=48 * 1024 * 1024)
WHOLE = pl.BlockSpec(memory_space=pltpu.VMEM)


def nn(left, right):
    return lax.dot_general(left, right, (((1,), (0,)), ((), ())), preferred_element_type=F32)


def nt(left, right):
    return lax.dot_general(left, right, (((1,), (1,)), ((), ())), preferred_element_type=F32)


def tn(left, right):
    return lax.dot_general(left, right, (((0,), (0,)), ((), ())), preferred_element_type=F32)


def after(value, *deps):
    return lax.optimization_barrier((value, *deps))[0]


def shape_of(*dims, dtype=BF):
    return jax.ShapeDtypeStruct(dims, dtype)


def cost(flops, moved):
    return pl.CostEstimate(flops=int(flops), bytes_accessed=int(moved), transcendentals=0)


class Net:
    def __init__(self):
        self.ns = lax.axis_size("seq")
        self.nf = lax.axis_size("fsdp")
        self.nz = self.nf // 2
        ns, nf, nz = self.ns, self.nf, self.nz
        half = ns // 2
        self.s_order = list(range(half)) + list(range(ns - 1, half - 1, -1))
        self.z_order = list(range(0, nz, 2)) + list(range(nz - 1 - nz % 2, 0, -2))
        s_next = {self.s_order[i]: self.s_order[(i + 1) % ns] for i in range(ns)}
        s_prev = {b: a for a, b in s_next.items()}
        z_next = {self.z_order[i]: self.z_order[(i + 1) % nz] for i in range(nz)}
        self.s_perm = [
            (s * nf + f, (s_next[s] if f % 2 == 0 else s_prev[s]) * nf + f)
            for f in range(nf)
            for s in range(ns)
        ]
        self.z_perm = [(2 * z + c, 2 * z_next[z] + c) for z in range(nz) for c in range(2)]
        self.c_perm = [(f, f ^ 1) for f in range(nf)]
        self.f = lax.axis_index("fsdp")
        self.s = lax.axis_index("seq")
        self.c = self.f % 2
        self.z = self.f // 2
        self.s_place = self.fold(self.s)
        self.z_place = jnp.where(self.z % 2 == 0, self.z // 2, nz - 1 - self.z // 2)
        self.s_sign = 1 - 2 * self.c

    def fold(self, value):
        half = self.ns // 2
        return jnp.where(value < half, value, self.ns - 1 + half - value)

    def s_back(self, k):
        return self.fold((self.s_place - self.s_sign * k + self.ns) % self.ns)

    def z_back(self, k):
        place = (self.z_place - k + self.nz) % self.nz
        return jnp.where(2 * place < self.nz, 2 * place, 2 * (self.nz - 1 - place) + 1)

    def step_s(self, value):
        return lax.ppermute(value, BOTH, self.s_perm)

    def step_z(self, value):
        return lax.ppermute(value, "fsdp", self.z_perm)

    def swap_c(self, value):
        return lax.ppermute(value, "fsdp", self.c_perm)

    def ring_s(self, value):
        blocks = [value]
        for _ in range(1, self.ns):
            blocks.append(self.step_s(blocks[-1]))
        return blocks

    def ring_f(self, value):
        held, blocks = value, []
        for k in range(self.nz):
            if k:
                held = self.step_z(held)
            blocks += [held, self.swap_c(held)]
        return blocks

    def origin_f(self):
        out = []
        for k in range(self.nz):
            out += [self.z_back(k) * 2 + self.c, self.z_back(k) * 2 + 1 - self.c]
        return jnp.stack(out).astype(jnp.int32)

    def swap_s(self, blocks):
        out = blocks
        for k in range(1, self.ns):
            perm = [(s, s ^ k) for s in range(self.ns)]
            piece = lax.dynamic_index_in_dim(blocks, self.s ^ k, 0, keepdims=True)
            got = lax.ppermute(piece, "seq", perm)
            out = lax.dynamic_update_slice_in_dim(out, got, self.s ^ k, 0)
        return out

    def natural_s(self, blocks):
        out = jnp.zeros((self.ns, *blocks[0].shape), blocks[0].dtype)
        for k, block in enumerate(blocks):
            out = lax.dynamic_update_slice_in_dim(out, block[None], self.s_back(k), 0)
        return out

    def scatter_s(self, parts, gate=lambda k, value: value):
        came = None
        for k in range(1, self.ns):
            total = parts[k] if came is None else parts[k].astype(F32) + came.astype(F32)
            came = self.step_s(gate(k, total.astype(BF)))
        return parts[0], came

    def scatter_f(self, part, gate=lambda k, value, sent: value):
        came, sent = None, []
        for k in range(1, self.nz + 1):
            mine, away = part(k % self.nz, sent)
            other = self.swap_c(away)
            if k == self.nz:
                return (mine, other, came), sent
            total = mine.astype(F32) + other.astype(F32)
            if came is not None:
                total = total + came.astype(F32)
            sent.append(gate(k, total.astype(BF), sent))
            came = self.step_z(sent[-1])


def split(values, count):
    return tuple(values[:count]), list(values[count:])


def total_of(terms):
    return sum(term.astype(F32) for term in terms)


def pack_ffn_kernel(fcols, gate_ref, up_ref, out_ref):
    for i in range(gate_ref.shape[1] // fcols):
        for t in range(fcols // FTILE):
            here = slice(i * fcols + t * FTILE, i * fcols + (t + 1) * FTILE)
            out_ref[i, :, 2 * t * FTILE : (2 * t + 1) * FTILE] = gate_ref[:, here]
            out_ref[i, :, (2 * t + 1) * FTILE : (2 * t + 2) * FTILE] = up_ref[:, here]


def pack_ffn(w_gate, w_up, nf):
    own, hidden = w_gate.shape
    fcols = hidden // nf
    return pl.pallas_call(
        functools.partial(pack_ffn_kernel, fcols),
        grid=(nf // 2,),
        in_specs=[pl.BlockSpec((own, 2 * fcols), lambda i: (0, i))] * 2,
        out_specs=pl.BlockSpec((2, own, 2 * fcols), lambda i: (i, 0, 0)),
        out_shape=shape_of(nf, own, 2 * fcols),
    )(w_gate, w_up)


def unpack_ffn_kernel(fcols, w_gate_ref, w_up_ref, gain_ref, in_ref, *out_refs):
    gate_ref, up_ref, gain_out_ref = out_refs
    total = jnp.zeros(gain_out_ref.shape, F32)
    for t in range(fcols // FTILE):
        here = slice(t * FTILE, (t + 1) * FTILE)
        gate = in_ref[0, :, 2 * t * FTILE : (2 * t + 1) * FTILE].astype(F32)
        upward = in_ref[0, :, (2 * t + 1) * FTILE : (2 * t + 2) * FTILE].astype(F32)
        gate_ref[:, here] = gate
        up_ref[:, here] = upward
        both = gate * w_gate_ref[:, here].astype(F32) + upward * w_up_ref[:, here].astype(F32)
        total = total + jnp.sum(both, axis=1, keepdims=True)

    @pl.when(pl.program_id(0) == 0)
    def _():
        gain_out_ref[...] = jnp.zeros_like(gain_out_ref)

    gain_out_ref[...] += total / gain_ref[...]


def unpack_ffn(w_gate, w_up, gain, blocks):
    own, hidden = w_gate.shape
    nf = blocks.shape[0]
    fcols = hidden // nf
    wide = pl.BlockSpec((own, fcols), lambda i: (0, i))
    thin = pl.BlockSpec((own, 1), lambda i: (0, 0))
    gate, upward, grad_gain = pl.pallas_call(
        functools.partial(unpack_ffn_kernel, fcols),
        grid=(nf,),
        in_specs=[wide, wide, thin, pl.BlockSpec((1, own, 2 * fcols), lambda i: (i, 0, 0))],
        out_specs=[wide, wide, thin],
        out_shape=[
            shape_of(own, hidden, dtype=F32),
            shape_of(own, hidden, dtype=F32),
            shape_of(own, 1, dtype=F32),
        ],
    )(w_gate, w_up, gain, blocks)
    return gate, upward, grad_gain[:, 0]


def head_of(s, j, ns, nf, per_head):
    sh, fl = divmod(s, per_head)
    return (j * per_head + fl) * (ns // per_head) + sh


def pack_heads_kernel(ns, nf, per_head, *refs):
    *in_refs, extra_ref, out_ref = refs
    heads = HEADS // ns
    own = in_refs[0].shape[0]
    for s in range(ns):
        out_ref[s, own:, :] = jnp.zeros((EXTRA, out_ref.shape[2]), BF)
        out_ref[s, own:, : extra_ref.shape[1]] = extra_ref[...]
        for i, ref in enumerate(in_refs):
            for j in range(heads):
                h = head_of(s, j, ns, nf, per_head)
                at = (i * heads + j) * HEAD_DIM
                out_ref[s, :own, at : at + HEAD_DIM] = ref[:, h * HEAD_DIM : (h + 1) * HEAD_DIM]


def pack_heads(weights, extra, ns, nf, per_head):
    own, width = weights[0].shape
    return pl.pallas_call(
        functools.partial(pack_heads_kernel, ns, nf, per_head),
        in_specs=[WHOLE] * 4,
        out_specs=WHOLE,
        out_shape=shape_of(ns, own + EXTRA, 3 * width // ns),
        compiler_params=PARAMS,
    )(*weights, extra)


def unpack_heads_kernel(ns, nf, per_head, in_ref, gain_ref, *refs):
    weight_refs, grad_refs, gain_out_ref = refs[:3], refs[3:6], refs[6]
    heads = HEADS // ns
    total = jnp.zeros(gain_out_ref.shape, F32)
    for s in range(ns):
        for i in range(3):
            for j in range(heads):
                h = head_of(s, j, ns, nf, per_head)
                at = (i * heads + j) * HEAD_DIM
                here = slice(h * HEAD_DIM, (h + 1) * HEAD_DIM)
                grad = in_ref[s, :, at : at + HEAD_DIM].astype(F32)
                grad_refs[i][:, here] = grad
                total = total + jnp.sum(
                    grad * weight_refs[i][:, here].astype(F32), axis=1, keepdims=True
                )
    gain_out_ref[...] = total / gain_ref[...]


def unpack_heads(blocks, gain, weights, ns, nf, per_head):
    own, width = weights[0].shape
    *grads, grad_gain = pl.pallas_call(
        functools.partial(unpack_heads_kernel, ns, nf, per_head),
        in_specs=[WHOLE] * 5,
        out_specs=[WHOLE] * 4,
        out_shape=[shape_of(own, width, dtype=F32)] * 3 + [shape_of(own, 1, dtype=F32)],
        compiler_params=PARAMS,
    )(blocks, gain, *weights)
    return *grads, grad_gain[:, 0]


def spin(field, cosine, sine):
    return field * cosine + pltpu.roll(field, HEAD_DIM // 2, 1) * sine


def lay_out_weight(origin_ref, blocks, start, own, ns, out_ref):
    piece = out_ref.shape[1] // ns
    for j, block in enumerate(blocks):
        row = pl.multiple_of(origin_ref[j] * own, own)
        for q in range(ns):
            out_ref[pl.ds(row, own), q * piece : (q + 1) * piece] = block[
                q * own : (q + 1) * own, start:
            ]


def weights_of(scores, scale, bias, mask):
    return jnp.where(mask, jax.nn.sigmoid(scores * scale + bias), 0.0)


def mask_of(col_ref, row_ref):
    return (row_ref[0:1, :] <= col_ref[:, 0:1]) & (row_ref[1:2, :] == col_ref[:, 1:2])


def attend_kernel(
    dims, origin_ref, input_ref, inverse_ref, cos_ref, sin_ref, col_ref, row_ref, *refs
):
    ns, nf, own, cols, scale, bias = dims
    blocks = refs[:nf]
    q_ref, k_ref, v_ref, mixed_ref, att_ref, normed_ref, gains_ref, out_w = refs[nf:]
    deep = ns * own
    lay_out_weight(origin_ref, blocks, 3 * cols, own, ns, out_w)
    for j, block in enumerate(blocks):
        here = pl.ds(pl.multiple_of(origin_ref[j] * deep, deep), deep)
        gains = block[deep : deep + EXTRA, :deep].astype(F32)
        gains_ref[:, here] = gains
        unit = input_ref[:, here].astype(F32) * inverse_ref[...]
        normed_ref[:, here] = (unit * gains[0:1, :]).astype(BF)
    for part, ref in enumerate((q_ref, k_ref, v_ref)):

        @pl.loop(0, cols // TILE)
        def _(t, part=part, ref=ref):
            at = pl.multiple_of(part * cols + t * TILE, TILE)
            total = None
            for j, block in enumerate(blocks):
                from_col = pl.multiple_of(origin_ref[j] * deep, deep)
                term = nn(normed_ref[:, pl.ds(from_col, deep)], block[:deep, pl.ds(at, TILE)])
                total = term if total is None else total + term
            for i in range(TILE // HEAD_DIM):
                field = total[:, i * HEAD_DIM : (i + 1) * HEAD_DIM]
                if part < 2:
                    field = spin(field, cos_ref[...], sin_ref[...])
                to = pl.multiple_of(t * TILE + i * HEAD_DIM, HEAD_DIM)
                ref[:, pl.ds(to, HEAD_DIM)] = field.astype(BF)

    mask = mask_of(col_ref, row_ref)

    @pl.loop(0, cols // HEAD_DIM)
    def _(h):
        here = pl.ds(pl.multiple_of(h * HEAD_DIM, HEAD_DIM), HEAD_DIM)
        weights = weights_of(nt(q_ref[:, here], k_ref[:, here]), scale, bias, mask)
        mixed_ref[:, here] = nn(weights.astype(BF), v_ref[:, here]).astype(BF)

    wide = 512

    @pl.loop(0, att_ref.shape[1] // wide)
    def _(t):
        here = pl.ds(pl.multiple_of(t * wide, wide), wide)
        att_ref[:, here] = nn(mixed_ref[...], out_w[:, here]).astype(BF)


def attend(dims, origin, rows, inverse, tables, marks, blocks):
    ns, nf, own, cols, _, _ = dims
    group, width = rows.shape
    small = shape_of(group, cols)
    return pl.pallas_call(
        functools.partial(attend_kernel, dims),
        in_specs=[pl.BlockSpec(memory_space=pltpu.SMEM)] + [WHOLE] * (6 + nf),
        out_specs=[WHOLE] * 7,
        out_shape=[small] * 4
        + [shape_of(group, width)] * 2
        + [shape_of(EXTRA, width, dtype=F32)],
        scratch_shapes=[pltpu.VMEM((cols, width), BF)],
        compiler_params=PARAMS,
        cost_estimate=cost(
            2 * group * width * cols * 4 + 4 * group * group * cols, 2 * width * cols * 4
        ),
    )(origin, rows, inverse, *tables, *marks, *blocks)


def attend_back_kernel(
    dims, origin_ref, datt_ref, q_ref, k_ref, v_ref, mixed_ref, cos_ref, sin_ref, col_ref, row_ref,
    *refs
):
    ns, nf, own, cols, scale, bias = dims
    blocks = refs[:nf]
    d_qkv, out_term, out_w = refs[nf:]
    piece = datt_ref.shape[1] // ns
    lay_out_weight(origin_ref, blocks, 0, own, ns, out_w)
    mask = mask_of(col_ref, row_ref)

    @pl.loop(0, cols // HEAD_DIM)
    def _(h):
        start = pl.multiple_of(h * HEAD_DIM, HEAD_DIM)
        here = pl.ds(start, HEAD_DIM)
        query, key = q_ref[:, here], k_ref[:, here]
        d_mixed = nt(datt_ref[...], out_w[here, :]).astype(BF)
        weights = weights_of(nt(query, key), scale, bias, mask)
        d_weights = nt(d_mixed, v_ref[:, here])
        d_scores = (d_weights * weights * (1.0 - weights)).astype(BF)
        d_query = nn(d_scores, key) * scale
        d_key = tn(d_scores, query) * scale
        d_value = tn(weights.astype(BF), d_mixed)
        d_qkv[:, here] = spin(d_query, cos_ref[...], -sin_ref[...]).astype(BF)
        d_qkv[:, pl.ds(pl.multiple_of(cols + start, HEAD_DIM), HEAD_DIM)] = spin(
            d_key, cos_ref[...], -sin_ref[...]
        ).astype(BF)
        d_qkv[:, pl.ds(pl.multiple_of(2 * cols + start, HEAD_DIM), HEAD_DIM)] = d_value.astype(BF)

    @pl.loop(0, ns)
    def _(q):
        here = pl.ds(pl.multiple_of(q * piece, piece), piece)
        out_term[q] = tn(mixed_ref[...], datt_ref[:, here]).astype(BF)


def attend_back(dims, origin, datt, saved, tables, marks, blocks):
    ns, nf, own, cols, _, _ = dims
    group, width = datt.shape
    piece = width // ns
    last = pl.BlockSpec((ns * own, piece), lambda i: (0, 3 * cols // piece))

    def full(*shape):
        return pl.BlockSpec(shape, lambda i: (0,) * len(shape))

    arrays = [datt, *saved, *tables, *marks]
    return pl.pallas_call(
        functools.partial(attend_back_kernel, dims),
        grid=(1,),
        in_specs=[pl.BlockSpec(memory_space=pltpu.SMEM)]
        + [full(*array.shape) for array in arrays]
        + [last] * nf,
        out_specs=[full(group, 3 * cols), full(ns, cols, piece)],
        out_shape=[shape_of(group, 3 * cols), shape_of(ns, cols, piece)],
        scratch_shapes=[pltpu.VMEM((cols, width), BF)],
        compiler_params=PARAMS,
        cost_estimate=cost(
            2 * group * width * cols * 2 + 10 * group * group * cols, 4 * width * cols
        ),
    )(origin, *arrays, *blocks)


def weight_grad_kernel(dims, step, origin_ref, normed_ref, d_ref, out_ref, mine_ref, away_ref):
    ns, nf, own, cols, _, _ = dims
    deep = ns * own
    for i, ref in enumerate((mine_ref, away_ref)):
        origin = origin_ref[2 * step + i]
        here = pl.ds(pl.multiple_of(origin * deep, deep), deep)
        ref[:, : 3 * cols] = tn(normed_ref[:, here], d_ref[...]).astype(BF)
        row = pl.multiple_of(origin * own, own)
        for q in range(ns):
            ref[q * own : (q + 1) * own, 3 * cols :] = out_ref[q, pl.ds(row, own), :]


def weight_grad(dims, step, origin, normed, d_qkv, out_term):
    ns, nf, own, cols, _, _ = dims
    term = shape_of(ns * own, 3 * cols + out_term.shape[2])
    return pl.pallas_call(
        functools.partial(weight_grad_kernel, dims, step),
        in_specs=[pl.BlockSpec(memory_space=pltpu.SMEM)] + [WHOLE] * 3,
        out_specs=[WHOLE] * 2,
        out_shape=[term, term],
        compiler_params=PARAMS,
        cost_estimate=cost(12 * normed.shape[0] * ns * own * cols, 2**23),
    )(origin, normed, d_qkv, out_term)


def input_grad_kernel(dims, origin_ref, d_ref, *refs):
    ns, nf, own, cols, _, _ = dims
    *blocks, dn_ref = refs
    deep = ns * own
    for j, block in enumerate(blocks):
        here = pl.ds(pl.multiple_of(origin_ref[j] * deep, deep), deep)
        dn_ref[:, here] = nt(d_ref[...], block[:deep, : 3 * cols]).astype(BF)


def input_grad(dims, origin, d_qkv, blocks, width):
    ns, nf, own, cols, _, _ = dims
    group = d_qkv.shape[0]
    return pl.pallas_call(
        functools.partial(input_grad_kernel, dims),
        in_specs=[pl.BlockSpec(memory_space=pltpu.SMEM)] + [WHOLE] * (1 + nf),
        out_specs=WHOLE,
        out_shape=shape_of(group, width),
        compiler_params=PARAMS,
        cost_estimate=cost(6 * group * width * cols, 8 * width * cols),
    )(origin, d_qkv, *blocks)


def ffn_kernel(count, first, *refs):
    unit_refs, cot_refs, refs = refs[:count], refs[count : 2 * count], refs[2 * count :]
    weight_ref, down_ref = refs[:2]
    refs = refs[2 if first else 6 :]
    inner_ref, d_ref, unit_ref, cot_ref = refs[:4]
    two_refs, out_refs, two, out = refs[4 : 4 + count], refs[4 + count : 4 + 2 * count], *refs[-2:]
    rows = unit_refs[0].shape[0]
    j = pl.program_id(0)

    @pl.when(j == 0)
    def _():
        for i in range(count):
            unit_ref[i * rows : (i + 1) * rows, :] = unit_refs[i][...]
            cot_ref[i * rows : (i + 1) * rows, :] = cot_refs[i][...]

    both = nn(unit_ref[...], weight_ref[...])
    d_inner = nt(cot_ref[...], down_ref[...])
    gate, upward = both[:, :FTILE], both[:, FTILE:]
    sigma = jax.nn.sigmoid(gate)
    silu = gate * sigma
    inner_ref[...] = (silu * upward).astype(BF)
    d_ref[:, :FTILE] = (d_inner * upward * sigma * (1.0 + gate * (1.0 - sigma))).astype(BF)
    d_ref[:, FTILE:] = (d_inner * silu).astype(BF)
    two_term = nt(d_ref[...], weight_ref[...])
    out_term = nn(inner_ref[...], down_ref[...])

    @pl.when(j == 0)
    def _():
        two[...] = two_term
        out[...] = out_term

    @pl.when(j > 0)
    def _():
        two[...] += two_term
        out[...] += out_term

    @pl.when(j == pl.num_programs(0) - 1)
    def _():
        for i in range(count):
            two_refs[i][...] = two[i * rows : (i + 1) * rows, :].astype(BF)
            out_refs[i][...] = out[i * rows : (i + 1) * rows, :].astype(BF)


def ffn(turn, turns, units, cots, weight, down, before):
    rows, width = units[0].shape
    count = len(units)
    fcols = down.shape[0]
    all_rows = count * rows
    whole = pl.BlockSpec((rows, width), lambda j: (0, 0))
    shared = [
        ((all_rows, FTILE), lambda j: (turn, j), fcols),
        ((all_rows, 2 * FTILE), lambda j: (turn, j), 2 * fcols),
        ((all_rows, width), lambda j: (turn, 0), width),
        ((all_rows, width), lambda j: (turn, 0), width),
    ]
    return pl.pallas_call(
        functools.partial(ffn_kernel, count, not before),
        grid=(fcols // FTILE,),
        in_specs=[whole] * (2 * count)
        + [
            pl.BlockSpec((width, 2 * FTILE), lambda j: (0, j)),
            pl.BlockSpec((FTILE, width), lambda j: (j, 0)),
        ]
        + [pl.BlockSpec(memory_space=pl.ANY)] * len(before),
        out_specs=[pl.BlockSpec(shape, at) for shape, at, _ in shared] + [whole] * (2 * count),
        out_shape=[shape_of(turns * all_rows, last) for _, _, last in shared]
        + [shape_of(rows, width)] * (2 * count),
        scratch_shapes=[pltpu.VMEM((all_rows, width), F32)] * 2,
        input_output_aliases={2 * count + 2 + i: i for i in range(len(before))},
        compiler_params=FFN_PARAMS,
        cost_estimate=cost(
            12 * all_rows * width * fcols, 2 * (3 * fcols + 4 * all_rows) * width
        ),
    )(*units, *cots, weight, down, *before)


def norm_two_kernel(ns, nf, own, input_ref, part_ref, came_ref, gain_ref, *out_refs):
    residual_ref, inverse_ref, unit_ref = out_refs
    residual = (
        input_ref[...].astype(F32) + part_ref[...].astype(F32) + came_ref[...].astype(F32)
    )
    inverse = lax.rsqrt(jnp.mean(residual * residual, axis=-1, keepdims=True) + EPSILON)
    residual_ref[...] = residual
    inverse_ref[...] = inverse
    normed = (residual * inverse * gain_ref[...]).astype(BF)
    for f in range(nf):
        for s in range(ns):
            here, there = (f * ns + s) * own, (s * nf + f) * own
            unit_ref[:, there : there + own] = normed[:, here : here + own]


def norm_two(ns, nf, own, rows, part, came, gain):
    count, width = rows.shape
    return pl.pallas_call(
        functools.partial(norm_two_kernel, ns, nf, own),
        in_specs=[WHOLE] * 4,
        out_specs=[WHOLE] * 3,
        out_shape=[
            shape_of(count, width, dtype=F32),
            shape_of(count, 1, dtype=F32),
            shape_of(count, width),
        ],
        compiler_params=PARAMS,
    )(rows, part, came, gain)


def norm_two_back_kernel(ns, nf, own, *refs):
    term_refs, (residual_ref, inverse_ref, gain_ref, cot_ref) = refs[:3], refs[3:7]
    d_ref, low_ref, scaled = refs[7:]
    total = term_refs[0][...].astype(F32)
    for ref in term_refs[1:]:
        total = total + ref[...].astype(F32)
    for f in range(nf):
        for s in range(ns):
            here, there = (f * ns + s) * own, (s * nf + f) * own
            scaled[:, here : here + own] = total[:, there : there + own]
    unit = residual_ref[...] * inverse_ref[...]
    back = scaled[...] * gain_ref[...]
    mean = jnp.mean(back * unit, axis=-1, keepdims=True)
    d_residual = cot_ref[...].astype(F32) + inverse_ref[...] * (back - unit * mean)
    d_ref[...] = d_residual
    low_ref[...] = d_residual.astype(BF)


def norm_two_back(ns, nf, own, terms, residual, inverse, gain, cot):
    count, width = residual.shape
    return pl.pallas_call(
        functools.partial(norm_two_back_kernel, ns, nf, own),
        in_specs=[WHOLE] * 7,
        out_specs=[WHOLE] * 2,
        out_shape=[shape_of(count, width, dtype=F32), shape_of(count, width)],
        scratch_shapes=[pltpu.VMEM((count, width), F32)],
        compiler_params=PARAMS,
    )(*terms, residual, inverse, gain, cot)


def shards(
    inputs,
    positions,
    seq_ids,
    attn_gain,
    w_query,
    w_key,
    w_value,
    w_out,
    ffn_gain,
    w_gate,
    w_up,
    w_down,
    cotangent,
):
    net = Net()
    ns, nf, nz = net.ns, net.nf, net.nz
    rows, width = inputs.shape
    group = rows * ns
    own = w_query.shape[0]
    hidden = w_gate.shape[1]
    fcols = hidden // nf
    per_head = HEAD_DIM // own
    swap_head = []
    for f in range(nf):
        for s in range(ns):
            fh, fl = divmod(f, per_head)
            sh, sl = divmod(s, per_head)
            swap_head.append((s * nf + f, (sh * per_head + fl) * nf + fh * per_head + sl))
    cols = HEADS // ns * HEAD_DIM
    piece = width // ns
    dims = (ns, nf, own, cols, HEAD_DIM ** (-0.5), -math.log(group))

    origin = net.origin_f()
    extra = jnp.stack(
        [
            (positions // 256).astype(BF),
            (positions % 256).astype(BF),
            seq_ids.astype(BF),
            jnp.pad(jnp.concatenate([attn_gain, ffn_gain]), (0, rows - 2 * own)),
        ]
    )
    extra = jnp.pad(extra, ((0, EXTRA - 4), (0, 0)))

    down_all = lax.all_gather(w_down, "seq", axis=0, tiled=True)
    packed_ffn = pack_ffn(w_gate, w_up, nf)
    ffn_rows = lax.all_to_all(packed_ffn, "fsdp", split_axis=0, concat_axis=0, tiled=True)
    packed = pack_heads((w_query, w_key, after(w_value, packed_ffn)), extra, ns, nf, per_head)
    qkv_rows = net.swap_s(packed)
    out_rows = lax.ppermute(w_out, BOTH, swap_head)
    input_ring = net.ring_s(inputs)
    marks = qkv_rows[:, own : own + 4, :rows].astype(F32)
    gain_rows = marks[:, 3, : 2 * own].reshape(ns, 2, own).transpose(1, 0, 2).reshape(2, ns * own)
    merged = jnp.concatenate(
        [
            qkv_rows[:, :own].reshape(ns * own, 3 * cols),
            out_rows.reshape(own, ns, piece).transpose(1, 0, 2).reshape(ns * own, piece),
        ],
        axis=1,
    )
    merged = jnp.concatenate(
        [
            merged,
            jnp.pad(gain_rows.astype(BF), ((0, EXTRA - 2), (0, 3 * cols + piece - ns * own))),
        ],
        axis=0,
    )
    blocks = net.ring_f(merged)
    w_ffn = lax.all_gather(
        after(ffn_rows, blocks[2]).reshape(nf * own, 2 * fcols), "seq", axis=0, tiled=True
    )

    input_all = jnp.concatenate(input_ring, axis=0)
    squares = jnp.mean(jnp.square(input_all.astype(F32)), axis=-1, keepdims=True)
    inverse_all = lax.rsqrt(squares + EPSILON)
    input_float = inputs.astype(F32)
    inverse_one = inverse_all[:rows]
    unit_one = input_float * inverse_one
    order = [net.s_back(k) for k in range(ns)]
    marks = jnp.stack([lax.dynamic_index_in_dim(marks, s, 0, keepdims=False) for s in order])
    places = (marks[:, 0] * 256.0 + marks[:, 1]).reshape(group)
    ids = marks[:, 2].reshape(group)
    index = jnp.concatenate([(s * rows + jnp.arange(rows)).astype(F32) for s in order])
    frequency = 10000.0 ** (-(jnp.arange(HEAD_DIM // 2, dtype=F32) * 2.0) / HEAD_DIM)
    angles = places[:, None] * frequency[None, :]
    cosine, sine = jnp.cos(angles), jnp.sin(angles)
    tables = (
        jnp.concatenate([cosine, cosine], axis=1),
        jnp.concatenate([-sine, sine], axis=1),
    )
    row_marks = jnp.stack([index, ids])
    pair_marks = (row_marks.T, row_marks)

    *saved, attended, normed_all, gains = attend(
        dims, origin, input_all, inverse_all, tables, pair_marks, blocks
    )
    gain_one, gain_two = gains[0:1], gains[1:2]
    cots = net.ring_f(after(cotangent, blocks[-2]))
    att_terms = net.scatter_s(
        attended.reshape(ns, rows, width),
        lambda k, value: after(value, cots[2 * k]) if k < nz else value,
    )

    residual, inverse_two, unit_low = norm_two(ns, nf, own, inputs, *att_terms, gain_two)
    unit_two = residual * inverse_two
    units = net.ring_f(unit_low)
    shared, two_parts, out_parts = (), [], []
    turns = nz // 2
    each = 2 * nz // turns
    for turn in range(turns):
        here = slice(each * turn, each * (turn + 1))
        shared, done = split(
            ffn(turn, turns, units[here], cots[here], w_ffn, down_all, shared), 4
        )
        two_parts += done[:each]
        out_parts += done[each:]
    inner, d_ffn, unit_all, cot_all = shared
    sums = {}

    def two_gate(k, value, sent):
        if k == 2:
            sums["ffn"] = tn(after(unit_all, sent[0]), d_ffn).astype(BF)
            return after(value, sums["ffn"])
        if k == 3:
            sums["down"] = tn(after(inner, sent[1]), cot_all).astype(BF)
            return after(value, sums["down"])
        return value

    two_terms, two_sent = net.scatter_f(lambda k, sent: two_parts[2 * k : 2 * k + 2], two_gate)
    d_residual, d_low = norm_two_back(
        ns, nf, own, two_terms, residual, inverse_two, gain_two, cotangent
    )
    d_attended = net.ring_s(d_low)
    ffn_sum = lax.psum_scatter(
        sums["ffn"].reshape(ns, nf * own, 2 * fcols), "seq", scatter_dimension=0, tiled=False
    )
    grad_down = lax.psum_scatter(
        after(sums["down"], ffn_sum), "seq", scatter_dimension=0, tiled=True
    ).astype(F32)
    out_terms, out_sent = net.scatter_f(
        lambda k, sent: out_parts[2 * k : 2 * k + 2],
        lambda k, value, sent: after(value, d_attended[k]) if k < ns else value,
    )
    layer_out = (residual + total_of(out_terms)).astype(BF)
    ffn_own = lax.all_to_all(
        ffn_sum.reshape(nf, own, 2 * fcols), "fsdp", split_axis=0, concat_axis=0, tiled=True
    )
    grad_gate, grad_up, grad_ffn_gain = unpack_ffn(
        w_gate,
        w_up,
        ffn_gain.astype(F32)[:, None],
        ffn_own,
    )

    d_qkv, out_grad = attend_back(
        dims, origin, jnp.concatenate(d_attended, axis=0), saved, tables, pair_marks, blocks
    )
    held = {}

    def weight_part(k, sent):
        if k == 1:
            ready = after(d_qkv, out_terms[2])
        else:
            ready = after(d_qkv, sent[min(len(sent), 2) - 1])
        return weight_grad(dims, k, origin, normed_all, ready, out_grad)

    def weight_gate(k, value, sent):
        if k == 2:
            dn_parts = input_grad(dims, origin, after(d_qkv, sent[0]), blocks, width)
            held["one"] = total_of(net.scatter_s(dn_parts.reshape(ns, rows, width)))
            return value
        return after(value, held["one"], ffn_own) if k == nz - 1 else value

    terms, _ = net.scatter_f(weight_part, weight_gate)
    one_sum = held["one"]
    scaled_one = one_sum * gain_one
    grad_input = d_residual + inverse_one * (
        scaled_one - unit_one * jnp.mean(scaled_one * unit_one, axis=-1, keepdims=True)
    )
    term = total_of(terms).astype(BF)
    qkv_own = net.swap_s(term[:, : 3 * cols].reshape(ns, own, 3 * cols))
    grad_query, grad_key, grad_value, grad_attn_gain = unpack_heads(
        qkv_own, attn_gain.astype(F32)[:, None], (w_query, w_key, w_value), ns, nf, per_head
    )
    out_mine = term[:, 3 * cols :].reshape(ns, own, piece).transpose(1, 0, 2).reshape(own, width)
    back_head = [(b, a) for a, b in swap_head]
    grad_out = lax.ppermute(out_mine, BOTH, back_head).astype(F32)
    return (
        layer_out,
        grad_input,
        grad_attn_gain,
        grad_query,
        grad_key,
        grad_value,
        grad_out,
        grad_ffn_gain,
        grad_gate,
        grad_up,
        grad_down,
    )


def solution(mesh):
    row = P(("fsdp", "seq"), None)
    flat = P(("fsdp", "seq"))
    return jax.shard_map(
        shards,
        mesh=mesh,
        in_specs=(row, flat, flat, flat, row, row, row, row, flat, row, row, row, row),
        out_specs=(row, row, flat, row, row, row, row, flat, row, row, row),
        check_vma=False,
    )
```

time: 854 us -> 620 us (0.73)
  Pallas kernels: 0 us -> 128 us
  local copies, waits for them, and re-layouts: 135 us -> 40.3 us
  waiting for transfers between devices: 379 us -> 294 us
  matrix products: 101 us -> 22.7 us
  starting transfers between devices: 148 us -> 73.9 us
  between operations: 31.5 us -> 14.9 us
  other arithmetic: 48.8 us -> 35.9 us
    pallas_call x0 -> x15, Pallas kernels: none -> 128 us  [the longest x2 44.2 us: ffn(): pl.pallas_call(functools.partial(ffn_kernel, count, not before), grid=(fc...]
    dot_general x16 -> x0, matrix products: 78.4 us -> none  [the longest x5 38.6 us: nt(): lax.dot_general(left, right, (((1,), (1,)), ((), ())), preferred_element_...]
    ppermute x18 -> x6, waiting for transfers between devices: 93 us -> 33.4 us  [swap_s(): got = lax.ppermute(piece, 'seq', perm)]
    ppermute x33 -> x12, waiting for transfers between devices: 116 us -> 65.9 us  [step_s(): return lax.ppermute(value, BOTH, self.s_perm)]
    ppermute x33 -> x12, starting transfers between devices: 39 us -> 6.58 us  [step_s(): return lax.ppermute(value, BOTH, self.s_perm)]
    dynamic_update_slice x68 -> x4, local copies, waits for them, and re-layouts: 32.6 us -> 2.38 us  [swap_s(): out = lax.dynamic_update_slice_in_dim(out, got, self.s ^ k, 0)]
    dot_general x5 -> x0, local copies, waits for them, and re-layouts: 29.8 us -> none  [the longest x3 19.4 us: nn(): lax.dot_general(left, right, (((1,), (0,)), ((), ())), preferred_element_...]
    ppermute x24 -> x18, starting transfers between devices: 71.1 us -> 43.8 us  [step_z(): return lax.ppermute(value, 'fsdp', self.z_perm)]
  transfers between devices with their start and end apart: 101 -> 68, of which waited for: 48 -> 30; matrix products, arithmetic and copies ran while one was open for 27% -> 11% of each run, Pallas kernels for 0% -> 21%
where the time goes in v2:
time: 620 us; the launch traced here: 611 us
  waiting for transfers between devices  294 us (47%)
  Pallas kernels  128 us (21%)
  starting transfers between devices  73.9 us (12%)
  local copies, waits for them, and re-layouts  40.3 us (6%)
  other arithmetic  35.9 us (6%)
  matrix products  22.7 us (4%)
  between operations  14.9 us (2%)
    ppermute x18, waiting for transfers between devices, step_z(): return lax.ppermute(value, 'fsdp', self.z_perm)  184 us
    ppermute x12, waiting for transfers between devices, step_s(): return lax.ppermute(value, BOTH, self.s_perm)  65.9 us
    pallas_call x2, Pallas kernels, ffn(): pl.pallas_call(functools.partial(ffn_kernel, count, not before), grid=(fc...  44.2 us
    ppermute x18, starting transfers between devices, step_z(): return lax.ppermute(value, 'fsdp', self.z_perm)  43.8 us
    ppermute x6, waiting for transfers between devices, swap_s(): got = lax.ppermute(piece, 'seq', perm)  33.4 us
    dot_general x2, matrix products, tn(): lax.dot_general(left, right, (((0,), (0,)), ((), ())), preferred_element_...  22.7 us
    pallas_call x4, Pallas kernels, weight_grad(): pl.pallas_call(functools.partial(weight_grad_kernel, dims, step), in_spec...  20.6 us
    unnamed x109, local copies, waits for them, and re-layouts  19.9 us
  transfers between devices with their start and end apart: 68, of which 30 were waited for; matrix products, arithmetic and copies ran while one was open for 11% of the time, Pallas kernels for 21%

profile of v2, /device:TPU:0, one launch (start us, length us, event | category | flops | bytes accessed | tf_op | source)
XLA Modules:
  0.0 610.6 jit_solution(2731888761649837826)
XLA Ops:
  24.5 11.8 %collective-permute-done.3 = bf16[1,80,1536]{2,1,0:T(8,128)(2,1)S(1)} collective-permute-done((bf16[1,80,1536]{2,1,0:T(8,128)(2,1)S(1)}, bf16[1,80,1536]{2,1,0:T(8,128)(2,1)S(1)}, u32[]{:S(2)}, u32[]{:S(2)}) %collective-permute-start.3) | collective-permute-done | bytes 245792 | tf_op jit(solution)/shard_map/ppermute | solution.py:122
  41.1 13.1 %collective-permute-done.4 = bf16[1,80,1536]{2,1,0:T(8,128)(2,1)S(1)} collective-permute-done((bf16[1,80,1536]{2,1,0:T(8,128)(2,1)S(1)}, bf16[1,80,1536]{2,1,0:T(8,128)(2,1)S(1)}, u32[]{:S(2)}, u32[]{:S(2)}) %collective-permute-start.4) | collective-permute-done | bytes 245792 | tf_op jit(solution)/shard_map/ppermute | solution.py:122
  62.7 21.0 %collective-permute-done.8.refs_2_ = bf16[272,2048]{1,0:T(8,128)(2,1)} collective-permute-done((bf16[272,2048]{1,0:T(8,128)(2,1)S(1)}, bf16[272,2048]{1,0:T(8,128)(2,1)}, u32[]{:S(2)}, u32[]{:S(2)}) %collective-permute-start.8) | collective-permute-done | bytes 1114144 | tf_op jit(solution)/shard_map/ppermute | solution.py:92
  96.6 22.3 %collective-permute-done.10.refs_4_ = bf16[272,2048]{1,0:T(8,128)(2,1)S(1)} collective-permute-done((bf16[272,2048]{1,0:T(8,128)(2,1)}, bf16[272,2048]{1,0:T(8,128)(2,1)S(1)}, u32[]{:S(2)}, u32[]{:S(2)}) %collective-permute-start.10) | collective-permute-done | bytes 1114144 | tf_op jit(solution)/shard_map/ppermute | solution.py:92
  133.9 10.3 %collective-permute-done.12.refs_6_ = bf16[272,2048]{1,0:T(8,128)(2,1)S(1)} collective-permute-done((bf16[272,2048]{1,0:T(8,128)(2,1)S(1)}, bf16[272,2048]{1,0:T(8,128)(2,1)S(1)}, u32[]{:S(2)}, u32[]{:S(2)}) %collective-permute-start.12) | collective-permute-done | bytes 1114144 | tf_op jit(solution)/shard_map/ppermute | solution.py:92
  159.7 16.5 %shard_map.214 = (bf16[512,512]{1,0:T(8,128)(2,1)}, bf16[512,512]{1,0:T(8,128)(2,1)}, bf16[512,512]{1,0:T(8,128)(2,1)}, bf16[512,512]{1,0:T(8,128)(2,1)}, bf16[5...) custom-call(s32[8]{0:T(128)} %stack.63.origin_ref, ...), custom_call_target="tpu_custom_call" | custom-call | flops 4831838208 | bytes 8388608 | tf_op jit(solution)/shard_map/pallas_call | solution.py:353
  180.1 11.8 %collective-permute-done.15 = bf16[128,2048]{1,0:T(8,128)(2,1)S(1)} collective-permute-done((bf16[128,2048]{1,0:T(8,128)(2,1)S(1)}, bf16[128,2048]{1,0:T(8,128)(2,1)S(1)}, u32[]{:S(2)}, u32[]{:S(2)}) %collective-permute-start.15) | collective-permute-done | bytes 524320 | tf_op jit(solution)/shard_map/ppermute | solution.py:89
  221.9 9.3 %collective-permute-done.21.refs_2_ = bf16[128,2048]{1,0:T(8,128)(2,1)S(1)} collective-permute-done((bf16[128,2048]{1,0:T(8,128)(2,1)}, bf16[128,2048]{1,0:T(8,128)(2,1)S(1)}, u32[]{:S(2)}, u32[]{:S(2)}) %collective-permute-start.21) | collective-permute-done | bytes 524320 | tf_op jit(solution)/shard_map/ppermute | solution.py:92
  235.1 7.7 %collective-permute-done.26.refs_0_ = bf16[128,2048]{1,0:T(8,128)(2,1)S(1)} collective-permute-done((bf16[128,2048]{1,0:T(8,128)(2,1)S(1)}, bf16[128,2048]{1,0:T(8,128)(2,1)S(1)}, u32[]{:S(2)}, u32[]{:S(2)}) %collective-permute-start.26) | collective-permute-done | bytes 524320 | tf_op jit(solution)/shard_map/ppermute | solution.py:92
  256.8 22.0 %shard_map.216 = (bf16[1024,1024]{1,0:T(8,128)(2,1)}, bf16[1024,2048]{1,0:T(8,128)(2,1)}, bf16[1024,2048]{1,0:T(8,128)(2,1)}, bf16[1024,2048]{1,0:T(8,128)(2,1)}...) custom-call(bf16[128,2048]{1,0:T(8,128)(2,1)S(1)} %copy-done.14, ...), custom_call_target="tpu_custom_call" | custom-call | flops 12884901888 | bytes 20971520 | tf_op jit(solution)/shard_map/pallas_call | solution.py:531
  284.8 22.2 %shard_map.217 = (bf16[1024,1024]{1,0:T(8,128)(2,1)}, bf16[1024,2048]{1,0:T(8,128)(2,1)}, bf16[1024,2048]{1,0:T(8,128)(2,1)}, bf16[1024,2048]{1,0:T(8,128)(2,1)}...) custom-call(bf16[128,2048]{1,0:T(8,128)(2,1)S(1)} %copy-done.11, ...), custom_call_target="tpu_custom_call", output_to_operand_aliasing={{0}: (10, {}), {1}: (11, {}), {2}: (12, {}), {3}: (13, {})} | custom-call | flops 12884901888 | bytes 20971520 | tf_op jit(solution)/shard_map/pallas_call | solution.py:531
  308.2 14.1 %convolution_convert_fusion = bf16[2048,2048]{1,0:T(8,128)(2,1)} fusion(bf16[1024,2048]{1,0:T(8,128)(2,1)} %get-tuple-element.112, bf16[1024,2048]{1,0:T(8,128)(2,1)} %get-tuple-element.113), kind=kOutput, calls=%fused_computation | convolution fusion | flops 8594128896 | bytes 16777216 | tf_op jit(solution)/shard_map/dot_general | solution.py:35
  326.8 11.4 %collective-permute-done.39 = bf16[128,2048]{1,0:T(8,128)(2,1)S(1)} collective-permute-done((bf16[128,2048]{1,0:T(8,128)(2,1)}, bf16[128,2048]{1,0:T(8,128)(2,1)S(1)}, u32[]{:S(2)}, u32[]{:S(2)}) %collective-permute-start.39) | collective-permute-done | bytes 524320 | tf_op jit(solution)/shard_map/ppermute | solution.py:92
  342.5 8.6 %convolution_convert_fusion.1 = bf16[1024,2048]{1,0:T(8,128)(2,1)} fusion(bf16[1024,1024]{1,0:T(8,128)(2,1)S(1)} %copy-done.52, bf16[1024,2048]{1,0:T(8,128)(2,1)} %get-tuple-element.117), kind=kOutput, calls=%fused_computation.2 | convolution fusion | flops 4297064448 | bytes 10485760 | tf_op jit(solution)/shard_map/dot_general | solution.py:35
  358.7 9.8 %collective-permute-done.41.refs_2_ = bf16[128,2048]{1,0:T(8,128)(2,1)S(1)} collective-permute-done((bf16[128,2048]{1,0:T(8,128)(2,1)S(1)}, bf16[128,2048]{1,0:T(8,128)(2,1)S(1)}, u32[]{:S(2)}, u32[]{:S(2)}) %collective-permute-start.41) | collective-permute-done | bytes 524320 | tf_op jit(solution)/shard_map/ppermute | solution.py:92
  373.6 8.9 %collective-permute-done.42 = bf16[128,2048]{1,0:T(8,128)(2,1)S(1)} collective-permute-done((bf16[128,2048]{1,0:T(8,128)(2,1)}, bf16[128,2048]{1,0:T(8,128)(2,1)S(1)}, u32[]{:S(2)}, u32[]{:S(2)}) %collective-permute-start.42) | collective-permute-done | bytes 524320 | tf_op jit(solution)/shard_map/ppermute | solution.py:89
  386.2 9.3 %collective-permute-done.43 = bf16[128,2048]{1,0:T(8,128)(2,1)S(1)} collective-permute-done((bf16[128,2048]{1,0:T(8,128)(2,1)S(1)}, bf16[128,2048]{1,0:T(8,128)(2,1)S(1)}, u32[]{:S(2)}, u32[]{:S(2)}) %collective-permute-start.43) | collective-permute-done | bytes 524320 | tf_op jit(solution)/shard_map/ppermute | solution.py:92
  395.7 10.7 %collective-permute-done.44 = bf16[128,2048]{1,0:T(8,128)(2,1)} collective-permute-done((bf16[128,2048]{1,0:T(8,128)(2,1)S(1)}, bf16[128,2048]{1,0:T(8,128)(2,1)}, u32[]{:S(2)}, u32[]{:S(2)}) %collective-permute-start.44) | collective-permute-done | bytes 524320 | tf_op jit(solution)/shard_map/ppermute | solution.py:89
  406.7 9.7 %collective-permute-done.45 = bf16[128,2048]{1,0:T(8,128)(2,1)S(1)} collective-permute-done((bf16[128,2048]{1,0:T(8,128)(2,1)S(1)}, bf16[128,2048]{1,0:T(8,128)(2,1)S(1)}, u32[]{:S(2)}, u32[]{:S(2)}) %collective-permute-start.45) | collective-permute-done | bytes 524320 | tf_op jit(solution)/shard_map/ppermute | solution.py:92
  425.9 14.8 %shard_map.219 = (bf16[512,1536]{1,0:T(8,128)(2,1)}, bf16[4,512,512]{2,1,0:T(8,128)(2,1)}) custom-call(s32[8]{0:T(128)} %stack.63.origin_ref, bf16[512,2048]{1,0:T(8,128)(2,1)} %pad_maximum_fusion.datt_ref, bf16[512,512]{1,0:T(8,128)(2,1)} %get-tuple-element.125.q_ref, bf16[512,512]{1,0:T(8,128)(2,1)} %get-tuple-element.126.k_ref, ...), custom_call_target="tpu_custom_call" | custom-call | flops 3489660928 | bytes 4194304 | tf_op jit(solution)/shard_map/pallas_call | solution.py:413
  459.3 9.7 %shard_map.221 = bf16[512,2048]{1,0:T(8,128)(2,1)} custom-call(s32[8]{0:T(128)} %stack.63.origin_ref, bf16[512,1536]{1,0:T(8,128)(2,1)} %get-tuple-element.138.d_ref, bf16[272,2048]{1,0:T(8,128)(2,1)} %copy-done.22, bf16[272,2048]{1,0:T(8,128)(2,1)} %collective-permute-done.7.refs_1_, bf16[272,2048]{1,0:T(8,128)(2,1)} %collective-permute-done.8.refs_2_, ...), custom_call_target="tpu_custom_call" | custom-call | flops 3221225472 | bytes 8388608 | tf_op jit(solution)/shard_map/pallas_call | solution.py:466
  471.4 36.6 %collective-permute-done.53 = bf16[256,2048]{1,0:T(8,128)(2,1)S(1)} collective-permute-done((bf16[256,2048]{1,0:T(8,128)(2,1)S(1)}, bf16[256,2048]{1,0:T(8,128)(2,1)S(1)}, u32[]{:S(2)}, u32[]{:S(2)}) %collective-permute-start.53) | collective-permute-done | bytes 1048608 | tf_op jit(solution)/shard_map/ppermute | solution.py:92
  527.9 11.0 %collective-permute-done.56 = bf16[256,2048]{1,0:T(8,128)(2,1)} collective-permute-done((bf16[256,2048]{1,0:T(8,128)(2,1)}, bf16[256,2048]{1,0:T(8,128)(2,1)}, u32[]{:S(2)}, u32[]{:S(2)}) %collective-permute-start.56) | collective-permute-done | bytes 1048608 | tf_op jit(solution)/shard_map/ppermute | solution.py:92
  555.6 14.0 %collective-permute-done.57 = bf16[256,2048]{1,0:T(8,128)(2,1)S(1)} collective-permute-done((bf16[256,2048]{1,0:T(8,128)(2,1)}, bf16[256,2048]{1,0:T(8,128)(2,1)S(1)}, u32[]{:S(2)}, u32[]{:S(2)}) %collective-permute-start.57) | collective-permute-done | bytes 1048608 | tf_op jit(solution)/shard_map/ppermute | solution.py:92
  (311 shorter events, 259.2 us)
Async XLA Ops:
  7.2 246.7 %all-gather.5.cloned.1.call-start = ((), (), s32[]{:S(2)}) async-start(), calls=%async_computation.5 | async-start | bytes 5242880 | tf_op jit(solution)/shard_map/all_gather | solution.py:656
  11.7 79.4 %all-to-all-start = ((bf16[8,64,2048]{2,1,0:T(8,128)(2,1)}), bf16[8,64,2048]{2,1,0:T(8,128)(2,1)S(1)}, u32[]{:S(2)}, u32[]{:S(2)}) async-start(bf16[8,64,2048]{2,1,0:T(8,128)(2,1)} %shard_map.212), calls=%async_computation | async-start | bytes 4194304 | tf_op jit(solution)/shard_map/all_to_all | solution.py:658
  18.2 236.6 %all-gather.3.cloned.1.call-start = ((), (), s32[]{:S(2)}) async-start(), calls=%async_computation.4 | async-start | bytes 10485760 | tf_op jit(solution)/shard_map/all_gather | solution.py:680
  92.5 353.7 %reduce-scatter.7.cloned.1.call-start = ((), (), s32[]{:S(2)}) async-start(), calls=%async_computation.7 | async-start | bytes 10485760
  92.5 26.4 %collective-permute-start.10 = (bf16[272,2048]{1,0:T(8,128)(2,1)}, bf16[272,2048]{1,0:T(8,128)(2,1)S(1)}, u32[]{:S(2)}, u32[]{:S(2)}) collective-permute-start(bf16[272,2048]{1,0:T(8,128)(2,1)} %collective-permute-done.8.refs_2_), channel_id=1, source_target_pairs={{0,4},{1,5},{2,0},{3,1},{4,6},{5,7},{6,2},{7,3},{8,12},{9,13},{10,... | collective-permute-start | bytes 3342344 | tf_op jit(solution)/shard_map/ppermute | solution.py:92
  92.6 28.2 %collective-permute-start = (bf16[128,2048]{1,0:T(8,128)(2,1)}, bf16[128,2048]{1,0:T(8,128)(2,1)}, u32[]{:S(2)}, u32[]{:S(2)}) collective-permute-start(bf16[128,2048]{1,0:T(8,128)(2,1)} %input_ref.1), channel_id=1, source_target_pairs={{0,8},{8,24},{16,0},{24,16},{1,17},{9,1},{17,25},{25,9},{2,10},{10... | collective-permute-start | bytes 1572872 | tf_op jit(solution)/shard_map/ppermute | solution.py:89
  118.9 25.3 %collective-permute-start.12 = (bf16[272,2048]{1,0:T(8,128)(2,1)S(1)}, bf16[272,2048]{1,0:T(8,128)(2,1)S(1)}, u32[]{:S(2)}, u32[]{:S(2)}) collective-permute-start(bf16[272,2048]{1,0:T(8,128)(2,1)S(1)} %collective-permute-done.10.refs_4_), channel_id=1, source_target_pairs={{0,4},{1,5},{2,0},{3,1},{4,6},{5,7},{6,2},{7,3},{8,12},{9,13},{10,... | collective-permute-start | bytes 3342344 | tf_op jit(solution)/shard_map/ppermute | solution.py:92
  120.1 39.6 %collective-permute-start.7 = (bf16[272,2048]{1,0:T(8,128)(2,1)S(1)}, bf16[272,2048]{1,0:T(8,128)(2,1)}, u32[]{:S(2)}, u32[]{:S(2)}) collective-permute-start(bf16[272,2048]{1,0:T(8,128)(2,1)S(1)} %fusion.1.refs_0_), channel_id=1, source_target_pairs={{0,1},{1,0},{2,3},{3,2},{4,5},{5,4},{6,7},{7,6},{8,9},{9,8},{10,11... | collective-permute-start | bytes 3342344 | tf_op jit(solution)/shard_map/ppermute | solution.py:95
  133.4 26.3 %collective-permute-start.9 = (bf16[272,2048]{1,0:T(8,128)(2,1)}, bf16[272,2048]{1,0:T(8,128)(2,1)}, u32[]{:S(2)}, u32[]{:S(2)}) collective-permute-start(bf16[272,2048]{1,0:T(8,128)(2,1)} %collective-permute-done.8.refs_2_), channel_id=1, source_target_pairs={{0,1},{1,0},{2,3},{3,2},{4,5},{5,4},{6,7},{7,6},{8,9},{9,8},{10,11... | collective-permute-start | bytes 3342344 | tf_op jit(solution)/shard_map/ppermute | solution.py:95
  133.5 26.1 %collective-permute-start.11 = (bf16[272,2048]{1,0:T(8,128)(2,1)S(1)}, bf16[272,2048]{1,0:T(8,128)(2,1)}, u32[]{:S(2)}, u32[]{:S(2)}) collective-permute-start(bf16[272,2048]{1,0:T(8,128)(2,1)S(1)} %collective-permute-done.10.refs_4_), channel_id=1, source_target_pairs={{0,1},{1,0},{2,3},{3,2},{4,5},{5,4},{6,7},{7,6},{8,9},{9,8},{10,11... | collective-permute-start | bytes 3342344 | tf_op jit(solution)/shard_map/ppermute | solution.py:95
  246.6 34.3 %collective-permute-start.30 = (bf16[128,2048]{1,0:T(8,128)(2,1)}, bf16[128,2048]{1,0:T(8,128)(2,1)}, u32[]{:S(2)}, u32[]{:S(2)}) collective-permute-start(bf16[128,2048]{1,0:T(8,128)(2,1)} %collective-permute-done.16.refs_4_), channel_id=1, source_target_pairs={{0,1},{1,0},{2,3},{3,2},{4,5},{5,4},{6,7},{7,6},{8,9},{9,8},{10,11... | collective-permute-start | bytes 1572872 | tf_op jit(solution)/shard_map/ppermute | solution.py:95
  247.1 33.8 %collective-permute-start.31 = (bf16[128,2048]{1,0:T(8,128)(2,1)}, bf16[128,2048]{1,0:T(8,128)(2,1)}, u32[]{:S(2)}, u32[]{:S(2)}) collective-permute-start(bf16[128,2048]{1,0:T(8,128)(2,1)} %collective-permute-done.18.refs_6_), channel_id=1, source_target_pairs={{0,1},{1,0},{2,3},{3,2},{4,5},{5,4},{6,7},{7,6},{8,9},{9,8},{10,11... | collective-permute-start | bytes 1572872 | tf_op jit(solution)/shard_map/ppermute | solution.py:95
  248.7 32.2 %collective-permute-start.27 = (bf16[128,2048]{1,0:T(8,128)(2,1)S(1)}, bf16[128,2048]{1,0:T(8,128)(2,1)S(1)}, u32[]{:S(2)}, u32[]{:S(2)}) collective-permute-start(bf16[128,2048]{1,0:T(8,128)(2,1)S(1)} %collective-permute-done.26.refs_0_), channel_id=1, source_target_pairs={{0,1},{1,0},{2,3},{3,2},{4,5},{5,4},{6,7},{7,6},{8,9},{9,8},{10,11... | collective-permute-start | bytes 1572872 | tf_op jit(solution)/shard_map/ppermute | solution.py:95
  253.8 27.9 %collective-permute-start.29 = (bf16[128,2048]{1,0:T(8,128)(2,1)S(1)}, bf16[128,2048]{1,0:T(8,128)(2,1)}, u32[]{:S(2)}, u32[]{:S(2)}) collective-permute-start(bf16[128,2048]{1,0:T(8,128)(2,1)S(1)} %collective-permute-done.28.refs_2_), channel_id=1, source_target_pairs={{0,1},{1,0},{2,3},{3,2},{4,5},{5,4},{6,7},{7,6},{8,9},{9,8},{10,11... | collective-permute-start | bytes 1572872 | tf_op jit(solution)/shard_map/ppermute | solution.py:95
  280.5 26.6 %collective-permute-start.38 = (bf16[128,2048]{1,0:T(8,128)(2,1)S(1)}, bf16[128,2048]{1,0:T(8,128)(2,1)S(1)}, u32[]{:S(2)}, u32[]{:S(2)}) collective-permute-start(bf16[128,2048]{1,0:T(8,128)(2,1)S(1)} %get-tuple-element.110), channel_id=1, source_target_pairs={{0,1},{1,0},{2,3},{3,2},{4,5},{5,4},{6,7},{7,6},{8,9},{9,8},{10,11... | collective-permute-start | bytes 1572872 | tf_op jit(solution)/shard_map/ppermute | solution.py:95
  322.4 258.3 %reduce-scatter.5.cloned.1.call-start = ((), (), s32[]{:S(2)}) async-start(), calls=%async_computation.6 | async-start | bytes 5242880 | tf_op jit(solution)/shard_map/reduce_scatter | solution.py:748
  326.3 32.4 %collective-permute-start.35 = (bf16[128,2048]{1,0:T(8,128)(2,1)}, bf16[128,2048]{1,0:T(8,128)(2,1)}, u32[]{:S(2)}, u32[]{:S(2)}) collective-permute-start(bf16[128,2048]{1,0:T(8,128)(2,1)} %copy-done.9), channel_id=1, source_target_pairs={{0,1},{1,0},{2,3},{3,2},{4,5},{5,4},{6,7},{7,6},{8,9},{9,8},{10,11... | collective-permute-start | bytes 1572872 | tf_op jit(solution)/shard_map/ppermute | solution.py:95
  446.2 98.5 %all-to-all-start.1 = ((bf16[8,64,2048]{2,1,0:T(8,128)(2,1)}), bf16[8,64,2048]{2,1,0:T(8,128)(2,1)}, u32[]{:S(2)}, u32[]{:S(2)}) async-start(bf16[8,64,2048]{2,1,0:T(8,128)(2,1)} %bitcast.58), calls=%async_computation.1 | async-start | bytes 4194304 | tf_op jit(solution)/shard_map/all_to_all | solution.py:756
  451.1 56.8 %collective-permute-start.53 = (bf16[256,2048]{1,0:T(8,128)(2,1)S(1)}, bf16[256,2048]{1,0:T(8,128)(2,1)S(1)}, u32[]{:S(2)}, u32[]{:S(2)}) collective-permute-start(bf16[256,2048]{1,0:T(8,128)(2,1)S(1)} %add_convert_fusion.3), channel_id=1, source_target_pairs={{0,4},{1,5},{2,0},{3,1},{4,6},{5,7},{6,2},{7,3},{8,12},{9,13},{10,... | collective-permute-start | bytes 3145736 | tf_op jit(solution)/shard_map/ppermute | solution.py:92
  459.3 48.6 %collective-permute-start.52 = (bf16[256,2048]{1,0:T(8,128)(2,1)}, bf16[256,2048]{1,0:T(8,128)(2,1)S(1)}, u32[]{:S(2)}, u32[]{:S(2)}) collective-permute-start(bf16[256,2048]{1,0:T(8,128)(2,1)} %get-tuple-element.137), channel_id=1, source_target_pairs={{0,1},{1,0},{2,3},{3,2},{4,5},{5,4},{6,7},{7,6},{8,9},{9,8},{10,11... | collective-permute-start | bytes 3145736 | tf_op jit(solution)/shard_map/ppermute | solution.py:95
  470.9 49.0 %collective-permute-start.49 = (bf16[128,2048]{1,0:T(8,128)(2,1)}, bf16[128,2048]{1,0:T(8,128)(2,1)}, u32[]{:S(2)}, u32[]{:S(2)}) collective-permute-start(bf16[128,2048]{1,0:T(8,128)(2,1)} %slice.93), channel_id=1, source_target_pairs={{0,8},{8,24},{16,0},{24,16},{1,17},{9,1},{17,25},{25,9},{2,10},{10... | collective-permute-start | bytes 1572872 | tf_op jit(solution)/shard_map/ppermute | solution.py:89
  509.5 29.3 %collective-permute-start.56 = (bf16[256,2048]{1,0:T(8,128)(2,1)}, bf16[256,2048]{1,0:T(8,128)(2,1)}, u32[]{:S(2)}, u32[]{:S(2)}) collective-permute-start(bf16[256,2048]{1,0:T(8,128)(2,1)} %add_convert_fusion.2), channel_id=1, source_target_pairs={{0,4},{1,5},{2,0},{3,1},{4,6},{5,7},{6,2},{7,3},{8,12},{9,13},{10,... | collective-permute-start | bytes 3145736 | tf_op jit(solution)/shard_map/ppermute | solution.py:92
  519.4 27.1 %collective-permute-start.25 = (bf16[128,2048]{1,0:T(8,128)(2,1)S(1)}, bf16[128,2048]{1,0:T(8,128)(2,1)}, u32[]{:S(2)}, u32[]{:S(2)}) collective-permute-start(bf16[128,2048]{1,0:T(8,128)(2,1)S(1)} %copy-done.2), channel_id=1, source_target_pairs={{0,1},{1,0},{2,3},{3,2},{4,5},{5,4},{6,7},{7,6},{8,9},{9,8},{10,11... | collective-permute-start | bytes 1572872 | tf_op jit(solution)/shard_map/ppermute | solution.py:95
  527.4 28.2 %collective-permute-start.54 = (bf16[256,2048]{1,0:T(8,128)(2,1)}, bf16[256,2048]{1,0:T(8,128)(2,1)}, u32[]{:S(2)}, u32[]{:S(2)}) collective-permute-start(bf16[256,2048]{1,0:T(8,128)(2,1)} %get-tuple-element.140), channel_id=1, source_target_pairs={{0,1},{1,0},{2,3},{3,2},{4,5},{5,4},{6,7},{7,6},{8,9},{9,8},{10,11... | collective-permute-start | bytes 3145736 | tf_op jit(solution)/shard_map/ppermute | solution.py:95
  (97 other events, 1360.9 us)
Sparse Core Ops, SparseCore 0:
  9.9 63.7 all-gather.4
  92.6 96.3 all-gather.2
  322.5 97.9 reduce-scatter.6
  423.6 52.1 reduce-scatter.4

commit v3 on v2

--- a/solution.py
+++ b/solution.py
@@ -100,11 +100,11 @@
             blocks.append(self.step_s(blocks[-1]))
         return blocks
 
-    def ring_f(self, value):
+    def ring_f(self, value, gate=lambda k, value: value):
         held, blocks = value, []
         for k in range(self.nz):
             if k:
-                held = self.step_z(held)
+                held = self.step_z(gate(k, held))
             blocks += [held, self.swap_c(held)]
         return blocks
 
@@ -714,44 +714,79 @@
 
     residual, inverse_two, unit_low = norm_two(ns, nf, own, inputs, *att_terms, gain_two)
     unit_two = residual * inverse_two
-    units = net.ring_f(unit_low)
+    turns = 2 if nz % 2 == 0 else 1
+    each = 2 * nz // turns
     shared, two_parts, out_parts = (), [], []
-    turns = nz // 2
-    each = 2 * nz // turns
-    for turn in range(turns):
+    units = []
+
+    def run_turn(turn, ready):
+        nonlocal shared
         here = slice(each * turn, each * (turn + 1))
         shared, done = split(
-            ffn(turn, turns, units[here], cots[here], w_ffn, down_all, shared), 4
+            ffn(turn, turns, units_at(here, ready), cots[here], w_ffn, down_all, shared), 4
         )
-        two_parts += done[:each]
-        out_parts += done[each:]
-    inner, d_ffn, unit_all, cot_all = shared
+        two_parts.extend(done[:each])
+        out_parts.extend(done[each:])
+
+    def units_at(here, ready):
+        return units[here] if ready is None else after(units[here], ready)
+
+    held_unit = unit_low
+    for k in range(nz):
+        if k:
+            held_unit = net.step_z(
+                after(held_unit, two_parts[0]) if k == each // 2 + 1 else held_unit
+            )
+        units += [held_unit, net.swap_c(held_unit)]
+        if 2 * k + 2 == each:
+            run_turn(0, None)
     sums = {}
 
+    def two_part(k, sent):
+        if 2 * k + 2 > len(two_parts):
+            run_turn(1, sent[0])
+        return two_parts[2 * k : 2 * k + 2]
+
     def two_gate(k, value, sent):
-        if k == 2:
-            sums["ffn"] = tn(after(unit_all, sent[0]), d_ffn).astype(BF)
-            return after(value, sums["ffn"])
-        if k == 3:
-            sums["down"] = tn(after(inner, sent[1]), cot_all).astype(BF)
+        if k == nz - 1:
+            inner, d_ffn, unit_all, cot_all = shared
+            sums["down"] = tn(after(inner, sent[-1]), cot_all).astype(BF)
             return after(value, sums["down"])
         return value
 
-    two_terms, two_sent = net.scatter_f(lambda k, sent: two_parts[2 * k : 2 * k + 2], two_gate)
+    two_terms, two_sent = net.scatter_f(two_part, two_gate)
+    inner, d_ffn, unit_all, cot_all = shared
+    grad_down = lax.psum_scatter(
+        sums["down"], "seq", scatter_dimension=0, tiled=True
+    ).astype(F32)
+    sums["ffn"] = tn(after(unit_all, two_sent[-1]), d_ffn).astype(BF)
+    two_terms = (after(two_terms[0], sums["ffn"]), *two_terms[1:])
     d_residual, d_low = norm_two_back(
         ns, nf, own, two_terms, residual, inverse_two, gain_two, cotangent
     )
-    d_attended = net.ring_s(d_low)
+    d_attended, out_came = [d_low], [None]
+
+    def send_out(k, ready):
+        other = net.swap_c(out_parts[2 * k + 1])
+        total = out_parts[2 * k].astype(F32) + other.astype(F32)
+        if k > 1:
+            total = total + out_came[-1].astype(F32)
+        out_came.append(net.step_z(after(total.astype(BF), ready)))
+
+    for k in range(1, ns):
+        value = d_attended[-1]
+        d_attended.append(net.step_s(after(value, out_came[1]) if k == ns - 1 else value))
+        if k == 1:
+            send_out(1, d_attended[1])
     ffn_sum = lax.psum_scatter(
-        sums["ffn"].reshape(ns, nf * own, 2 * fcols), "seq", scatter_dimension=0, tiled=False
-    )
-    grad_down = lax.psum_scatter(
-        after(sums["down"], ffn_sum), "seq", scatter_dimension=0, tiled=True
-    ).astype(F32)
-    out_terms, out_sent = net.scatter_f(
-        lambda k, sent: out_parts[2 * k : 2 * k + 2],
-        lambda k, value, sent: after(value, d_attended[k]) if k < ns else value,
-    )
+        after(sums["ffn"], d_attended[-1]).reshape(ns, nf * own, 2 * fcols),
+        "seq",
+        scatter_dimension=0,
+        tiled=False,
+    )
+    for k in range(2, nz):
+        send_out(k, d_low)
+    out_terms = (out_parts[0], net.swap_c(out_parts[1]), out_came[-1])
     layer_out = (residual + total_of(out_terms)).astype(BF)
     ffn_own = lax.all_to_all(
         ffn_sum.reshape(nf, own, 2 * fcols), "fsdp", split_axis=0, concat_axis=0, tiled=True
@@ -770,7 +805,7 @@
 
     def weight_part(k, sent):
         if k == 1:
-            ready = after(d_qkv, out_terms[2])
+            ready = after(d_qkv, out_came[-2])
         else:
             ready = after(d_qkv, sent[min(len(sent), 2) - 1])
         return weight_grad(dims, k, origin, normed_all, ready, out_grad)
@@ -779,8 +814,8 @@
         if k == 2:
             dn_parts = input_grad(dims, origin, after(d_qkv, sent[0]), blocks, width)
             held["one"] = total_of(net.scatter_s(dn_parts.reshape(ns, rows, width)))
-            return value
-        return after(value, held["one"], ffn_own) if k == nz - 1 else value
+            return after(value, out_terms[2])
+        return after(value, held["one"]) if k == nz - 1 else value
 
     terms, _ = net.scatter_f(weight_part, weight_gate)
     one_sum = held["one"]

time: 620 us -> 575 us (0.927)
  waiting for transfers between devices: 294 us -> 257 us
    ppermute x18, waiting for transfers between devices: 184 us -> 139 us  [step_z(): return lax.ppermute(value, 'fsdp', self.z_perm)]
    ppermute x18, starting transfers between devices: 43.8 us -> 32.5 us  [step_z(): return lax.ppermute(value, 'fsdp', self.z_perm)]
    unnamed x109 -> x103, local copies, waits for them, and re-layouts: 19.9 us -> 17.8 us
  transfers between devices with their start and end apart: 68 -> 68, of which waited for: 30 -> 32; matrix products, arithmetic and copies ran while one was open for 11% -> 14% of each run, Pallas kernels for 21% -> 22%
where the time goes in v3:
time: 575 us; the launch traced here: 565 us
  waiting for transfers between devices  257 us (45%)
  Pallas kernels  129 us (22%)
  starting transfers between devices  68.5 us (12%)
  local copies, waits for them, and re-layouts  36.6 us (6%)
  other arithmetic  36 us (6%)
  matrix products  22.3 us (4%)
  between operations  14.8 us (3%)
    ppermute x18, waiting for transfers between devices, step_z(): return lax.ppermute(value, 'fsdp', self.z_perm)  139 us
    ppermute x12, waiting for transfers between devices, step_s(): return lax.ppermute(value, BOTH, self.s_perm)  69.5 us
    pallas_call x2, Pallas kernels, ffn(): pl.pallas_call(functools.partial(ffn_kernel, count, not before), grid=(fc...  44.5 us
    ppermute x6, waiting for transfers between devices, swap_s(): got = lax.ppermute(piece, 'seq', perm)  33.2 us
    ppermute x18, starting transfers between devices, step_z(): return lax.ppermute(value, 'fsdp', self.z_perm)  32.5 us
    dot_general x2, matrix products, tn(): lax.dot_general(left, right, (((0,), (0,)), ((), ())), preferred_element_...  22.3 us
    pallas_call x4, Pallas kernels, weight_grad(): pl.pallas_call(functools.partial(weight_grad_kernel, dims, step), in_spec...  21.2 us
    unnamed x103, local copies, waits for them, and re-layouts  17.8 us
  transfers between devices with their start and end apart: 68, of which 32 were waited for; matrix products, arithmetic and copies ran while one was open for 14% of the time, Pallas kernels for 22%

profile of v3, /device:TPU:0, one launch (start us, length us, event | category | flops | bytes accessed | tf_op | source)
XLA Modules:
  0.0 564.5 jit_solution(15015862940003019397)
XLA Ops:
  24.5 11.8 %collective-permute-done.3 = bf16[1,80,1536]{2,1,0:T(8,128)(2,1)S(1)} collective-permute-done((bf16[1,80,1536]{2,1,0:T(8,128)(2,1)S(1)}, bf16[1,80,1536]{2,1,0:T(8,128)(2,1)S(1)}, u32[]{:S(2)}, u32[]{:S(2)}) %collective-permute-start.3) | collective-permute-done | bytes 245792 | tf_op jit(solution)/shard_map/ppermute | solution.py:122
  41.1 13.1 %collective-permute-done.4 = bf16[1,80,1536]{2,1,0:T(8,128)(2,1)S(1)} collective-permute-done((bf16[1,80,1536]{2,1,0:T(8,128)(2,1)S(1)}, bf16[1,80,1536]{2,1,0:T(8,128)(2,1)S(1)}, u32[]{:S(2)}, u32[]{:S(2)}) %collective-permute-start.4) | collective-permute-done | bytes 245792 | tf_op jit(solution)/shard_map/ppermute | solution.py:122
  62.7 21.0 %collective-permute-done.8.refs_2_ = bf16[272,2048]{1,0:T(8,128)(2,1)} collective-permute-done((bf16[272,2048]{1,0:T(8,128)(2,1)S(1)}, bf16[272,2048]{1,0:T(8,128)(2,1)}, u32[]{:S(2)}, u32[]{:S(2)}) %collective-permute-start.8) | collective-permute-done | bytes 1114144 | tf_op jit(solution)/shard_map/ppermute | solution.py:92
  83.6 7.5 %all-to-all-done = bf16[8,64,2048]{2,1,0:T(8,128)(2,1)S(1)} async-done(((bf16[8,64,2048]{2,1,0:T(8,128)(2,1)}), bf16[8,64,2048]{2,1,0:T(8,128)(2,1)S(1)}, u32[]{:S(2)}, u32[]{:S(2)}) %all-to-all-start) | async-done | bytes 2097184 | tf_op jit(solution)/shard_map/all_to_all | solution.py:658
  96.7 22.2 %collective-permute-done.10.refs_4_ = bf16[272,2048]{1,0:T(8,128)(2,1)S(1)} collective-permute-done((bf16[272,2048]{1,0:T(8,128)(2,1)}, bf16[272,2048]{1,0:T(8,128)(2,1)S(1)}, u32[]{:S(2)}, u32[]{:S(2)}) %collective-permute-start.10) | collective-permute-done | bytes 1114144 | tf_op jit(solution)/shard_map/ppermute | solution.py:92
  125.1 6.9 %collective-permute-done.1 = bf16[128,2048]{1,0:T(8,128)(2,1)} collective-permute-done((bf16[128,2048]{1,0:T(8,128)(2,1)}, bf16[128,2048]{1,0:T(8,128)(2,1)}, u32[]{:S(2)}, u32[]{:S(2)}) %collective-permute-start.1) | collective-permute-done | bytes 524320 | tf_op jit(solution)/shard_map/ppermute | solution.py:89
  133.9 10.3 %collective-permute-done.12.refs_6_ = bf16[272,2048]{1,0:T(8,128)(2,1)S(1)} collective-permute-done((bf16[272,2048]{1,0:T(8,128)(2,1)S(1)}, bf16[272,2048]{1,0:T(8,128)(2,1)S(1)}, u32[]{:S(2)}, u32[]{:S(2)}) %collective-permute-start.12) | collective-permute-done | bytes 1114144 | tf_op jit(solution)/shard_map/ppermute | solution.py:92
  159.7 16.5 %shard_map.214 = (bf16[512,512]{1,0:T(8,128)(2,1)}, bf16[512,512]{1,0:T(8,128)(2,1)}, bf16[512,512]{1,0:T(8,128)(2,1)}, bf16[512,512]{1,0:T(8,128)(2,1)}, bf16[5...) custom-call(s32[8]{0:T(128)} %stack.63.origin_ref, ...), custom_call_target="tpu_custom_call" | custom-call | flops 4831838208 | bytes 8388608 | tf_op jit(solution)/shard_map/pallas_call | solution.py:353
  180.1 11.8 %collective-permute-done.15 = bf16[128,2048]{1,0:T(8,128)(2,1)S(1)} collective-permute-done((bf16[128,2048]{1,0:T(8,128)(2,1)S(1)}, bf16[128,2048]{1,0:T(8,128)(2,1)S(1)}, u32[]{:S(2)}, u32[]{:S(2)}) %collective-permute-start.15) | collective-permute-done | bytes 524320 | tf_op jit(solution)/shard_map/ppermute | solution.py:89
  222.1 8.8 %collective-permute-done.21.refs_2_ = bf16[128,2048]{1,0:T(8,128)(2,1)S(1)} collective-permute-done((bf16[128,2048]{1,0:T(8,128)(2,1)}, bf16[128,2048]{1,0:T(8,128)(2,1)S(1)}, u32[]{:S(2)}, u32[]{:S(2)}) %collective-permute-start.21) | collective-permute-done | bytes 524320 | tf_op jit(solution)/shard_map/ppermute | solution.py:92
  237.3 22.3 %shard_map.216 = (bf16[1024,1024]{1,0:T(8,128)(2,1)}, bf16[1024,2048]{1,0:T(8,128)(2,1)}, bf16[1024,2048]{1,0:T(8,128)(2,1)}, bf16[1024,2048]{1,0:T(8,128)(2,1)}...) custom-call(bf16[128,2048]{1,0:T(8,128)(2,1)S(1)} %copy-done.7, ...), custom_call_target="tpu_custom_call" | custom-call | flops 12884901888 | bytes 20971520 | tf_op jit(solution)/shard_map/pallas_call | solution.py:531
  261.6 12.9 %collective-permute-done.28.refs_2_ = bf16[128,2048]{1,0:T(8,128)(2,1)S(1)} collective-permute-done((bf16[128,2048]{1,0:T(8,128)(2,1)S(1)}, bf16[128,2048]{1,0:T(8,128)(2,1)S(1)}, u32[]{:S(2)}, u32[]{:S(2)}) %collective-permute-start.28) | collective-permute-done | bytes 524320 | tf_op jit(solution)/shard_map/ppermute | solution.py:92
  279.8 22.2 %shard_map.217 = (bf16[1024,1024]{1,0:T(8,128)(2,1)}, bf16[1024,2048]{1,0:T(8,128)(2,1)}, bf16[1024,2048]{1,0:T(8,128)(2,1)}, bf16[1024,2048]{1,0:T(8,128)(2,1)}...) custom-call(bf16[128,2048]{1,0:T(8,128)(2,1)S(1)} %copy-done.6, ...), custom_call_target="tpu_custom_call", output_to_operand_aliasing={{0}: (10, {}), {1}: (11, {}), {2}: (12, {}), {3}: (13, {})} | custom-call | flops 12884901888 | bytes 20971520 | tf_op jit(solution)/shard_map/pallas_call | solution.py:531
  306.4 8.3 %convolution_convert_fusion.1 = bf16[1024,2048]{1,0:T(8,128)(2,1)} fusion(bf16[1024,1024]{1,0:T(8,128)(2,1)S(1)} %copy-done.49, bf16[1024,2048]{1,0:T(8,128)(2,1)} %get-tuple-element.126), kind=kOutput, calls=%fused_computation.2 | convolution fusion | flops 4297064448 | bytes 10485760 | tf_op jit(solution)/shard_map/dot_general | solution.py:35
  323.5 14.0 %convolution_convert_fusion = bf16[2048,2048]{1,0:T(8,128)(2,1)} fusion(bf16[1024,2048]{1,0:T(8,128)(2,1)} %get-tuple-element.128, bf16[1024,2048]{1,0:T(8,128)(2,1)} %get-tuple-element.129), kind=kOutput, calls=%fused_computation | convolution fusion | flops 8594128896 | bytes 16777216 | tf_op jit(solution)/shard_map/dot_general | solution.py:35
  343.7 7.8 %collective-permute-done.42 = bf16[128,2048]{1,0:T(8,128)(2,1)S(1)} collective-permute-done((bf16[128,2048]{1,0:T(8,128)(2,1)}, bf16[128,2048]{1,0:T(8,128)(2,1)S(1)}, u32[]{:S(2)}, u32[]{:S(2)}) %collective-permute-start.42) | collective-permute-done | bytes 524320 | tf_op jit(solution)/shard_map/ppermute | solution.py:89
  352.2 11.6 %collective-permute-done.43 = bf16[128,2048]{1,0:T(8,128)(2,1)S(1)} collective-permute-done((bf16[128,2048]{1,0:T(8,128)(2,1)S(1)}, bf16[128,2048]{1,0:T(8,128)(2,1)S(1)}, u32[]{:S(2)}, u32[]{:S(2)}) %collective-permute-start.43) | collective-permute-done | bytes 524320 | tf_op jit(solution)/shard_map/ppermute | solution.py:92
  364.3 8.8 %collective-permute-done.47 = bf16[128,2048]{1,0:T(8,128)(2,1)S(1)} collective-permute-done((bf16[128,2048]{1,0:T(8,128)(2,1)S(1)}, bf16[128,2048]{1,0:T(8,128)(2,1)S(1)}, u32[]{:S(2)}, u32[]{:S(2)}) %collective-permute-start.47) | collective-permute-done | bytes 524320 | tf_op jit(solution)/shard_map/ppermute | solution.py:89
  379.9 14.9 %shard_map.219 = (bf16[512,1536]{1,0:T(8,128)(2,1)}, bf16[4,512,512]{2,1,0:T(8,128)(2,1)}) custom-call(s32[8]{0:T(128)} %stack.63.origin_ref, bf16[512,2048]{1,0:T(8,128)(2,1)} %pad_maximum_fusion.datt_ref, bf16[512,512]{1,0:T(8,128)(2,1)} %get-tuple-element.139.q_ref, bf16[512,512]{1,0:T(8,128)(2,1)} %get-tuple-element.140.k_ref, ...), custom_call_target="tpu_custom_call" | custom-call | flops 3489660928 | bytes 4194304 | tf_op jit(solution)/shard_map/pallas_call | solution.py:413
  414.0 9.2 %shard_map.221 = bf16[512,2048]{1,0:T(8,128)(2,1)} custom-call(s32[8]{0:T(128)} %stack.63.origin_ref, bf16[512,1536]{1,0:T(8,128)(2,1)} %get-tuple-element.153.d_ref, bf16[272,2048]{1,0:T(8,128)(2,1)} %copy-done.9, bf16[272,2048]{1,0:T(8,128)(2,1)} %collective-permute-done.7.refs_1_, bf16[272,2048]{1,0:T(8,128)(2,1)} %collective-permute-done.8.refs_2_, ...), custom_call_target="tpu_custom_call" | custom-call | flops 3221225472 | bytes 8388608 | tf_op jit(solution)/shard_map/pallas_call | solution.py:466
  432.6 8.8 %collective-permute-done.45 = bf16[128,2048]{1,0:T(8,128)(2,1)S(1)} collective-permute-done((bf16[128,2048]{1,0:T(8,128)(2,1)}, bf16[128,2048]{1,0:T(8,128)(2,1)S(1)}, u32[]{:S(2)}, u32[]{:S(2)}) %collective-permute-start.45) | collective-permute-done | bytes 524320 | tf_op jit(solution)/shard_map/ppermute | solution.py:92
  475.9 17.0 %collective-permute-done.51 = bf16[128,2048]{1,0:T(8,128)(2,1)S(1)} collective-permute-done((bf16[128,2048]{1,0:T(8,128)(2,1)S(1)}, bf16[128,2048]{1,0:T(8,128)(2,1)S(1)}, u32[]{:S(2)}, u32[]{:S(2)}) %collective-permute-start.51) | collective-permute-done | bytes 524320 | tf_op jit(solution)/shard_map/ppermute | solution.py:89
  493.3 28.9 %collective-permute-done.57 = bf16[256,2048]{1,0:T(8,128)(2,1)S(1)} collective-permute-done((bf16[256,2048]{1,0:T(8,128)(2,1)S(1)}, bf16[256,2048]{1,0:T(8,128)(2,1)S(1)}, u32[]{:S(2)}, u32[]{:S(2)}) %collective-permute-start.57) | collective-permute-done | bytes 1048608 | tf_op jit(solution)/shard_map/ppermute | solution.py:92
  549.1 7.1 %shard_map.226 = (f32[64,8192]{1,0:T(8,128)}, f32[64,8192]{1,0:T(8,128)}, f32[64,1]{1,0:T(8,128)}) custom-call(bf16[64,8192]{1,0:T(8,128)(2,1)} %w_gate_ref.1, bf16[64,8192]{1,0:T(8,128)(2,1)} %w_up_ref.1, f32[64,1]{1,0:T(8,128)} %copy.50.gain_ref, bf16[8,64,2048]{2,1,0:T(8,128)(2,1)} %all-to-all-done.1.in_ref), custom_call_target="tpu_custom_call" | custom-call | tf_op jit(solution)/shard_map/pallas_call | solution.py:206
  (305 shorter events, 226.2 us)
Async XLA Ops:
  7.2 228.3 %all-gather.5.cloned.1.call-start = ((), (), s32[]{:S(2)}) async-start(), calls=%async_computation.5 | async-start | bytes 5242880 | tf_op jit(solution)/shard_map/all_gather | solution.py:656
  11.7 79.4 %all-to-all-start = ((bf16[8,64,2048]{2,1,0:T(8,128)(2,1)}), bf16[8,64,2048]{2,1,0:T(8,128)(2,1)S(1)}, u32[]{:S(2)}, u32[]{:S(2)}) async-start(bf16[8,64,2048]{2,1,0:T(8,128)(2,1)} %shard_map.212), calls=%async_computation | async-start | bytes 4194304 | tf_op jit(solution)/shard_map/all_to_all | solution.py:658
  18.2 218.1 %all-gather.3.cloned.1.call-start = ((), (), s32[]{:S(2)}) async-start(), calls=%async_computation.4 | async-start | bytes 10485760 | tf_op jit(solution)/shard_map/all_gather | solution.py:680
  59.8 23.8 %collective-permute-start.8 = (bf16[272,2048]{1,0:T(8,128)(2,1)S(1)}, bf16[272,2048]{1,0:T(8,128)(2,1)}, u32[]{:S(2)}, u32[]{:S(2)}) collective-permute-start(bf16[272,2048]{1,0:T(8,128)(2,1)S(1)} %fusion.1.refs_0_), channel_id=1, source_target_pairs={{0,4},{1,5},{2,0},{3,1},{4,6},{5,7},{6,2},{7,3},{8,12},{9,13},{10,... | collective-permute-start | bytes 3342344 | tf_op jit(solution)/shard_map/ppermute | solution.py:92
  92.5 367.1 %reduce-scatter.7.cloned.1.call-start = ((), (), s32[]{:S(2)}) async-start(), calls=%async_computation.7 | async-start | bytes 10485760
  92.5 26.4 %collective-permute-start.10 = (bf16[272,2048]{1,0:T(8,128)(2,1)}, bf16[272,2048]{1,0:T(8,128)(2,1)S(1)}, u32[]{:S(2)}, u32[]{:S(2)}) collective-permute-start(bf16[272,2048]{1,0:T(8,128)(2,1)} %collective-permute-done.8.refs_2_), channel_id=1, source_target_pairs={{0,4},{1,5},{2,0},{3,1},{4,6},{5,7},{6,2},{7,3},{8,12},{9,13},{10,... | collective-permute-start | bytes 3342344 | tf_op jit(solution)/shard_map/ppermute | solution.py:92
  92.6 28.2 %collective-permute-start = (bf16[128,2048]{1,0:T(8,128)(2,1)}, bf16[128,2048]{1,0:T(8,128)(2,1)}, u32[]{:S(2)}, u32[]{:S(2)}) collective-permute-start(bf16[128,2048]{1,0:T(8,128)(2,1)} %input_ref.1), channel_id=1, source_target_pairs={{0,8},{8,24},{16,0},{24,16},{1,17},{9,1},{17,25},{25,9},{2,10},{10... | collective-permute-start | bytes 1572872 | tf_op jit(solution)/shard_map/ppermute | solution.py:89
  118.9 25.3 %collective-permute-start.12 = (bf16[272,2048]{1,0:T(8,128)(2,1)S(1)}, bf16[272,2048]{1,0:T(8,128)(2,1)S(1)}, u32[]{:S(2)}, u32[]{:S(2)}) collective-permute-start(bf16[272,2048]{1,0:T(8,128)(2,1)S(1)} %collective-permute-done.10.refs_4_), channel_id=1, source_target_pairs={{0,4},{1,5},{2,0},{3,1},{4,6},{5,7},{6,2},{7,3},{8,12},{9,13},{10,... | collective-permute-start | bytes 3342344 | tf_op jit(solution)/shard_map/ppermute | solution.py:92
  120.1 39.6 %collective-permute-start.7 = (bf16[272,2048]{1,0:T(8,128)(2,1)S(1)}, bf16[272,2048]{1,0:T(8,128)(2,1)}, u32[]{:S(2)}, u32[]{:S(2)}) collective-permute-start(bf16[272,2048]{1,0:T(8,128)(2,1)S(1)} %fusion.1.refs_0_), channel_id=1, source_target_pairs={{0,1},{1,0},{2,3},{3,2},{4,5},{5,4},{6,7},{7,6},{8,9},{9,8},{10,11... | collective-permute-start | bytes 3342344 | tf_op jit(solution)/shard_map/ppermute | solution.py:95
  133.4 26.3 %collective-permute-start.9 = (bf16[272,2048]{1,0:T(8,128)(2,1)}, bf16[272,2048]{1,0:T(8,128)(2,1)}, u32[]{:S(2)}, u32[]{:S(2)}) collective-permute-start(bf16[272,2048]{1,0:T(8,128)(2,1)} %collective-permute-done.8.refs_2_), channel_id=1, source_target_pairs={{0,1},{1,0},{2,3},{3,2},{4,5},{5,4},{6,7},{7,6},{8,9},{9,8},{10,11... | collective-permute-start | bytes 3342344 | tf_op jit(solution)/shard_map/ppermute | solution.py:95
  133.5 26.1 %collective-permute-start.11 = (bf16[272,2048]{1,0:T(8,128)(2,1)S(1)}, bf16[272,2048]{1,0:T(8,128)(2,1)}, u32[]{:S(2)}, u32[]{:S(2)}) collective-permute-start(bf16[272,2048]{1,0:T(8,128)(2,1)S(1)} %collective-permute-done.10.refs_4_), channel_id=1, source_target_pairs={{0,1},{1,0},{2,3},{3,2},{4,5},{5,4},{6,7},{7,6},{8,9},{9,8},{10,11... | collective-permute-start | bytes 3342344 | tf_op jit(solution)/shard_map/ppermute | solution.py:95
  230.9 29.5 %collective-permute-start.26 = (bf16[128,2048]{1,0:T(8,128)(2,1)S(1)}, bf16[128,2048]{1,0:T(8,128)(2,1)S(1)}, u32[]{:S(2)}, u32[]{:S(2)}) collective-permute-start(bf16[128,2048]{1,0:T(8,128)(2,1)S(1)} %collective-permute-done.21.refs_2_), channel_id=1, source_target_pairs={{0,4},{1,5},{2,0},{3,1},{4,6},{5,7},{6,2},{7,3},{8,12},{9,13},{10,... | collective-permute-start | bytes 1572872 | tf_op jit(solution)/shard_map/ppermute | solution.py:92
  275.2 27.9 %collective-permute-start.38 = (bf16[128,2048]{1,0:T(8,128)(2,1)S(1)}, bf16[128,2048]{1,0:T(8,128)(2,1)S(1)}, u32[]{:S(2)}, u32[]{:S(2)}) collective-permute-start(bf16[128,2048]{1,0:T(8,128)(2,1)S(1)} %add_convert_fusion.12), channel_id=1, source_target_pairs={{0,4},{1,5},{2,0},{3,1},{4,6},{5,7},{6,2},{7,3},{8,12},{9,13},{10,... | collective-permute-start | bytes 1572872 | tf_op jit(solution)/shard_map/ppermute | solution.py:92
  302.4 40.2 %collective-permute-start.35 = (bf16[128,2048]{1,0:T(8,128)(2,1)}, bf16[128,2048]{1,0:T(8,128)(2,1)}, u32[]{:S(2)}, u32[]{:S(2)}) collective-permute-start(bf16[128,2048]{1,0:T(8,128)(2,1)} %get-tuple-element.118), channel_id=1, source_target_pairs={{0,1},{1,0},{2,3},{3,2},{4,5},{5,4},{6,7},{7,6},{8,9},{9,8},{10,11... | collective-permute-start | bytes 1572872 | tf_op jit(solution)/shard_map/ppermute | solution.py:95
  302.5 35.0 %collective-permute-start.40 = (bf16[128,2048]{1,0:T(8,128)(2,1)}, bf16[128,2048]{1,0:T(8,128)(2,1)}, u32[]{:S(2)}, u32[]{:S(2)}) collective-permute-start(bf16[128,2048]{1,0:T(8,128)(2,1)} %get-tuple-element.131), channel_id=1, source_target_pairs={{0,1},{1,0},{2,3},{3,2},{4,5},{5,4},{6,7},{7,6},{8,9},{9,8},{10,11... | collective-permute-start | bytes 1572872 | tf_op jit(solution)/shard_map/ppermute | solution.py:95
  373.9 172.4 %reduce-scatter.5.cloned.1.call-start = ((), (), s32[]{:S(2)}) async-start(), calls=%async_computation.6 | async-start | bytes 5242880 | tf_op jit(solution)/shard_map/reduce_scatter | solution.py:759
  404.9 26.1 %collective-permute-start.53 = (bf16[256,2048]{1,0:T(8,128)(2,1)S(1)}, bf16[256,2048]{1,0:T(8,128)(2,1)S(1)}, u32[]{:S(2)}, u32[]{:S(2)}) collective-permute-start(bf16[256,2048]{1,0:T(8,128)(2,1)S(1)} %add_convert_fusion.3), channel_id=1, source_target_pairs={{0,4},{1,5},{2,0},{3,1},{4,6},{5,7},{6,2},{7,3},{8,12},{9,13},{10,... | collective-permute-start | bytes 3145736 | tf_op jit(solution)/shard_map/ppermute | solution.py:92
  412.5 29.0 %collective-permute-start.45 = (bf16[128,2048]{1,0:T(8,128)(2,1)}, bf16[128,2048]{1,0:T(8,128)(2,1)S(1)}, u32[]{:S(2)}, u32[]{:S(2)}) collective-permute-start(bf16[128,2048]{1,0:T(8,128)(2,1)} %add_convert_fusion.7), channel_id=1, source_target_pairs={{0,4},{1,5},{2,0},{3,1},{4,6},{5,7},{6,2},{7,3},{8,12},{9,13},{10,... | collective-permute-start | bytes 1572872 | tf_op jit(solution)/shard_map/ppermute | solution.py:92
  425.1 25.5 %collective-permute-start.49 = (bf16[128,2048]{1,0:T(8,128)(2,1)}, bf16[128,2048]{1,0:T(8,128)(2,1)}, u32[]{:S(2)}, u32[]{:S(2)}) collective-permute-start(bf16[128,2048]{1,0:T(8,128)(2,1)} %slice.93), channel_id=1, source_target_pairs={{0,8},{8,24},{16,0},{24,16},{1,17},{9,1},{17,25},{25,9},{2,10},{10... | collective-permute-start | bytes 1572872 | tf_op jit(solution)/shard_map/ppermute | solution.py:89
  441.4 24.8 %collective-permute-start.56 = (bf16[256,2048]{1,0:T(8,128)(2,1)}, bf16[256,2048]{1,0:T(8,128)(2,1)}, u32[]{:S(2)}, u32[]{:S(2)}) collective-permute-start(bf16[256,2048]{1,0:T(8,128)(2,1)} %add_convert_fusion.2), channel_id=1, source_target_pairs={{0,4},{1,5},{2,0},{3,1},{4,6},{5,7},{6,2},{7,3},{8,12},{9,13},{10,... | collective-permute-start | bytes 3145736 | tf_op jit(solution)/shard_map/ppermute | solution.py:92
  450.1 23.5 %collective-permute-start.25 = (bf16[128,2048]{1,0:T(8,128)(2,1)S(1)}, bf16[128,2048]{1,0:T(8,128)(2,1)}, u32[]{:S(2)}, u32[]{:S(2)}) collective-permute-start(bf16[128,2048]{1,0:T(8,128)(2,1)S(1)} %get-tuple-element.100), channel_id=1, source_target_pairs={{0,1},{1,0},{2,3},{3,2},{4,5},{5,4},{6,7},{7,6},{8,9},{9,8},{10,11... | collective-permute-start | bytes 1572872 | tf_op jit(solution)/shard_map/ppermute | solution.py:95
  458.7 34.7 %collective-permute-start.54 = (bf16[256,2048]{1,0:T(8,128)(2,1)}, bf16[256,2048]{1,0:T(8,128)(2,1)}, u32[]{:S(2)}, u32[]{:S(2)}) collective-permute-start(bf16[256,2048]{1,0:T(8,128)(2,1)} %get-tuple-element.155), channel_id=1, source_target_pairs={{0,1},{1,0},{2,3},{3,2},{4,5},{5,4},{6,7},{7,6},{8,9},{9,8},{10,11... | collective-permute-start | bytes 3145736 | tf_op jit(solution)/shard_map/ppermute | solution.py:95
  459.6 89.5 %all-to-all-start.1 = ((bf16[8,64,2048]{2,1,0:T(8,128)(2,1)}), bf16[8,64,2048]{2,1,0:T(8,128)(2,1)}, u32[]{:S(2)}, u32[]{:S(2)}) async-start(bf16[8,64,2048]{2,1,0:T(8,128)(2,1)} %bitcast.58), calls=%async_computation.1 | async-start | bytes 4194304 | tf_op jit(solution)/shard_map/all_to_all | solution.py:791
  468.8 53.5 %collective-permute-start.57 = (bf16[256,2048]{1,0:T(8,128)(2,1)S(1)}, bf16[256,2048]{1,0:T(8,128)(2,1)S(1)}, u32[]{:S(2)}, u32[]{:S(2)}) collective-permute-start(bf16[256,2048]{1,0:T(8,128)(2,1)S(1)} %add_convert_fusion.1), channel_id=1, source_target_pairs={{0,4},{1,5},{2,0},{3,1},{4,6},{5,7},{6,2},{7,3},{8,12},{9,13},{10,... | collective-permute-start | bytes 3145736 | tf_op jit(solution)/shard_map/ppermute | solution.py:92
  (94 other events, 1081.5 us)
Sparse Core Ops, SparseCore 0:
  9.9 63.7 all-gather.4
  92.6 96.3 all-gather.2
  374.0 85.5 reduce-scatter.6
  462.7 59.1 reduce-scatter.4

commit v4 on v3

--- a/solution.py
+++ b/solution.py
@@ -17,7 +17,7 @@
 TILE = 256
 EXTRA = 16
 FTILE = 512
-VMEM_LIMIT = 56 * 1024 * 1024
+VMEM_LIMIT = 32 * 1024 * 1024
 PARAMS = pltpu.CompilerParams(vmem_limit_bytes=VMEM_LIMIT)
 FFN_PARAMS = pltpu.CompilerParams(vmem_limit_bytes=48 * 1024 * 1024)
 WHOLE = pl.BlockSpec(memory_space=pltpu.VMEM)
@@ -788,16 +788,6 @@
         send_out(k, d_low)
     out_terms = (out_parts[0], net.swap_c(out_parts[1]), out_came[-1])
     layer_out = (residual + total_of(out_terms)).astype(BF)
-    ffn_own = lax.all_to_all(
-        ffn_sum.reshape(nf, own, 2 * fcols), "fsdp", split_axis=0, concat_axis=0, tiled=True
-    )
-    grad_gate, grad_up, grad_ffn_gain = unpack_ffn(
-        w_gate,
-        w_up,
-        ffn_gain.astype(F32)[:, None],
-        ffn_own,
-    )
-
     d_qkv, out_grad = attend_back(
         dims, origin, jnp.concatenate(d_attended, axis=0), saved, tables, pair_marks, blocks
     )
@@ -815,9 +805,18 @@
             dn_parts = input_grad(dims, origin, after(d_qkv, sent[0]), blocks, width)
             held["one"] = total_of(net.scatter_s(dn_parts.reshape(ns, rows, width)))
             return after(value, out_terms[2])
-        return after(value, held["one"]) if k == nz - 1 else value
-
-    terms, _ = net.scatter_f(weight_part, weight_gate)
+        return value
+
+    terms, weight_sent = net.scatter_f(weight_part, weight_gate)
+    ffn_own = lax.all_to_all(
+        after(ffn_sum, weight_sent[-1]).reshape(nf, own, 2 * fcols), "fsdp", split_axis=0, concat_axis=0, tiled=True
+    )
+    grad_gate, grad_up, grad_ffn_gain = unpack_ffn(
+        w_gate,
+        w_up,
+        ffn_gain.astype(F32)[:, None],
+        ffn_own,
+    )
     one_sum = held["one"]
     scaled_one = one_sum * gain_one
     grad_input = d_residual + inverse_one * (

time: 575 us -> 573 us (level)
  waiting for transfers between devices: 257 us -> 294 us
  Pallas kernels: 129 us -> 98.6 us
  other arithmetic: 36 us -> 26.7 us
    ppermute x12, waiting for transfers between devices: 69.5 us -> 86.7 us  [step_s(): return lax.ppermute(value, BOTH, self.s_perm)]
    pallas_call x4, Pallas kernels: 21.2 us -> 7.32 us  [weight_grad(): pl.pallas_call(functools.partial(weight_grad_kernel, dims, step), in_spec...]
    ppermute x18, waiting for transfers between devices: 139 us -> 152 us  [step_z(): return lax.ppermute(value, 'fsdp', self.z_perm)]
    unnamed x103 -> x181, local copies, waits for them, and re-layouts: 17.8 us -> 26.6 us
    all_to_all x1, waiting for transfers between devices: 7.47 us -> 14.3 us  [shards(): lax.all_to_all(packed_ffn, 'fsdp', split_axis=0, concat_axis=0, tiled=True)]
  transfers between devices with their start and end apart: 68 -> 68, of which waited for: 32 -> 31; matrix products, arithmetic and copies ran while one was open for 14% -> 11% of each run, Pallas kernels for 22% -> 16%
where the time goes in v4:
time: 573 us; the launch traced here: 563 us
  waiting for transfers between devices  294 us (51%)
  Pallas kernels  98.6 us (17%)
  starting transfers between devices  72.5 us (13%)
  local copies, waits for them, and re-layouts  33.3 us (6%)
  other arithmetic  26.7 us (5%)
  matrix products  22.5 us (4%)
  between operations  15.4 us (3%)
    ppermute x18, waiting for transfers between devices, step_z(): return lax.ppermute(value, 'fsdp', self.z_perm)  152 us
    ppermute x12, waiting for transfers between devices, step_s(): return lax.ppermute(value, BOTH, self.s_perm)  86.7 us
    pallas_call x2, Pallas kernels, ffn(): pl.pallas_call(functools.partial(ffn_kernel, count, not before), grid=(fc...  45.1 us
    ppermute x18, starting transfers between devices, step_z(): return lax.ppermute(value, 'fsdp', self.z_perm)  34.1 us
    ppermute x6, waiting for transfers between devices, swap_s(): got = lax.ppermute(piece, 'seq', perm)  30.7 us
    unnamed x181, local copies, waits for them, and re-layouts  26.6 us
    dot_general x2, matrix products, tn(): lax.dot_general(left, right, (((0,), (0,)), ((), ())), preferred_element_...  22.5 us
    all_to_all x1, waiting for transfers between devices, shards(): lax.all_to_all(packed_ffn, 'fsdp', split_axis=0, concat_axis=0, tiled=True)  14.3 us
  transfers between devices with their start and end apart: 68, of which 31 were waited for; matrix products, arithmetic and copies ran while one was open for 11% of the time, Pallas kernels for 16%

profile of v4, /device:TPU:0, one launch (start us, length us, event | category | flops | bytes accessed | tf_op | source)
XLA Modules:
  0.0 562.6 jit_solution(9650609378472001987)
XLA Ops:
  20.9 10.6 %collective-permute-done.3 = bf16[1,80,1536]{2,1,0:T(8,128)(2,1)S(1)} collective-permute-done((bf16[1,80,1536]{2,1,0:T(8,128)(2,1)S(1)}, bf16[1,80,1536]{2,1,0:T(8,128)(2,1)S(1)}, u32[]{:S(2)}, u32[]{:S(2)}) %collective-permute-start.3) | collective-permute-done | bytes 245792 | tf_op jit(solution)/shard_map/ppermute | solution.py:122
  52.4 24.6 %collective-permute-done.8.refs_2_ = bf16[272,2048]{1,0:T(8,128)(2,1)} collective-permute-done((bf16[272,2048]{1,0:T(8,128)(2,1)S(1)}, bf16[272,2048]{1,0:T(8,128)(2,1)}, u32[]{:S(2)}, u32[]{:S(2)}) %collective-permute-start.8) | collective-permute-done | bytes 1114144 | tf_op jit(solution)/shard_map/ppermute | solution.py:92
  76.9 14.3 %all-to-all-done = bf16[8,64,2048]{2,1,0:T(8,128)(2,1)} async-done(((bf16[8,64,2048]{2,1,0:T(8,128)(2,1)}), bf16[8,64,2048]{2,1,0:T(8,128)(2,1)}, u32[]{:S(2)}, u32[]{:S(2)}) %all-to-all-start) | async-done | bytes 2097184 | tf_op jit(solution)/shard_map/all_to_all | solution.py:658
  93.9 23.9 %collective-permute-done.10.refs_4_ = bf16[272,2048]{1,0:T(8,128)(2,1)} collective-permute-done((bf16[272,2048]{1,0:T(8,128)(2,1)}, bf16[272,2048]{1,0:T(8,128)(2,1)}, u32[]{:S(2)}, u32[]{:S(2)}) %collective-permute-start.10) | collective-permute-done | bytes 1114144 | tf_op jit(solution)/shard_map/ppermute | solution.py:92
  122.6 8.2 %collective-permute-done.1 = bf16[128,2048]{1,0:T(8,128)(2,1)} collective-permute-done((bf16[128,2048]{1,0:T(8,128)(2,1)S(1)}, bf16[128,2048]{1,0:T(8,128)(2,1)}, u32[]{:S(2)}, u32[]{:S(2)}) %collective-permute-start.1) | collective-permute-done | bytes 524320 | tf_op jit(solution)/shard_map/ppermute | solution.py:89
  132.2 11.2 %collective-permute-done.12.refs_6_ = bf16[272,2048]{1,0:T(8,128)(2,1)} collective-permute-done((bf16[272,2048]{1,0:T(8,128)(2,1)}, bf16[272,2048]{1,0:T(8,128)(2,1)}, u32[]{:S(2)}, u32[]{:S(2)}) %collective-permute-start.12) | collective-permute-done | bytes 1114144 | tf_op jit(solution)/shard_map/ppermute | solution.py:92
  161.1 12.7 %shard_map.214 = (bf16[512,512]{1,0:T(8,128)(2,1)S(1)}, bf16[512,512]{1,0:T(8,128)(2,1)S(1)}, bf16[512,512]{1,0:T(8,128)(2,1)S(1)}, bf16[512,512]{1,0:T(8,128)(2...) custom-call(s32[8]{0:T(128)S(1)} %stack.63.origin_ref, ...), custom_call_target="tpu_custom_call" | custom-call | flops 4831838208 | bytes 8388608 | tf_op jit(solution)/shard_map/pallas_call | solution.py:353
  176.4 14.3 %collective-permute-done.15 = bf16[128,2048]{1,0:T(8,128)(2,1)S(1)} collective-permute-done((bf16[128,2048]{1,0:T(8,128)(2,1)S(1)}, bf16[128,2048]{1,0:T(8,128)(2,1)S(1)}, u32[]{:S(2)}, u32[]{:S(2)}) %collective-permute-start.15) | collective-permute-done | bytes 524320 | tf_op jit(solution)/shard_map/ppermute | solution.py:89
  206.1 7.4 %collective-permute-done.19.came_ref = bf16[128,2048]{1,0:T(8,128)(2,1)S(1)} collective-permute-done((bf16[128,2048]{1,0:T(8,128)(2,1)S(1)}, bf16[128,2048]{1,0:T(8,128)(2,1)S(1)}, u32[]{:S(2)}, u32[]{:S(2)}) %collective-permute-start.19) | collective-permute-done | bytes 524320 | tf_op jit(solution)/shard_map/ppermute | solution.py:89
  219.0 7.8 %collective-permute-done.21.refs_2_ = bf16[128,2048]{1,0:T(8,128)(2,1)} collective-permute-done((bf16[128,2048]{1,0:T(8,128)(2,1)S(1)}, bf16[128,2048]{1,0:T(8,128)(2,1)}, u32[]{:S(2)}, u32[]{:S(2)}) %collective-permute-start.21) | collective-permute-done | bytes 524320 | tf_op jit(solution)/shard_map/ppermute | solution.py:92
  232.6 22.8 %shard_map.216 = (bf16[1024,1024]{1,0:T(8,128)(2,1)}, bf16[1024,2048]{1,0:T(8,128)(2,1)}, bf16[1024,2048]{1,0:T(8,128)(2,1)}, bf16[1024,2048]{1,0:T(8,128)(2,1)}...) custom-call(bf16[128,2048]{1,0:T(8,128)(2,1)S(1)} %copy-done.56, ...), custom_call_target="tpu_custom_call" | custom-call | flops 12884901888 | bytes 20971520 | tf_op jit(solution)/shard_map/pallas_call | solution.py:531
  257.7 12.8 %collective-permute-done.28.refs_2_ = bf16[128,2048]{1,0:T(8,128)(2,1)S(1)} collective-permute-done((bf16[128,2048]{1,0:T(8,128)(2,1)}, bf16[128,2048]{1,0:T(8,128)(2,1)S(1)}, u32[]{:S(2)}, u32[]{:S(2)}) %collective-permute-start.28) | collective-permute-done | bytes 524320 | tf_op jit(solution)/shard_map/ppermute | solution.py:92
  274.7 22.3 %shard_map.217 = (bf16[1024,1024]{1,0:T(8,128)(2,1)}, bf16[1024,2048]{1,0:T(8,128)(2,1)}, bf16[1024,2048]{1,0:T(8,128)(2,1)}, bf16[1024,2048]{1,0:T(8,128)(2,1)}...) custom-call(bf16[128,2048]{1,0:T(8,128)(2,1)} %collective-permute-do, ...), custom_call_target="tpu_custom_call", output_to_operand_aliasing={{0}: (10, {}), {1}: (11, {}), {2}: (12, {}), {3}: (13, {})} | custom-call | flops 12884901888 | bytes 20971520 | tf_op jit(solution)/shard_map/pallas_call | solution.py:531
  304.1 8.3 %convolution_convert_fusion.1 = bf16[1024,2048]{1,0:T(8,128)(2,1)} fusion(bf16[1024,1024]{1,0:T(8,128)(2,1)S(1)} %copy-done.88, bf16[1024,2048]{1,0:T(8,128)(2,1)} %get-tuple-element.126), kind=kOutput, calls=%fused_computation.2 | convolution fusion | flops 4297064448 | bytes 10485760 | tf_op jit(solution)/shard_map/dot_general | solution.py:35
  321.2 14.2 %convolution_convert_fusion = bf16[2048,2048]{1,0:T(8,128)(2,1)} fusion(bf16[1024,2048]{1,0:T(8,128)(2,1)} %get-tuple-element.128, bf16[1024,2048]{1,0:T(8,128)(2,1)} %get-tuple-element.129), kind=kOutput, calls=%fused_computation | convolution fusion | flops 8594128896 | bytes 16777216 | tf_op jit(solution)/shard_map/dot_general | solution.py:35
  340.2 7.2 %collective-permute-done.42 = bf16[128,2048]{1,0:T(8,128)(2,1)S(1)} collective-permute-done((bf16[128,2048]{1,0:T(8,128)(2,1)S(1)}, bf16[128,2048]{1,0:T(8,128)(2,1)S(1)}, u32[]{:S(2)}, u32[]{:S(2)}) %collective-permute-start.42) | collective-permute-done | bytes 524320 | tf_op jit(solution)/shard_map/ppermute | solution.py:89
  348.3 11.1 %collective-permute-done.43 = bf16[128,2048]{1,0:T(8,128)(2,1)S(1)} collective-permute-done((bf16[128,2048]{1,0:T(8,128)(2,1)S(1)}, bf16[128,2048]{1,0:T(8,128)(2,1)S(1)}, u32[]{:S(2)}, u32[]{:S(2)}) %collective-permute-start.43) | collective-permute-done | bytes 524320 | tf_op jit(solution)/shard_map/ppermute | solution.py:92
  361.1 8.4 %collective-permute-done.47 = bf16[128,2048]{1,0:T(8,128)(2,1)S(1)} collective-permute-done((bf16[128,2048]{1,0:T(8,128)(2,1)S(1)}, bf16[128,2048]{1,0:T(8,128)(2,1)S(1)}, u32[]{:S(2)}, u32[]{:S(2)}) %collective-permute-start.47) | collective-permute-done | bytes 524320 | tf_op jit(solution)/shard_map/ppermute | solution.py:89
  377.2 12.0 %shard_map.219 = (bf16[512,1536]{1,0:T(8,128)(2,1)S(1)}, bf16[4,512,512]{2,1,0:T(8,128)(2,1)S(1)}) custom-call(s32[8]{0:T(128)S(1)} %stack.63.origin_ref, bf16[512,2048]{1,0:T(8,128)(2,1)S(1)} %pad_maximum_fusion.datt_ref, bf16[512,512]{1,0:T(8,128)(2,1)S(1)} %copy-done.33, bf16[512,512]{1,0:T(8,128)(2,1)S(1)} %copy-done.35, ...), custom_call_target="tpu_custom_call" | custom-call | flops 3489660928 | bytes 4194304 | tf_op jit(solution)/shard_map/pallas_call | solution.py:413
  406.8 17.1 %collective-permute-done.53 = bf16[256,2048]{1,0:T(8,128)(2,1)S(1)} collective-permute-done((bf16[256,2048]{1,0:T(8,128)(2,1)S(1)}, bf16[256,2048]{1,0:T(8,128)(2,1)S(1)}, u32[]{:S(2)}, u32[]{:S(2)}) %collective-permute-start.53) | collective-permute-done | bytes 1048608 | tf_op jit(solution)/shard_map/ppermute | solution.py:92
  424.5 9.8 %collective-permute-done.45 = bf16[128,2048]{1,0:T(8,128)(2,1)S(1)} collective-permute-done((bf16[128,2048]{1,0:T(8,128)(2,1)S(1)}, bf16[128,2048]{1,0:T(8,128)(2,1)S(1)}, u32[]{:S(2)}, u32[]{:S(2)}) %collective-permute-start.45) | collective-permute-done | bytes 524320 | tf_op jit(solution)/shard_map/ppermute | solution.py:92
  446.1 13.2 %collective-permute-done.49 = bf16[128,2048]{1,0:T(8,128)(2,1)S(1)} collective-permute-done((bf16[128,2048]{1,0:T(8,128)(2,1)S(1)}, bf16[128,2048]{1,0:T(8,128)(2,1)S(1)}, u32[]{:S(2)}, u32[]{:S(2)}) %collective-permute-start.49) | collective-permute-done | bytes 524320 | tf_op jit(solution)/shard_map/ppermute | solution.py:89
  480.8 17.8 %collective-permute-done.51 = bf16[128,2048]{1,0:T(8,128)(2,1)S(1)} collective-permute-done((bf16[128,2048]{1,0:T(8,128)(2,1)S(1)}, bf16[128,2048]{1,0:T(8,128)(2,1)S(1)}, u32[]{:S(2)}, u32[]{:S(2)}) %collective-permute-start.51) | collective-permute-done | bytes 524320 | tf_op jit(solution)/shard_map/ppermute | solution.py:89
  499.0 25.5 %collective-permute-done.57 = bf16[256,2048]{1,0:T(8,128)(2,1)S(1)} collective-permute-done((bf16[256,2048]{1,0:T(8,128)(2,1)S(1)}, bf16[256,2048]{1,0:T(8,128)(2,1)S(1)}, u32[]{:S(2)}, u32[]{:S(2)}) %collective-permute-start.57) | collective-permute-done | bytes 1048608 | tf_op jit(solution)/shard_map/ppermute | solution.py:92
  (383 shorter events, 210.0 us)
Async XLA Ops:
  7.2 224.3 %all-gather.5.cloned.1.call-start = ((), (), s32[]{:S(2)}) async-start(), calls=%async_computation.5 | async-start | bytes 5242880 | tf_op jit(solution)/shard_map/all_gather | solution.py:656
  11.7 79.5 %all-to-all-start = ((bf16[8,64,2048]{2,1,0:T(8,128)(2,1)}), bf16[8,64,2048]{2,1,0:T(8,128)(2,1)}, u32[]{:S(2)}, u32[]{:S(2)}) async-start(bf16[8,64,2048]{2,1,0:T(8,128)(2,1)} %shard_map.212), calls=%async_computation | async-start | bytes 4194304 | tf_op jit(solution)/shard_map/all_to_all | solution.py:658
  18.2 213.3 %all-gather.3.cloned.1.call-start = ((), (), s32[]{:S(2)}) async-start(), calls=%async_computation.4 | async-start | bytes 10485760 | tf_op jit(solution)/shard_map/all_gather | solution.py:680
  49.7 27.2 %collective-permute-start.8 = (bf16[272,2048]{1,0:T(8,128)(2,1)S(1)}, bf16[272,2048]{1,0:T(8,128)(2,1)}, u32[]{:S(2)}, u32[]{:S(2)}) collective-permute-start(bf16[272,2048]{1,0:T(8,128)(2,1)S(1)} %fusion.1.refs_0_), channel_id=1, source_target_pairs={{0,4},{1,5},{2,0},{3,1},{4,6},{5,7},{6,2},{7,3},{8,12},{9,13},{10,... | collective-permute-start | bytes 3342344 | tf_op jit(solution)/shard_map/ppermute | solution.py:92
  91.3 370.9 %reduce-scatter.7.cloned.1.call-start = ((), (), s32[]{:S(2)}) async-start(), calls=%async_computation.7 | async-start | bytes 10485760
  91.3 26.5 %collective-permute-start.10 = (bf16[272,2048]{1,0:T(8,128)(2,1)}, bf16[272,2048]{1,0:T(8,128)(2,1)}, u32[]{:S(2)}, u32[]{:S(2)}) collective-permute-start(bf16[272,2048]{1,0:T(8,128)(2,1)} %collective-permute-done.8.refs_2_), channel_id=1, source_target_pairs={{0,4},{1,5},{2,0},{3,1},{4,6},{5,7},{6,2},{7,3},{8,12},{9,13},{10,... | collective-permute-start | bytes 3342344 | tf_op jit(solution)/shard_map/ppermute | solution.py:92
  91.4 27.6 %collective-permute-start = (bf16[128,2048]{1,0:T(8,128)(2,1)S(1)}, bf16[128,2048]{1,0:T(8,128)(2,1)S(1)}, u32[]{:S(2)}, u32[]{:S(2)}) collective-permute-start(bf16[128,2048]{1,0:T(8,128)(2,1)S(1)} %copy-done.9), channel_id=1, source_target_pairs={{0,8},{8,24},{16,0},{24,16},{1,17},{9,1},{17,25},{25,9},{2,10},{10... | collective-permute-start | bytes 1572872 | tf_op jit(solution)/shard_map/ppermute | solution.py:89
  117.8 25.5 %collective-permute-start.12 = (bf16[272,2048]{1,0:T(8,128)(2,1)}, bf16[272,2048]{1,0:T(8,128)(2,1)}, u32[]{:S(2)}, u32[]{:S(2)}) collective-permute-start(bf16[272,2048]{1,0:T(8,128)(2,1)} %collective-permute-done.10.refs_4_), channel_id=1, source_target_pairs={{0,4},{1,5},{2,0},{3,1},{4,6},{5,7},{6,2},{7,3},{8,12},{9,13},{10,... | collective-permute-start | bytes 3342344 | tf_op jit(solution)/shard_map/ppermute | solution.py:92
  119.0 38.2 %collective-permute-start.7 = (bf16[272,2048]{1,0:T(8,128)(2,1)S(1)}, bf16[272,2048]{1,0:T(8,128)(2,1)}, u32[]{:S(2)}, u32[]{:S(2)}) collective-permute-start(bf16[272,2048]{1,0:T(8,128)(2,1)S(1)} %fusion.1.refs_0_), channel_id=1, source_target_pairs={{0,1},{1,0},{2,3},{3,2},{4,5},{5,4},{6,7},{7,6},{8,9},{9,8},{10,11... | collective-permute-start | bytes 3342344 | tf_op jit(solution)/shard_map/ppermute | solution.py:95
  131.6 25.5 %collective-permute-start.9 = (bf16[272,2048]{1,0:T(8,128)(2,1)}, bf16[272,2048]{1,0:T(8,128)(2,1)S(1)}, u32[]{:S(2)}, u32[]{:S(2)}) collective-permute-start(bf16[272,2048]{1,0:T(8,128)(2,1)} %collective-permute-done.8.refs_2_), channel_id=1, source_target_pairs={{0,1},{1,0},{2,3},{3,2},{4,5},{5,4},{6,7},{7,6},{8,9},{9,8},{10,11... | collective-permute-start | bytes 3342344 | tf_op jit(solution)/shard_map/ppermute | solution.py:95
  131.8 25.4 %collective-permute-start.11 = (bf16[272,2048]{1,0:T(8,128)(2,1)}, bf16[272,2048]{1,0:T(8,128)(2,1)}, u32[]{:S(2)}, u32[]{:S(2)}) collective-permute-start(bf16[272,2048]{1,0:T(8,128)(2,1)} %collective-permute-done.10.refs_4_), channel_id=1, source_target_pairs={{0,1},{1,0},{2,3},{3,2},{4,5},{5,4},{6,7},{7,6},{8,9},{9,8},{10,11... | collective-permute-start | bytes 3342344 | tf_op jit(solution)/shard_map/ppermute | solution.py:95
  226.8 29.4 %collective-permute-start.26 = (bf16[128,2048]{1,0:T(8,128)(2,1)}, bf16[128,2048]{1,0:T(8,128)(2,1)}, u32[]{:S(2)}, u32[]{:S(2)}) collective-permute-start(bf16[128,2048]{1,0:T(8,128)(2,1)} %collective-permute-done.21.refs_2_), channel_id=1, source_target_pairs={{0,4},{1,5},{2,0},{3,1},{4,6},{5,7},{6,2},{7,3},{8,12},{9,13},{10,... | collective-permute-start | bytes 1572872 | tf_op jit(solution)/shard_map/ppermute | solution.py:92
  271.2 29.2 %collective-permute-start.38 = (bf16[128,2048]{1,0:T(8,128)(2,1)S(1)}, bf16[128,2048]{1,0:T(8,128)(2,1)S(1)}, u32[]{:S(2)}, u32[]{:S(2)}) collective-permute-start(bf16[128,2048]{1,0:T(8,128)(2,1)S(1)} %add_convert_fusion.12), channel_id=1, source_target_pairs={{0,4},{1,5},{2,0},{3,1},{4,6},{5,7},{6,2},{7,3},{8,12},{9,13},{10,... | collective-permute-start | bytes 1572872 | tf_op jit(solution)/shard_map/ppermute | solution.py:92
  299.5 39.5 %collective-permute-start.35 = (bf16[128,2048]{1,0:T(8,128)(2,1)}, bf16[128,2048]{1,0:T(8,128)(2,1)}, u32[]{:S(2)}, u32[]{:S(2)}) collective-permute-start(bf16[128,2048]{1,0:T(8,128)(2,1)} %get-tuple-element.118), channel_id=1, source_target_pairs={{0,1},{1,0},{2,3},{3,2},{4,5},{5,4},{6,7},{7,6},{8,9},{9,8},{10,11... | collective-permute-start | bytes 1572872 | tf_op jit(solution)/shard_map/ppermute | solution.py:95
  299.9 35.4 %collective-permute-start.40 = (bf16[128,2048]{1,0:T(8,128)(2,1)}, bf16[128,2048]{1,0:T(8,128)(2,1)}, u32[]{:S(2)}, u32[]{:S(2)}) collective-permute-start(bf16[128,2048]{1,0:T(8,128)(2,1)} %get-tuple-element.131), channel_id=1, source_target_pairs={{0,1},{1,0},{2,3},{3,2},{4,5},{5,4},{6,7},{7,6},{8,9},{9,8},{10,11... | collective-permute-start | bytes 1572872 | tf_op jit(solution)/shard_map/ppermute | solution.py:95
  370.3 174.1 %reduce-scatter.5.cloned.1.call-start = ((), (), s32[]{:S(2)}) async-start(), calls=%async_computation.6 | async-start | bytes 5242880 | tf_op jit(solution)/shard_map/reduce_scatter | solution.py:759
  397.8 26.1 %collective-permute-start.53 = (bf16[256,2048]{1,0:T(8,128)(2,1)S(1)}, bf16[256,2048]{1,0:T(8,128)(2,1)S(1)}, u32[]{:S(2)}, u32[]{:S(2)}) collective-permute-start(bf16[256,2048]{1,0:T(8,128)(2,1)S(1)} %add_convert_fusion.3), channel_id=1, source_target_pairs={{0,4},{1,5},{2,0},{3,1},{4,6},{5,7},{6,2},{7,3},{8,12},{9,13},{10,... | collective-permute-start | bytes 3145736 | tf_op jit(solution)/shard_map/ppermute | solution.py:92
  402.6 21.3 %collective-permute-start.52 = (bf16[256,2048]{1,0:T(8,128)(2,1)S(1)}, bf16[256,2048]{1,0:T(8,128)(2,1)S(1)}, u32[]{:S(2)}, u32[]{:S(2)}) collective-permute-start(bf16[256,2048]{1,0:T(8,128)(2,1)S(1)} %get-tuple-element.151), channel_id=1, source_target_pairs={{0,1},{1,0},{2,3},{3,2},{4,5},{5,4},{6,7},{7,6},{8,9},{9,8},{10,11... | collective-permute-start | bytes 3145736 | tf_op jit(solution)/shard_map/ppermute | solution.py:95
  406.3 27.9 %collective-permute-start.45 = (bf16[128,2048]{1,0:T(8,128)(2,1)S(1)}, bf16[128,2048]{1,0:T(8,128)(2,1)S(1)}, u32[]{:S(2)}, u32[]{:S(2)}) collective-permute-start(bf16[128,2048]{1,0:T(8,128)(2,1)S(1)} %add_convert_fusion.7), channel_id=1, source_target_pairs={{0,4},{1,5},{2,0},{3,1},{4,6},{5,7},{6,2},{7,3},{8,12},{9,13},{10,... | collective-permute-start | bytes 1572872 | tf_op jit(solution)/shard_map/ppermute | solution.py:92
  434.3 26.3 %collective-permute-start.56 = (bf16[256,2048]{1,0:T(8,128)(2,1)S(1)}, bf16[256,2048]{1,0:T(8,128)(2,1)S(1)}, u32[]{:S(2)}, u32[]{:S(2)}) collective-permute-start(bf16[256,2048]{1,0:T(8,128)(2,1)S(1)} %add_convert_fusion.2), channel_id=1, source_target_pairs={{0,4},{1,5},{2,0},{3,1},{4,6},{5,7},{6,2},{7,3},{8,12},{9,13},{10,... | collective-permute-start | bytes 3145736 | tf_op jit(solution)/shard_map/ppermute | solution.py:92
  438.4 22.2 %collective-permute-start.55 = (bf16[256,2048]{1,0:T(8,128)(2,1)S(1)}, bf16[256,2048]{1,0:T(8,128)(2,1)S(1)}, u32[]{:S(2)}, u32[]{:S(2)}) collective-permute-start(bf16[256,2048]{1,0:T(8,128)(2,1)S(1)} %get-tuple-element.157), channel_id=1, source_target_pairs={{0,1},{1,0},{2,3},{3,2},{4,5},{5,4},{6,7},{7,6},{8,9},{9,8},{10,11... | collective-permute-start | bytes 3145736 | tf_op jit(solution)/shard_map/ppermute | solution.py:95
  462.2 84.9 %all-to-all-start.1 = ((bf16[8,64,2048]{2,1,0:T(8,128)(2,1)}), bf16[8,64,2048]{2,1,0:T(8,128)(2,1)}, u32[]{:S(2)}, u32[]{:S(2)}) async-start(bf16[8,64,2048]{2,1,0:T(8,128)(2,1)} %bitcast.58), calls=%async_computation.1 | async-start | bytes 4194304 | tf_op jit(solution)/shard_map/all_to_all | solution.py:811
  474.0 25.0 %collective-permute-start.54 = (bf16[256,2048]{1,0:T(8,128)(2,1)S(1)}, bf16[256,2048]{1,0:T(8,128)(2,1)S(1)}, u32[]{:S(2)}, u32[]{:S(2)}) collective-permute-start(bf16[256,2048]{1,0:T(8,128)(2,1)S(1)} %get-tuple-element.155), channel_id=1, source_target_pairs={{0,1},{1,0},{2,3},{3,2},{4,5},{5,4},{6,7},{7,6},{8,9},{9,8},{10,11... | collective-permute-start | bytes 3145736 | tf_op jit(solution)/shard_map/ppermute | solution.py:95
  474.2 50.3 %collective-permute-start.57 = (bf16[256,2048]{1,0:T(8,128)(2,1)S(1)}, bf16[256,2048]{1,0:T(8,128)(2,1)S(1)}, u32[]{:S(2)}, u32[]{:S(2)}) collective-permute-start(bf16[256,2048]{1,0:T(8,128)(2,1)S(1)} %copy-done.57), channel_id=1, source_target_pairs={{0,4},{1,5},{2,0},{3,1},{4,6},{5,7},{6,2},{7,3},{8,12},{9,13},{10,... | collective-permute-start | bytes 3145736 | tf_op jit(solution)/shard_map/ppermute | solution.py:92
  (133 other events, 1420.3 us)
Sparse Core Ops, SparseCore 0:
  9.9 64.4 all-gather.4
  91.4 97.7 all-gather.2
  370.4 87.5 reduce-scatter.6
  461.0 59.6 reduce-scatter.4
